TPU v7x, 128 devices: a whole 4x4x4 slice. The times are simulated.
128 devices in a mesh: gr: 8 (over z_hi, y), gc: 16 (over z_lo, x, core).
Axes of the slice: x: 4, y: 4, z: 4 (z_hi: 2, z_lo: 2; z = z_hi * 2 + z_lo), core: 2. Of those that a mesh axis runs over, the one named last changes fastest.
Arguments:
- a_matrix: bfloat16 [65536, 18432], P('gr', 'gc'), may hold values from -0.5 to 0.5
- scaling: float32 [18432], P('gc'), may hold values from 0.1 to 1
Outputs:
- normal_slab: float32 [1024, 65536], P('gc', 'gr')
All inputs are finite; a program needn't handle non-finite values.
Results may differ from a plain program's by a relative error of at most 0.0027.
Values may be sent and summed in bfloat16 or wider, within the bound.
No kernel may reach another device: no remote copies, remote signals or barrier semaphores. Data moves between devices by JAX's collectives and lax.ppermute only.
A program may use at most 128 MiB of HBM per device.

v0:
```python
import jax
import jax.numpy as jnp
from jax import lax
from jax.sharding import PartitionSpec as P

SLAB_DEV = 128


def shards(a_matrix, scaling):
    scaled = (a_matrix[:SLAB_DEV].astype(jnp.float32) * scaling[None, :]).astype(jnp.bfloat16)
    partial_sums = lax.dot_general(
        lax.all_gather(scaled, "gr", axis=0, tiled=True),
        a_matrix,
        (((1,), (1,)), ((), ())),
        preferred_element_type=jnp.float32,
    )
    return lax.psum_scatter(partial_sums, "gc", scatter_dimension=0, tiled=True)


def solution(mesh):
    placed = (P("gr", "gc"), P("gc"))
    return jax.shard_map(
        shards, mesh=mesh, in_specs=placed, out_specs=P("gc", "gr"), check_vma=False
    )
```

profile of v0, /device:TPU:0, one launch (start us, length us, event | category | flops | bytes accessed | tf_op | source)
XLA Modules:
  0.0 286.1 jit_solution(7390684504320413703)
XLA Ops:
  6.5 0.0 all-gather.2.cloned.1.call-start
  6.5 1.7 multiply_convert_fusion
  8.3 0.0 all-gather.2.cloned.1.call-update
  8.3 0.0 reduce-scatter.2.cloned.1.call-start
  8.4 60.7 %all-gather.2.cloned.1.call-done = bf16[1024,1152]{1,0:T(8,128)(2,1)} async-done(((bf16[128,1152]{1,0:T(8,128)(2,1)}), bf16[1024,1152]{1,0:T(8,128)(2,1)}) %all-gather.2.cloned.1.call-update) | async-done | bytes 2359312 | tf_op jit(solution)/shard_map/all_gather | solution.py:12
  69.1 28.7 %fusion = f32[1024,8192]{1,0:T(8,128)} fusion(bf16[1024,1152]{1,0:T(8,128)(2,1)} %all-gather.2.cloned.1.call-done, bf16[8192,1152]{1,0:T(8,128)(2,1)} %param.2), kind=kOutput, calls=%fused_computation.1 | convolution fusion | flops 19327352832 | bytes 54788096 | tf_op jit(solution)/shard_map/dot_general | solution.py:11
  97.8 0.0 reduce-scatter.2.cloned.1.call-update
  97.9 181.4 %reduce-scatter.2.cloned.1.call-done = f32[64,8192]{1,0:T(8,128)} async-done(((f32[1024,8192]{1,0:T(8,128)}), f32[64,8192]{1,0:T(8,128)}) %reduce-scatter.2.cloned.1.call-update) | async-done | bytes 2097168 | tf_op jit(solution)/shard_map/reduce_scatter | solution.py:17
Async XLA Ops:
  6.5 62.5 %all-gather.2.cloned.1.call-start = ((), (), s32[]{:S(2)}) async-start(), calls=%async_computation.1 | async-start | bytes 2654208 | tf_op jit(solution)/shard_map/all_gather | solution.py:12
  8.3 270.9 %reduce-scatter.2.cloned.1.call-start = ((), (), s32[]{:S(2)}) async-start(), calls=%async_computation.2 | async-start | bytes 35651584 | tf_op jit(solution)/shard_map/reduce_scatter | solution.py:17
Sparse Core Ops, SparseCore 0:
  9.7 59.3 all-gather.1
  98.0 181.1 reduce-scatter.1
where the time goes:
time: 286 us
  waiting for transfers between devices  242 us (85%)
  matrix products  28.7 us (10%)
  between operations  13.4 us (5%)
    reduce_scatter x1, waiting for transfers between devices, shards(): return lax.psum_scatter(partial_sums, 'gc', scatter_dimension=0, tiled=True)  181 us
    all_gather x1, waiting for transfers between devices, shards(): lax.all_gather(scaled, 'gr', axis=0, tiled=True)  60.7 us
    dot_general x1, matrix products, shards(): lax.dot_general(lax.all_gather(scaled, 'gr', axis=0, tiled=True), a_matri...  28.7 us
  transfers between devices with their start and end apart: 2, of which 2 were waited for; matrix products, arithmetic and copies ran while one was open for 0% of the time, Pallas kernels for 0%

commit v1 on v0

v1 whole, which is shorter than its diff:
```python
import jax
import jax.numpy as jnp
from jax import lax
from jax.experimental import pallas as pl
from jax.experimental.pallas import tpu as pltpu
from jax.sharding import PartitionSpec as P

F32, BF16 = jnp.float32, jnp.bfloat16
SLAB_DEV = 128
HALF = 64
VMEM = 47 * 1024 * 1024

Y_UP = [(z * 4 + y, z * 4 + (y + 1) % 4) for z in range(2) for y in range(4)]
Y_DOWN = [(d, s) for s, d in Y_UP]
Y_FAR = [(z * 4 + y, z * 4 + (y + 2) % 4) for z in range(2) for y in range(4)]
Z_FAR = [(z * 4 + y, (1 - z) * 4 + y) for z in range(2) for y in range(4)]


def gc(z, x, c):
    return (z * 4 + x % 4) * 2 + c


EACH = [(z, x, c) for z in range(2) for x in range(4) for c in range(2)]
X_UP = [(gc(z, x, c), gc(z, x + 1, c)) for z, x, c in EACH]
X_DOWN = [(gc(z, x, c), gc(z, x - 1, c)) for z, x, c in EACH]
Z_NEAR = [(gc(z, x, c), gc(1 - z, x, c)) for z, x, c in EACH]
CORE = [(gc(z, x, c), gc(z, x, 1 - c)) for z, x, c in EACH]

UNITS = [[256, 256, 512], [512, 256, 256]]
PLAN = [
    ("order", 0, 0),
    ("product", 0, 0),
    ("product", 0, 1),
    ("first", 0, 0),
    ("product", 0, 2),
    ("first", 0, 1),
    ("second", 0, 0),
    ("order", 1, 0),
    ("first", 0, 2),
    ("product", 1, 0),
    ("second", 0, 1),
    ("sum", 0, 0),
    ("first", 1, 0),
    ("product", 1, 1),
    ("second", 0, 2),
    ("sum", 0, 1),
    ("product", 1, 2),
    ("first", 1, 1),
    ("second", 1, 0),
    ("sum", 0, 2),
    ("first", 1, 2),
    ("second", 1, 1),
    ("sum", 1, 0),
    ("second", 1, 2),
    ("sum", 1, 1),
    ("finish", 1, 0),
    ("finish", 1, 1),
    ("sum", 1, 2),
    ("finish", 1, 2),
]


def dot(s, a):
    return lax.dot_general(s, a, (((1,), (1,)), ((), ())), preferred_element_type=F32)


def cost(flops, nbytes):
    return pl.CostEstimate(flops=flops, bytes_accessed=nbytes, transcendentals=0)


def params():
    return pltpu.CompilerParams(vmem_limit_bytes=VMEM)


def order_one(place, *refs):
    pieces, out = refs[:4], refs[4]
    for d in range(4):
        for h in range(2):
            to = (place[1] ^ h) * 4 + (d + place[0]) % 4
            out[pl.ds(pl.multiple_of(to * HALF, HALF), HALF), :] = pieces[d][h * HALF : (h + 1) * HALF, :]


def order(place, pieces, dep):
    k = pieces[0].shape[1]
    whole = lambda: (0, 0)
    ins = [(place, None, pltpu.SMEM)] + [(piece, piece.shape, whole) for piece in pieces]
    return run(order_one, (), [(((4 * SLAB_DEV, k), BF16), (4 * SLAB_DEV, k), whole)], ins, dep)[0]


def run(kernel, grid, outs, ins, dep, aliases={}):
    shapes = [jax.ShapeDtypeStruct(shape, dtype) for (shape, dtype), _, _ in outs]
    out_specs = [pl.BlockSpec(block, where) for _, block, where in outs]
    in_specs = [pl.BlockSpec(block, where) if block else pl.BlockSpec(memory_space=where) for _, block, where in ins]
    arrays = [array for array, _, _ in ins]
    arrays += dep
    in_specs += [pl.BlockSpec(memory_space=pl.ANY)] * len(dep)

    def body(*refs):
        kernel(*refs[: len(ins)], *refs[len(arrays) :])

    return pl.pallas_call(
        body,
        grid=grid,
        out_shape=shapes,
        in_specs=in_specs,
        out_specs=out_specs,
        input_output_aliases=aliases,
        compiler_params=params(),
        cost_estimate=cost(1000, 1000),
    )(*arrays)


def product(slab, a, start, n, tile, dep):
    rows, k = slab.shape[0] // 2, slab.shape[1]

    def kernel(s, a_ref, own, sibling):
        total = dot(s[...], a_ref[...])
        own[...] = total[:rows]
        sibling[...] = total[rows:].astype(BF16)

    return run(
        kernel,
        (n // tile,),
        [(((rows, n), F32), (rows, tile), lambda i: (0, i)), (((rows, n), BF16), (rows, tile), lambda i: (0, i))],
        [(slab, (2 * rows, k), lambda i: (0, 0)), (a, (tile, k), lambda i: (start // tile + i, 0))],
        dep,
    )


def first_messages(own, came, tile, dep):
    half = own.shape[1] // 2
    tile = min(half, tile)
    to = half // tile

    def kernel(l, r, c_l, c_r, up, down):
        up[:HALF] = (l[128:192] + wide(c_l[128:192])).astype(BF16)
        up[HALF:] = (r[64:128] + wide(c_r[64:128])).astype(BF16)
        down[:HALF] = (r[128:192] + wide(c_r[128:192])).astype(BF16)
        down[HALF:] = (l[192:256] + wide(c_l[192:256])).astype(BF16)

    left, right = lambda i: (0, i), lambda i: (0, to + i)
    return run(
        kernel,
        (to,),
        [(((128, half), BF16), (128, tile), left)] * 2,
        [(own, (256, tile), left), (own, (256, tile), right), (came, (256, tile), left), (came, (256, tile), right)],
        dep,
    )


def second_messages(own, came, up1, down1, tile, dep):
    half = own.shape[1] // 2
    tile = min(half, tile)
    to = half // tile

    def kernel(o1, c1, u, o3, c3, d, up, down):
        up[...] = (o1[...] + wide(c1[...]) + wide(u[...])).astype(BF16)
        down[...] = (o3[...] + wide(c3[...]) + wide(d[...])).astype(BF16)

    block = (64, tile)
    first = lambda i: (0, i)
    return run(
        kernel,
        (to,),
        [(((64, half), BF16), block, first)] * 2,
        [
            (own, block, lambda i: (1, i)),
            (came, block, lambda i: (1, i)),
            (up1, block, first),
            (own, block, lambda i: (3, to + i)),
            (came, block, lambda i: (3, to + i)),
            (down1, block, first),
        ],
        dep,
    )


def x_parts(own, came, up1, down1, up2, down2, tile):
    half = own.shape[1] // 2
    to = half // tile
    block = (64, tile)
    cut = lambda j, i: (0, j * to + i)
    low = lambda j, i: (0, i)
    high = lambda j, i: (1, i)
    ins = [(own, block, cut), (came, block, cut)]
    ins += [(up2, block, low), (down1, block, high), (down2, block, low), (up1, block, high)]
    return (2, to), cut, ins


def x_total(o, c, u2, d1, d2, u1):
    left = pl.program_id(0) == 0
    return o[...] + wide(c[...]) + jnp.where(left, wide(u2[...]) + wide(d1[...]), wide(d2[...]) + wide(u1[...]))


def sum_over_x(parts, held, start, tile, dep):
    n = parts[0].shape[1]
    tile = min(n // 2, tile)
    grid, cut, ins = x_parts(*parts, tile)
    at = start // tile
    spread = lambda j, i: (0, at + cut(j, i)[1])

    def kernel(o, c, u2, d1, d2, u1, _, out):
        out[...] = x_total(o, c, u2, d1, d2, u1)

    return run(
        kernel,
        grid,
        [((held.shape, F32), (64, tile), spread)],
        ins + [(held, None, pl.ANY)],
        dep,
        {6: 0},
    )[0]


def split_over_z(parts, held, start, same, tile, dep):
    n = parts[0].shape[1]
    tile = min(n // 2, tile)
    grid, cut, ins = x_parts(*parts, tile)
    at = start // tile
    spread = lambda j, i: (0, at + cut(j, i)[1])

    def kernel(o, c, u2, d1, d2, u1, h, same_ref, stays, goes):
        total = x_total(o, c, u2, d1, d2, u1)
        yes = same_ref[0] == 1
        stays[...] = jnp.where(yes, h[...], total)
        goes[...] = jnp.where(yes, total, h[...]).astype(BF16)

    return run(
        kernel,
        grid,
        [(((64, n), F32), (64, tile), cut), (((64, n), BF16), (64, tile), cut)],
        ins + [(held, (64, tile), spread), (same, None, pltpu.SMEM)],
        dep,
    )


def finish(stays, came, out, start, tile, dep):
    n = stays.shape[1]
    tile = min(n, tile)
    at = start // tile

    def kernel(s, c, _, o):
        o[...] = s[...] + wide(c[...])

    here = lambda i: (0, i)
    return run(
        kernel,
        (n // tile,),
        [((out.shape, F32), (64, tile), lambda i: (0, at + i))],
        [(stays, (64, tile), here), (came, (64, tile), here), (out, None, pl.ANY)],
        dep,
        {2: 0},
    )[0]


def wide(v):
    return v.astype(F32)


def shards(a, scaling):
    n_all = a.shape[0]
    gr, at = lax.axis_index("gr"), lax.axis_index("gc")
    core, x, z_lo = at % 2, (at // 2) % 4, at // 8
    y, z_hi = gr % 4, gr // 4
    same = (z_lo == z_hi)
    place = jnp.stack([(y - x + 4) % 4, core, z_lo ^ z_hi]).astype(jnp.int32)

    mine = (a[:SLAB_DEV].astype(F32) * scaling[None, :]).astype(BF16)
    y_up = lax.ppermute(mine, "gr", Y_UP)
    y_down = lax.ppermute(mine, "gr", Y_DOWN)
    y_far = lax.ppermute(mine, "gr", Y_FAR)
    z_far = lax.ppermute(mine, "gr", Z_FAR)
    near = [mine, y_down, y_far, y_up]
    far = [z_far, lax.ppermute(z_far, "gr", Y_DOWN), lax.ppermute(y_far, "gr", Z_FAR), lax.ppermute(z_far, "gr", Y_UP)]
    slabs = [None, None]
    tile = n_all // 8
    start = [[0], [0]]
    for e in range(2):
        for size in UNITS[e]:
            start[e].append(start[e][-1] + size * n_all // 1024)
    held = jnp.zeros((HALF, n_all), F32)
    out = jnp.zeros((HALF, n_all), F32)
    flag = same.astype(jnp.int32).reshape(1)
    units, z_units = {}, {}
    dep = [z_far]
    for what, e, i in PLAN:
        if what == "order":
            slabs[e] = order(place, far if e else near, dep)
            dep = [slabs[e]]
            continue
        begin, n = start[e][i], start[e][i + 1] - start[e][i]
        if what == "product":
            own, sibling = product(slabs[e], a, begin, n, tile, dep)
            units[e, i] = [own, lax.ppermute(sibling, "gc", CORE)]
            dep = [sibling]
        elif what == "first":
            if e == i == 0:
                dep += far
            up, down = first_messages(*units[e, i], tile, dep)
            units[e, i] += [lax.ppermute(up, "gc", X_UP), lax.ppermute(down, "gc", X_DOWN)]
            dep = [down]
        elif what == "second":
            up, down = second_messages(*units[e, i], tile, dep)
            units[e, i] += [lax.ppermute(up, "gc", X_UP), lax.ppermute(down, "gc", X_DOWN)]
            dep = [down]
        elif what == "sum" and e == 0:
            held = sum_over_x(units[e, i], held, begin, tile, dep)
            dep = [held]
        elif what == "sum":
            stays, goes = split_over_z(units[e, i], held, begin, flag, tile, dep)
            z_units[i] = stays, lax.ppermute(goes, "gc", Z_NEAR)
            dep = [goes]
        else:
            out = finish(*z_units[i], out, begin, tile, dep)
            dep = [out]
    return out


def solution(mesh):
    placed = (P("gr", "gc"), P("gc"))
    return jax.shard_map(shards, mesh=mesh, in_specs=placed, out_specs=P("gc", "gr"), check_vma=False)
```

time: 286 us -> 188 us (0.66)
  waiting for transfers between devices: 242 us -> 45.6 us
  Pallas kernels: 0 us -> 69.9 us
  starting transfers between devices: 0.04 us -> 55.4 us
  matrix products: 28.7 us -> 0 us
  local copies, waits for them, and re-layouts: 0 us -> 14.4 us
  between operations: 13.4 us -> 0.55 us
    reduce_scatter x1 -> x0, waiting for transfers between devices: 181 us -> none  [shards(): return lax.psum_scatter(partial_sums, 'gc', scatter_dimension=0, tiled=True)]
    pallas_call x0 -> x29, Pallas kernels: none -> 69.9 us  [run(): pl.pallas_call(body, grid=grid, out_shape=shapes, in_specs=in_specs, out_...]
    all_gather x1 -> x0, waiting for transfers between devices: 60.7 us -> none  [shards(): lax.all_gather(scaled, 'gr', axis=0, tiled=True)]
    ppermute x0 -> x40, starting transfers between devices: none -> 55.4 us  [the longest x12 35.3 us: shards(): lax.ppermute(down, 'gc', X_DOWN)]
    ppermute x0 -> x40, waiting for transfers between devices: none -> 45.6 us  [the longest x12 19.2 us: shards(): lax.ppermute(up, 'gc', X_UP)]
    dot_general x1 -> x0, matrix products: 28.7 us -> none  [shards(): lax.dot_general(lax.all_gather(scaled, 'gr', axis=0, tiled=True), a_matri...]
    unnamed x0 -> x81, local copies, waits for them, and re-layouts: none -> 14.1 us
  transfers between devices with their start and end apart: 2 -> 40, of which waited for: 2 -> 15; matrix products, arithmetic and copies ran while one was open for 0% -> 1% of each run, Pallas kernels for 0% -> 21%
where the time goes in v1:
time: 188 us; the launch traced here: 187 us
  Pallas kernels  69.9 us (37%)
  starting transfers between devices  55.4 us (29%)
  waiting for transfers between devices  45.6 us (24%)
  local copies, waits for them, and re-layouts  14.4 us (8%)
    pallas_call x29, Pallas kernels, run(): pl.pallas_call(body, grid=grid, out_shape=shapes, in_specs=in_specs, out_...  69.9 us
    ppermute x12, starting transfers between devices, shards(): lax.ppermute(down, 'gc', X_DOWN)  35.3 us
    ppermute x12, waiting for transfers between devices, shards(): lax.ppermute(up, 'gc', X_UP)  19.2 us
    unnamed x81, local copies, waits for them, and re-layouts  14.1 us
    ppermute x3, waiting for transfers between devices, shards(): z_units[i] = (stays, lax.ppermute(goes, 'gc', Z_NEAR))  8.19 us
    ppermute x1, waiting for transfers between devices, shards(): y_down = lax.ppermute(mine, 'gr', Y_DOWN)  5.24 us
    ppermute x1, waiting for transfers between devices, shards(): y_far = lax.ppermute(mine, 'gr', Y_FAR)  4.43 us
    ppermute x1, starting transfers between devices, shards(): z_far = lax.ppermute(mine, 'gr', Z_FAR)  4.04 us
  transfers between devices with their start and end apart: 40, of which 15 were waited for; matrix products, arithmetic and copies ran while one was open for 1% of the time, Pallas kernels for 21%

profile of v1, /device:TPU:0, one launch (start us, length us, event | category | flops | bytes accessed | tf_op | source)
XLA Modules:
  0.0 186.9 jit_solution(6083684178584016118)
XLA Ops:
  1.0 4.0 %collective-permute-start = (bf16[128,1152]{1,0:T(8,128)(2,1)S(1)}, bf16[128,1152]{1,0:T(8,128)(2,1)S(1)}, u32[]{:S(2)}, u32[]{:S(2)}) collective-permute-start(bf16[128,1152]{1,0:T(8,128)(2,1)S(1)} %multiply_convert_fusion.refs_1_), channel_id=1, source_target_pairs={{0,64},{16,80},{32,96},{48,112},{64,0},{80,16},{96,32},{112,48},{1... | collective-permute-start | bytes 884744 | tf_op jit(solution)/shard_map/ppermute | solution.py:272
  5.1 3.2 %collective-permute-start.2 = (bf16[128,1152]{1,0:T(8,128)(2,1)S(1)}, bf16[128,1152]{1,0:T(8,128)(2,1)S(1)}, u32[]{:S(2)}, u32[]{:S(2)}) collective-permute-start(bf16[128,1152]{1,0:T(8,128)(2,1)S(1)} %multiply_convert_fusion.refs_1_), channel_id=1, source_target_pairs={{0,32},{16,48},{32,0},{48,16},{64,96},{80,112},{96,64},{112,80},{1... | collective-permute-start | bytes 884744 | tf_op jit(solution)/shard_map/ppermute | solution.py:271
  10.4 1.7 collective-permute-done.refs_5_.refs_1_
  12.1 4.4 %collective-permute-done.2.refs_3_ = bf16[128,1152]{1,0:T(8,128)(2,1)S(1)} collective-permute-done((bf16[128,1152]{1,0:T(8,128)(2,1)S(1)}, bf16[128,1152]{1,0:T(8,128)(2,1)S(1)}, u32[]{:S(2)}, u32[]{:S(2)}) %collective-permute-start.2) | collective-permute-done | bytes 294944 | tf_op jit(solution)/shard_map/ppermute | solution.py:271
  16.5 5.2 %collective-permute-done.5.refs_2_ = bf16[128,1152]{1,0:T(8,128)(2,1)S(1)} collective-permute-done((bf16[128,1152]{1,0:T(8,128)(2,1)S(1)}, bf16[128,1152]{1,0:T(8,128)(2,1)S(1)}, u32[]{:S(2)}, u32[]{:S(2)}) %collective-permute-start.5) | collective-permute-done | bytes 294944 | tf_op jit(solution)/shard_map/ppermute | solution.py:270
  22.4 5.0 %shard_map.29 = (f32[256,2048]{1,0:T(8,128)S(1)}, bf16[256,2048]{1,0:T(8,128)(2,1)S(1)}) custom-call(bf16[512,1152]{1,0:T(8,128)(2,1)S(1)} %shard_map.28.refs_0_.refs_2_, bf16[8192,1152]{1,0:T(8,128)(2,1)} %refs_1_.11, bf16[512,1152]{1,0:T(8,128)(2,1)S(1)} %shard_map.28.refs_0_.refs_2_), custom_call_target="tpu_custom_call" | custom-call | flops 1000 | bytes 1000 | tf_op jit(solution)/shard_map/pallas_call | solution.py:101
  27.5 2.7 %collective-permute-start.1 = (bf16[128,1152]{1,0:T(8,128)(2,1)S(1)}, bf16[128,1152]{1,0:T(8,128)(2,1)S(1)}, u32[]{:S(2)}, u32[]{:S(2)}) collective-permute-start(bf16[128,1152]{1,0:T(8,128)(2,1)S(1)} %collective-permute-done.refs_5_.refs_1_), channel_id=1, source_target_pairs={{16,0},{32,16},{48,32},{0,48},{80,64},{96,80},{112,96},{64,112},{1... | collective-permute-start | bytes 884744 | tf_op jit(solution)/shard_map/ppermute | solution.py:274
  30.6 5.0 %shard_map.30 = (f32[256,2048]{1,0:T(8,128)S(1)}, bf16[256,2048]{1,0:T(8,128)(2,1)S(1)}) custom-call(bf16[512,1152]{1,0:T(8,128)(2,1)S(1)} %shard_map.28.refs_0_.refs_2_, bf16[8192,1152]{1,0:T(8,128)(2,1)} %refs_1_.11, bf16[256,2048]{1,0:T(8,128)(2,1)S(1)} %get-tuple-element.48.refs_2_), custom_call_target="tpu_custom_call" | custom-call | flops 1000 | bytes 1000 | tf_op jit(solution)/shard_map/pallas_call | solution.py:101
  35.6 1.5 collective-permute-done.1.refs_6_.refs_2_
  37.1 3.4 %collective-permute-done.4.refs_8_.refs_4_ = bf16[128,1152]{1,0:T(8,128)(2,1)S(1)} collective-permute-done((bf16[128,1152]{1,0:T(8,128)(2,1)S(1)}, bf16[128,1152]{1,0:T(8,128)(2,1)S(1)}, u32[]{:S(2)}, u32[]{:S(2)}) %collective-permute-start.4) | collective-permute-done | bytes 294944 | tf_op jit(solution)/shard_map/ppermute | solution.py:274
  40.9 9.8 %shard_map.32 = (f32[256,4096]{1,0:T(8,128)}, bf16[256,4096]{1,0:T(8,128)(2,1)}) custom-call(bf16[512,1152]{1,0:T(8,128)(2,1)S(1)} %shard_map.28.refs_0_.refs_2_, bf16[8192,1152]{1,0:T(8,128)(2,1)} %refs_1_.11, bf16[128,1024]{1,0:T(8,128)(2,1)S(1)} %get-tuple-element.51.refs_2_), custom_call_target="tpu_custom_call" | custom-call | flops 1000 | bytes 1000 | tf_op jit(solution)/shard_map/pallas_call | solution.py:101
  51.2 1.5 collective-permute-start.8
  52.7 1.7 collective-permute-start.9
  54.4 1.5 collective-permute-done.10.refs_2_.refs_3_.refs_1_.refs_4_
  56.1 4.6 %collective-permute-done.8.refs_2_.refs_5_ = bf16[128,1024]{1,0:T(8,128)(2,1)S(1)} collective-permute-done((bf16[128,1024]{1,0:T(8,128)(2,1)S(1)}, bf16[128,1024]{1,0:T(8,128)(2,1)S(1)}, u32[]{:S(2)}, u32[]{:S(2)}) %collective-permute-start.8) | collective-permute-done | bytes 262176 | tf_op jit(solution)/shard_map/ppermute | solution.py:300
  62.0 3.9 %shard_map.36 = (bf16[128,2048]{1,0:T(8,128)(2,1)}, bf16[128,2048]{1,0:T(8,128)(2,1)}) custom-call(f32[256,4096]{1,0:T(8,128)} %get-tuple-element.57.refs_0_.refs_1_.refs_3_, f32[256,4096]{1,0:T(8,128)} %get-tuple-element.57.refs_0_.refs_1_.refs_3_, bf16[256,4096]{1,0:T(8,128)(2,1)S(1)} %collective-permute-done.13.refs_2_.refs_3_.refs_1_.refs_4_, ...), custom_call_target="tpu_custom_call" | custom-call | flops 1000 | bytes 1000 | tf_op jit(solution)/shard_map/pallas_call | solution.py:101
  65.9 9.7 %shard_map.37 = (f32[256,4096]{1,0:T(8,128)}, bf16[256,4096]{1,0:T(8,128)(2,1)}) custom-call(bf16[512,1152]{1,0:T(8,128)(2,1)S(1)} %shard_map.35.refs_4_.refs_0_, bf16[8192,1152]{1,0:T(8,128)(2,1)} %refs_1_.11, bf16[128,2048]{1,0:T(8,128)(2,1)} %get-tuple-element.58.refs_2_), custom_call_target="tpu_custom_call" | custom-call | flops 1000 | bytes 1000 | tf_op jit(solution)/shard_map/pallas_call | solution.py:101
  75.6 1.5 collective-permute-start.11
  77.1 1.7 collective-permute-start.12
  79.1 3.0 %collective-permute-start.17 = (bf16[64,1024]{1,0:T(8,128)(2,1)S(1)}, bf16[64,1024]{1,0:T(8,128)(2,1)S(1)}, u32[]{:S(2)}, u32[]{:S(2)}) collective-permute-start(bf16[64,1024]{1,0:T(8,128)(2,1)S(1)} %get-tuple-element.55.refs_5_), channel_id=1, source_target_pairs={{0,6},{1,7},{2,0},{3,1},{4,2},{5,3},{6,4},{7,5},{8,14},{9,15},{10,... | collective-permute-start | bytes 393224 | tf_op jit(solution)/shard_map/ppermute | solution.py:304
  82.1 3.8 %collective-permute-done.11.refs_2_.refs_5_ = bf16[128,1024]{1,0:T(8,128)(2,1)S(1)} collective-permute-done((bf16[128,1024]{1,0:T(8,128)(2,1)S(1)}, bf16[128,1024]{1,0:T(8,128)(2,1)S(1)}, u32[]{:S(2)}, u32[]{:S(2)}) %collective-permute-start.11) | collective-permute-done | bytes 262176 | tf_op jit(solution)/shard_map/ppermute | solution.py:300
  86.2 3.0 %collective-permute-start.19 = (bf16[128,2048]{1,0:T(8,128)(2,1)}, bf16[128,2048]{1,0:T(8,128)(2,1)S(1)}, u32[]{:S(2)}, u32[]{:S(2)}) collective-permute-start(bf16[128,2048]{1,0:T(8,128)(2,1)} %get-tuple-element.58.refs_2_), channel_id=1, source_target_pairs={{0,6},{1,7},{2,0},{3,1},{4,2},{5,3},{6,4},{7,5},{8,14},{9,15},{10,... | collective-permute-start | bytes 1572872 | tf_op jit(solution)/shard_map/ppermute | solution.py:300
  91.2 3.1 %shard_map.40 = (bf16[128,2048]{1,0:T(8,128)(2,1)S(1)}, bf16[128,2048]{1,0:T(8,128)(2,1)S(1)}) custom-call(f32[256,4096]{1,0:T(8,128)} %get-tuple-element.64.refs_0_.refs_1_.refs_3_, f32[256,4096]{1,0:T(8,128)} %get-tuple-element.64.refs_0_.refs_1_.refs_3_, bf16[256,4096]{1,0:T(8,128)(2,1)S(1)} %collective-permute-done.20.refs_2_.refs_3_.refs_1_.refs_4_, ...), custom_call_target="tpu_custom_call" | custom-call | flops 1000 | bytes 1000 | tf_op jit(solution)/shard_map/pallas_call | solution.py:101
  94.4 6.1 %shard_map.41 = (f32[256,2048]{1,0:T(8,128)S(1)}, bf16[256,2048]{1,0:T(8,128)(2,1)}) custom-call(bf16[512,1152]{1,0:T(8,128)(2,1)S(1)} %shard_map.35.refs_4_.refs_0_, bf16[8192,1152]{1,0:T(8,128)(2,1)} %refs_1_.11, bf16[128,2048]{1,0:T(8,128)(2,1)S(1)} %get-tuple-element.65.refs_2_), custom_call_target="tpu_custom_call" | custom-call | flops 1000 | bytes 1000 | tf_op jit(solution)/shard_map/pallas_call | solution.py:101
  100.7 3.2 %collective-permute-start.15 = (bf16[64,1024]{1,0:T(8,128)(2,1)S(1)}, bf16[64,1024]{1,0:T(8,128)(2,1)S(1)}, u32[]{:S(2)}, u32[]{:S(2)}) collective-permute-start(bf16[64,1024]{1,0:T(8,128)(2,1)S(1)} %get-tuple-element.61.refs_7_), channel_id=1, source_target_pairs={{0,6},{1,7},{2,0},{3,1},{4,2},{5,3},{6,4},{7,5},{8,14},{9,15},{10,... | collective-permute-start | bytes 393224 | tf_op jit(solution)/shard_map/ppermute | solution.py:304
  107.6 2.0 %shard_map.42 = (bf16[64,2048]{1,0:T(8,128)(2,1)}, bf16[64,2048]{1,0:T(8,128)(2,1)}) custom-call(f32[256,4096]{1,0:T(8,128)} %get-tuple-element.57.refs_0_.refs_1_.refs_3_, bf16[256,4096]{1,0:T(8,128)(2,1)S(1)} %collective-permute-done.13.refs_2_.refs_3_.refs_1_.refs_4_, bf16[128,2048]{1,0:T(8,128)(2,1)S(1)} %copy-done.17, ...), custom_call_target="tpu_custom_call" | custom-call | flops 1000 | bytes 1000 | tf_op jit(solution)/shard_map/pallas_call | solution.py:101
  110.0 5.8 %shard_map.44 = (f32[256,2048]{1,0:T(8,128)S(1)}, bf16[256,2048]{1,0:T(8,128)(2,1)}) custom-call(bf16[512,1152]{1,0:T(8,128)(2,1)S(1)} %shard_map.35.refs_4_.refs_0_, bf16[8192,1152]{1,0:T(8,128)(2,1)} %refs_1_.11, f32[64,8192]{1,0:T(8,128)S(1)} %shard_map.43.refs_2_.refs_6_), custom_call_target="tpu_custom_call" | custom-call | flops 1000 | bytes 1000 | tf_op jit(solution)/shard_map/pallas_call | solution.py:101
  115.9 3.2 %collective-permute-start.25 = (bf16[128,2048]{1,0:T(8,128)(2,1)S(1)}, bf16[128,2048]{1,0:T(8,128)(2,1)S(1)}, u32[]{:S(2)}, u32[]{:S(2)}) collective-permute-start(bf16[128,2048]{1,0:T(8,128)(2,1)S(1)} %copy-done.33), channel_id=1, source_target_pairs={{0,6},{1,7},{2,0},{3,1},{4,2},{5,3},{6,4},{7,5},{8,14},{9,15},{10,... | collective-permute-start | bytes 1572872 | tf_op jit(solution)/shard_map/ppermute | solution.py:300
  119.2 3.2 %collective-permute-start.23 = (bf16[64,2048]{1,0:T(8,128)(2,1)}, bf16[64,2048]{1,0:T(8,128)(2,1)S(1)}, u32[]{:S(2)}, u32[]{:S(2)}) collective-permute-start(bf16[64,2048]{1,0:T(8,128)(2,1)} %get-tuple-element.67.refs_7_), channel_id=1, source_target_pairs={{0,6},{1,7},{2,0},{3,1},{4,2},{5,3},{6,4},{7,5},{8,14},{9,15},{10,... | collective-permute-start | bytes 786440 | tf_op jit(solution)/shard_map/ppermute | solution.py:304
  123.3 8.6 %collective-permute-done.24.refs_2_.refs_5_ = bf16[128,2048]{1,0:T(8,128)(2,1)S(1)} collective-permute-done((bf16[128,2048]{1,0:T(8,128)(2,1)S(1)}, bf16[128,2048]{1,0:T(8,128)(2,1)S(1)}, u32[]{:S(2)}, u32[]{:S(2)}) %collective-permute-start.24) | collective-permute-done | bytes 524320 | tf_op jit(solution)/shard_map/ppermute | solution.py:300
  131.9 3.3 %collective-permute-start.32 = (bf16[128,1024]{1,0:T(8,128)(2,1)}, bf16[128,1024]{1,0:T(8,128)(2,1)}, u32[]{:S(2)}, u32[]{:S(2)}) collective-permute-start(bf16[128,1024]{1,0:T(8,128)(2,1)} %get-tuple-element.73.refs_6_), channel_id=1, source_target_pairs={{0,6},{1,7},{2,0},{3,1},{4,2},{5,3},{6,4},{7,5},{8,14},{9,15},{10,... | collective-permute-start | bytes 786440 | tf_op jit(solution)/shard_map/ppermute | solution.py:300
  135.1 2.0 %shard_map.46 = (bf16[64,2048]{1,0:T(8,128)(2,1)}, bf16[64,2048]{1,0:T(8,128)(2,1)}) custom-call(f32[256,4096]{1,0:T(8,128)} %get-tuple-element.64.refs_0_.refs_1_.refs_3_, bf16[256,4096]{1,0:T(8,128)(2,1)S(1)} %collective-permute-done.20.refs_2_.refs_3_.refs_1_.refs_4_, bf16[128,2048]{1,0:T(8,128)(2,1)S(1)} %collective-permute-done.24.refs_2_.refs_5_, ...), custom_call_target="tpu_custom_call" | custom-call | flops 1000 | bytes 1000 | tf_op jit(solution)/shard_map/pallas_call | solution.py:101
  138.9 3.2 %collective-permute-start.30 = (bf16[64,2048]{1,0:T(8,128)(2,1)}, bf16[64,2048]{1,0:T(8,128)(2,1)}, u32[]{:S(2)}, u32[]{:S(2)}) collective-permute-start(bf16[64,2048]{1,0:T(8,128)(2,1)} %get-tuple-element.74.refs_7_), channel_id=1, source_target_pairs={{0,6},{1,7},{2,0},{3,1},{4,2},{5,3},{6,4},{7,5},{8,14},{9,15},{10,... | collective-permute-start | bytes 786440 | tf_op jit(solution)/shard_map/ppermute | solution.py:304
  142.1 1.6 copy-done.7
  147.7 2.5 %shard_map.47.refs_4_.refs_6_ = f32[64,8192]{1,0:T(8,128)S(1)} custom-call(f32[256,4096]{1,0:T(8,128)} %get-tuple-element.57.refs_0_.refs_1_.refs_3_, bf16[256,4096]{1,0:T(8,128)(2,1)S(1)} %copy-done.7, bf16[64,2048]{1,0:T(8,128)(2,1)S(1)} %copy-done.35, bf16[128,2048]{1,0:T(8,128)(2,1)S(1)} %copy-done.21, ...), custom_call_target="tpu_custom_call", output_to_operand_aliasing={{}: (6, {})} | custom-call | flops 1000 | bytes 1000 | tf_op jit(solution)/shard_map/pallas_call | solution.py:101
  150.3 2.1 %shard_map.48 = (bf16[128,1024]{1,0:T(8,128)(2,1)S(1)}, bf16[128,1024]{1,0:T(8,128)(2,1)S(1)}) custom-call(f32[256,2048]{1,0:T(8,128)S(1)} %copy-done.9, f32[256,2048]{1,0:T(8,128)S(1)} %copy-done.9, bf16[256,2048]{1,0:T(8,128)(2,1)} %collective-permute-done.21.refs_2_.refs_3_.refs_1_.refs_4_, ...), custom_call_target="tpu_custom_call" | custom-call | flops 1000 | bytes 1000 | tf_op jit(solution)/shard_map/pallas_call | solution.py:101
  152.5 3.3 %collective-permute-start.28 = (bf16[128,1024]{1,0:T(8,128)(2,1)S(1)}, bf16[128,1024]{1,0:T(8,128)(2,1)S(1)}, u32[]{:S(2)}, u32[]{:S(2)}) collective-permute-start(bf16[128,1024]{1,0:T(8,128)(2,1)S(1)} %get-tuple-element.76.refs_6_), channel_id=1, source_target_pairs={{0,6},{1,7},{2,0},{3,1},{4,2},{5,3},{6,4},{7,5},{8,14},{9,15},{10,... | collective-permute-start | bytes 786440 | tf_op jit(solution)/shard_map/ppermute | solution.py:300
  156.9 2.9 %shard_map.50 = (f32[64,4096]{1,0:T(8,128)S(1)}, bf16[64,4096]{1,0:T(8,128)(2,1)S(1)}) custom-call(f32[256,4096]{1,0:T(8,128)} %get-tuple-element.64.refs_0_.refs_1_.refs_3_, bf16[256,4096]{1,0:T(8,128)(2,1)S(1)} %copy-done.5, bf16[64,2048]{1,0:T(8,128)(2,1)} %collective-permute-done.29.refs_2_, bf16[128,2048]{1,0:T(8,128)(2,1)S(1)} %copy-done.25, ...), custom_call_target="tpu_custom_call" | custom-call | flops 1000 | bytes 1000 | tf_op jit(solution)/shard_map/pallas_call | solution.py:101
  159.9 1.1 collective-permute-start.38
  161.0 3.2 %collective-permute-start.36 = (bf16[64,1024]{1,0:T(8,128)(2,1)S(1)}, bf16[64,1024]{1,0:T(8,128)(2,1)S(1)}, u32[]{:S(2)}, u32[]{:S(2)}) collective-permute-start(bf16[64,1024]{1,0:T(8,128)(2,1)S(1)} %get-tuple-element.79.refs_8_), channel_id=1, source_target_pairs={{0,6},{1,7},{2,0},{3,1},{4,2},{5,3},{6,4},{7,5},{8,14},{9,15},{10,... | collective-permute-start | bytes 393224 | tf_op jit(solution)/shard_map/ppermute | solution.py:304
  165.3 1.9 collective-permute-done.35.refs_2_
  167.1 1.3 shard_map.52
  169.5 3.2 %collective-permute-start.34 = (bf16[64,1024]{1,0:T(8,128)(2,1)S(1)}, bf16[64,1024]{1,0:T(8,128)(2,1)S(1)}, u32[]{:S(2)}, u32[]{:S(2)}) collective-permute-start(bf16[64,1024]{1,0:T(8,128)(2,1)S(1)} %get-tuple-element.82.refs_8_), channel_id=1, source_target_pairs={{0,6},{1,7},{2,0},{3,1},{4,2},{5,3},{6,4},{7,5},{8,14},{9,15},{10,... | collective-permute-start | bytes 393224 | tf_op jit(solution)/shard_map/ppermute | solution.py:304
  172.8 1.9 collective-permute-done.38.refs_1_
  175.1 1.3 copy.13.refs_2_
  178.3 1.3 shard_map.55
  179.6 1.1 collective-permute-start.39
  180.7 5.3 %collective-permute-done.39.refs_1_ = bf16[64,2048]{1,0:T(8,128)(2,1)S(1)} collective-permute-done((bf16[64,2048]{1,0:T(8,128)(2,1)S(1)}, bf16[64,2048]{1,0:T(8,128)(2,1)S(1)}, u32[]{:S(2)}, u32[]{:S(2)}) %collective-permute-start.39) | collective-permute-done | bytes 262176 | tf_op jit(solution)/shard_map/ppermute | solution.py:311
  (146 shorter events, 26.7 us)
Async XLA Ops:
  1.0 11.0 %collective-permute-start = (bf16[128,1152]{1,0:T(8,128)(2,1)S(1)}, bf16[128,1152]{1,0:T(8,128)(2,1)S(1)}, u32[]{:S(2)}, u32[]{:S(2)}) collective-permute-start(bf16[128,1152]{1,0:T(8,128)(2,1)S(1)} %multiply_convert_fusion.refs_1_), channel_id=1, source_target_pairs={{0,64},{16,80},{32,96},{48,112},{64,0},{80,16},{96,32},{112,48},{1... | collective-permute-start | bytes 884744 | tf_op jit(solution)/shard_map/ppermute | solution.py:272
  5.1 11.4 %collective-permute-start.2 = (bf16[128,1152]{1,0:T(8,128)(2,1)S(1)}, bf16[128,1152]{1,0:T(8,128)(2,1)S(1)}, u32[]{:S(2)}, u32[]{:S(2)}) collective-permute-start(bf16[128,1152]{1,0:T(8,128)(2,1)S(1)} %multiply_convert_fusion.refs_1_), channel_id=1, source_target_pairs={{0,32},{16,48},{32,0},{48,16},{64,96},{80,112},{96,64},{112,80},{1... | collective-permute-start | bytes 884744 | tf_op jit(solution)/shard_map/ppermute | solution.py:271
  8.3 13.5 %collective-permute-start.5 = (bf16[128,1152]{1,0:T(8,128)(2,1)S(1)}, bf16[128,1152]{1,0:T(8,128)(2,1)S(1)}, u32[]{:S(2)}, u32[]{:S(2)}) collective-permute-start(bf16[128,1152]{1,0:T(8,128)(2,1)S(1)} %multiply_convert_fusion.refs_1_), channel_id=1, source_target_pairs={{16,0},{32,16},{48,32},{0,48},{80,64},{96,80},{112,96},{64,112},{1... | collective-permute-start | bytes 884744 | tf_op jit(solution)/shard_map/ppermute | solution.py:270
  9.3 12.4 %collective-permute-start.6 = (bf16[128,1152]{1,0:T(8,128)(2,1)S(1)}, bf16[128,1152]{1,0:T(8,128)(2,1)S(1)}, u32[]{:S(2)}, u32[]{:S(2)}) collective-permute-start(bf16[128,1152]{1,0:T(8,128)(2,1)S(1)} %multiply_convert_fusion.refs_1_), channel_id=1, source_target_pairs={{0,16},{16,32},{32,48},{48,0},{64,80},{80,96},{96,112},{112,64},{1... | collective-permute-start | bytes 884744 | tf_op jit(solution)/shard_map/ppermute | solution.py:269
  27.4 33.2 %copy-start.12 = (f32[256,2048]{1,0:T(8,128)}, f32[256,2048]{1,0:T(8,128)S(1)}, u32[]{:S(2)}) copy-start(f32[256,2048]{1,0:T(8,128)S(1)} %get-tuple-element.47.refs_0_.refs_1_.refs_3_) | copy-start | bytes 6291460
  27.4 13.4 %collective-permute-start.7 = (bf16[256,2048]{1,0:T(8,128)(2,1)S(1)}, bf16[256,2048]{1,0:T(8,128)(2,1)S(1)}, u32[]{:S(2)}, u32[]{:S(2)}) collective-permute-start(bf16[256,2048]{1,0:T(8,128)(2,1)S(1)} %get-tuple-element.48.refs_2_), channel_id=1, source_target_pairs={{0,1},{1,0},{2,3},{3,2},{4,5},{5,4},{6,7},{7,6},{8,9},{9,8},{10,11... | collective-permute-start | bytes 3145736 | tf_op jit(solution)/shard_map/ppermute | solution.py:294
  27.5 9.6 %collective-permute-start.1 = (bf16[128,1152]{1,0:T(8,128)(2,1)S(1)}, bf16[128,1152]{1,0:T(8,128)(2,1)S(1)}, u32[]{:S(2)}, u32[]{:S(2)}) collective-permute-start(bf16[128,1152]{1,0:T(8,128)(2,1)S(1)} %collective-permute-done.refs_5_.refs_1_), channel_id=1, source_target_pairs={{16,0},{32,16},{48,32},{0,48},{80,64},{96,80},{112,96},{64,112},{1... | collective-permute-start | bytes 884744 | tf_op jit(solution)/shard_map/ppermute | solution.py:274
  30.2 10.3 %collective-permute-start.4 = (bf16[128,1152]{1,0:T(8,128)(2,1)S(1)}, bf16[128,1152]{1,0:T(8,128)(2,1)S(1)}, u32[]{:S(2)}, u32[]{:S(2)}) collective-permute-start(bf16[128,1152]{1,0:T(8,128)(2,1)S(1)} %collective-permute-done.refs_5_.refs_1_), channel_id=1, source_target_pairs={{0,16},{16,32},{32,48},{48,0},{64,80},{80,96},{96,112},{112,64},{1... | collective-permute-start | bytes 884744 | tf_op jit(solution)/shard_map/ppermute | solution.py:274
  30.2 10.6 %collective-permute-start.3 = (bf16[128,1152]{1,0:T(8,128)(2,1)S(1)}, bf16[128,1152]{1,0:T(8,128)(2,1)S(1)}, u32[]{:S(2)}, u32[]{:S(2)}) collective-permute-start(bf16[128,1152]{1,0:T(8,128)(2,1)S(1)} %collective-permute-done.2.refs_3_), channel_id=1, source_target_pairs={{0,64},{16,80},{32,96},{48,112},{64,0},{80,16},{96,32},{112,48},{1... | collective-permute-start | bytes 884744 | tf_op jit(solution)/shard_map/ppermute | solution.py:274
  35.6 53.6 %copy-start.10 = (f32[256,2048]{1,0:T(8,128)}, f32[256,2048]{1,0:T(8,128)S(1)}, u32[]{:S(2)}) copy-start(f32[256,2048]{1,0:T(8,128)S(1)} %get-tuple-element.52.refs_0_.refs_1_.refs_3_) | copy-start | bytes 6291460
  50.7 11.3 %collective-permute-start.13 = (bf16[256,4096]{1,0:T(8,128)(2,1)}, bf16[256,4096]{1,0:T(8,128)(2,1)S(1)}, u32[]{:S(2)}, u32[]{:S(2)}) collective-permute-start(bf16[256,4096]{1,0:T(8,128)(2,1)} %get-tuple-element.53.refs_4_), channel_id=1, source_target_pairs={{0,1},{1,0},{2,3},{3,2},{4,5},{5,4},{6,7},{7,6},{8,9},{9,8},{10,11... | collective-permute-start | bytes 6291464 | tf_op jit(solution)/shard_map/ppermute | solution.py:294
  50.7 5.3 %collective-permute-start.10 = (bf16[256,2048]{1,0:T(8,128)(2,1)S(1)}, bf16[256,2048]{1,0:T(8,128)(2,1)S(1)}, u32[]{:S(2)}, u32[]{:S(2)}) collective-permute-start(bf16[256,2048]{1,0:T(8,128)(2,1)S(1)} %get-tuple-element.49.refs_4_), channel_id=1, source_target_pairs={{0,1},{1,0},{2,3},{3,2},{4,5},{5,4},{6,7},{7,6},{8,9},{9,8},{10,11... | collective-permute-start | bytes 3145736 | tf_op jit(solution)/shard_map/ppermute | solution.py:294
  51.2 9.4 %collective-permute-start.8 = (bf16[128,1024]{1,0:T(8,128)(2,1)S(1)}, bf16[128,1024]{1,0:T(8,128)(2,1)S(1)}, u32[]{:S(2)}, u32[]{:S(2)}) collective-permute-start(bf16[128,1024]{1,0:T(8,128)(2,1)S(1)} %get-tuple-element.50), channel_id=1, source_target_pairs={{0,2},{1,3},{2,4},{3,5},{4,6},{5,7},{6,0},{7,1},{8,10},{9,11},{10,... | collective-permute-start | bytes 786440 | tf_op jit(solution)/shard_map/ppermute | solution.py:300
  52.7 7.9 %collective-permute-start.9 = (bf16[128,1024]{1,0:T(8,128)(2,1)S(1)}, bf16[128,1024]{1,0:T(8,128)(2,1)S(1)}, u32[]{:S(2)}, u32[]{:S(2)}) collective-permute-start(bf16[128,1024]{1,0:T(8,128)(2,1)S(1)} %get-tuple-element.51.refs_2_), channel_id=1, source_target_pairs={{0,6},{1,7},{2,0},{3,1},{4,2},{5,3},{6,4},{7,5},{8,14},{9,15},{10,... | collective-permute-start | bytes 786440 | tf_op jit(solution)/shard_map/ppermute | solution.py:300
  56.0 33.2 %copy-start.14 = (bf16[256,2048]{1,0:T(8,128)(2,1)}, bf16[256,2048]{1,0:T(8,128)(2,1)S(1)}, u32[]{:S(2)}) copy-start(bf16[256,2048]{1,0:T(8,128)(2,1)S(1)} %collective-permute-done.10.refs_2_.refs_3_.refs_1_.refs_4_) | copy-start | bytes 3145732
  62.0 42.7 %copy-start.6 = (bf16[256,4096]{1,0:T(8,128)(2,1)}, bf16[256,4096]{1,0:T(8,128)(2,1)S(1)}, u32[]{:S(2)}) copy-start(bf16[256,4096]{1,0:T(8,128)(2,1)S(1)} %collective-permute-done.13.refs_2_.refs_3_.refs_1_.refs_4_) | copy-start | bytes 6291460
  75.6 15.6 %collective-permute-start.20 = (bf16[256,4096]{1,0:T(8,128)(2,1)}, bf16[256,4096]{1,0:T(8,128)(2,1)S(1)}, u32[]{:S(2)}, u32[]{:S(2)}) collective-permute-start(bf16[256,4096]{1,0:T(8,128)(2,1)} %get-tuple-element.59.refs_6_), channel_id=1, source_target_pairs={{0,1},{1,0},{2,3},{3,2},{4,5},{5,4},{6,7},{7,6},{8,9},{9,8},{10,11... | collective-permute-start | bytes 6291464 | tf_op jit(solution)/shard_map/ppermute | solution.py:294
  75.6 10.3 %collective-permute-start.11 = (bf16[128,1024]{1,0:T(8,128)(2,1)S(1)}, bf16[128,1024]{1,0:T(8,128)(2,1)S(1)}, u32[]{:S(2)}, u32[]{:S(2)}) collective-permute-start(bf16[128,1024]{1,0:T(8,128)(2,1)S(1)} %get-tuple-element.56), channel_id=1, source_target_pairs={{0,2},{1,3},{2,4},{3,5},{4,6},{5,7},{6,0},{7,1},{8,10},{9,11},{10,... | collective-permute-start | bytes 786440 | tf_op jit(solution)/shard_map/ppermute | solution.py:300
  77.1 9.1 %collective-permute-start.12 = (bf16[128,1024]{1,0:T(8,128)(2,1)S(1)}, bf16[128,1024]{1,0:T(8,128)(2,1)S(1)}, u32[]{:S(2)}, u32[]{:S(2)}) collective-permute-start(bf16[128,1024]{1,0:T(8,128)(2,1)S(1)} %get-tuple-element.54.refs_6_), channel_id=1, source_target_pairs={{0,6},{1,7},{2,0},{3,1},{4,2},{5,3},{6,4},{7,5},{8,14},{9,15},{10,... | collective-permute-start | bytes 786440 | tf_op jit(solution)/shard_map/ppermute | solution.py:300
  78.8 10.5 %collective-permute-start.16 = (bf16[64,1024]{1,0:T(8,128)(2,1)S(1)}, bf16[64,1024]{1,0:T(8,128)(2,1)S(1)}, u32[]{:S(2)}, u32[]{:S(2)}) collective-permute-start(bf16[64,1024]{1,0:T(8,128)(2,1)S(1)} %get-tuple-element.62), channel_id=1, source_target_pairs={{0,2},{1,3},{2,4},{3,5},{4,6},{5,7},{6,0},{7,1},{8,10},{9,11},{10,... | collective-permute-start | bytes 393224 | tf_op jit(solution)/shard_map/ppermute | solution.py:304
  79.1 10.2 %collective-permute-start.17 = (bf16[64,1024]{1,0:T(8,128)(2,1)S(1)}, bf16[64,1024]{1,0:T(8,128)(2,1)S(1)}, u32[]{:S(2)}, u32[]{:S(2)}) collective-permute-start(bf16[64,1024]{1,0:T(8,128)(2,1)S(1)} %get-tuple-element.55.refs_5_), channel_id=1, source_target_pairs={{0,6},{1,7},{2,0},{3,1},{4,2},{5,3},{6,4},{7,5},{8,14},{9,15},{10,... | collective-permute-start | bytes 393224 | tf_op jit(solution)/shard_map/ppermute | solution.py:304
  85.9 18.0 %collective-permute-start.18 = (bf16[128,2048]{1,0:T(8,128)(2,1)}, bf16[128,2048]{1,0:T(8,128)(2,1)S(1)}, u32[]{:S(2)}, u32[]{:S(2)}) collective-permute-start(bf16[128,2048]{1,0:T(8,128)(2,1)} %get-tuple-element.63), channel_id=1, source_target_pairs={{0,2},{1,3},{2,4},{3,5},{4,6},{5,7},{6,0},{7,1},{8,10},{9,11},{10,... | collective-permute-start | bytes 1572872 | tf_op jit(solution)/shard_map/ppermute | solution.py:300
  86.2 18.4 %collective-permute-start.19 = (bf16[128,2048]{1,0:T(8,128)(2,1)}, bf16[128,2048]{1,0:T(8,128)(2,1)S(1)}, u32[]{:S(2)}, u32[]{:S(2)}) collective-permute-start(bf16[128,2048]{1,0:T(8,128)(2,1)} %get-tuple-element.58.refs_2_), channel_id=1, source_target_pairs={{0,6},{1,7},{2,0},{3,1},{4,2},{5,3},{6,4},{7,5},{8,14},{9,15},{10,... | collective-permute-start | bytes 1572872 | tf_op jit(solution)/shard_map/ppermute | solution.py:300
  91.2 43.9 %copy-start.4 = (bf16[256,4096]{1,0:T(8,128)(2,1)}, bf16[256,4096]{1,0:T(8,128)(2,1)S(1)}, u32[]{:S(2)}) copy-start(bf16[256,4096]{1,0:T(8,128)(2,1)S(1)} %collective-permute-done.20.refs_2_.refs_3_.refs_1_.refs_4_) | copy-start | bytes 6291460
  100.5 21.9 %copy-start.2 = (f32[256,2048]{1,0:T(8,128)}, f32[256,2048]{1,0:T(8,128)S(1)}, u32[]{:S(2)}) copy-start(f32[256,2048]{1,0:T(8,128)S(1)} %get-tuple-element.72.refs_0_.refs_1_.refs_3_) | copy-start | bytes 6291460
  100.5 18.7 %collective-permute-start.26 = (bf16[256,2048]{1,0:T(8,128)(2,1)}, bf16[256,2048]{1,0:T(8,128)(2,1)S(1)}, u32[]{:S(2)}, u32[]{:S(2)}) collective-permute-start(bf16[256,2048]{1,0:T(8,128)(2,1)} %get-tuple-element.66.refs_6_), channel_id=1, source_target_pairs={{0,1},{1,0},{2,3},{3,2},{4,5},{5,4},{6,7},{7,6},{8,9},{9,8},{10,11... | collective-permute-start | bytes 3145736 | tf_op jit(solution)/shard_map/ppermute | solution.py:294
  100.6 9.1 %copy-start.11 = (f32[256,2048]{1,0:T(8,128)S(1)}, f32[256,2048]{1,0:T(8,128)}, u32[]{:S(2)}) copy-start(f32[256,2048]{1,0:T(8,128)} %copy-done.10) | copy-start | bytes 6291460
  100.6 9.1 %copy-start.15 = (bf16[256,2048]{1,0:T(8,128)(2,1)S(1)}, bf16[256,2048]{1,0:T(8,128)(2,1)}, u32[]{:S(2)}) copy-start(bf16[256,2048]{1,0:T(8,128)(2,1)} %copy-done.14) | copy-start | bytes 3145732
  100.6 9.0 %collective-permute-start.14 = (bf16[64,1024]{1,0:T(8,128)(2,1)S(1)}, bf16[64,1024]{1,0:T(8,128)(2,1)S(1)}, u32[]{:S(2)}, u32[]{:S(2)}) collective-permute-start(bf16[64,1024]{1,0:T(8,128)(2,1)S(1)} %get-tuple-element.60), channel_id=1, source_target_pairs={{0,2},{1,3},{2,4},{3,5},{4,6},{5,7},{6,0},{7,1},{8,10},{9,11},{10,... | collective-permute-start | bytes 393224 | tf_op jit(solution)/shard_map/ppermute | solution.py:304
  100.7 9.0 %collective-permute-start.15 = (bf16[64,1024]{1,0:T(8,128)(2,1)S(1)}, bf16[64,1024]{1,0:T(8,128)(2,1)S(1)}, u32[]{:S(2)}, u32[]{:S(2)}) collective-permute-start(bf16[64,1024]{1,0:T(8,128)(2,1)S(1)} %get-tuple-element.61.refs_7_), channel_id=1, source_target_pairs={{0,6},{1,7},{2,0},{3,1},{4,2},{5,3},{6,4},{7,5},{8,14},{9,15},{10,... | collective-permute-start | bytes 393224 | tf_op jit(solution)/shard_map/ppermute | solution.py:304
  115.8 34.4 %collective-permute-start.21 = (bf16[256,2048]{1,0:T(8,128)(2,1)}, bf16[256,2048]{1,0:T(8,128)(2,1)}, u32[]{:S(2)}, u32[]{:S(2)}) collective-permute-start(bf16[256,2048]{1,0:T(8,128)(2,1)} %get-tuple-element.69.refs_4_), channel_id=1, source_target_pairs={{0,1},{1,0},{2,3},{3,2},{4,5},{5,4},{6,7},{7,6},{8,9},{9,8},{10,11... | collective-permute-start | bytes 3145736 | tf_op jit(solution)/shard_map/ppermute | solution.py:294
  115.8 16.0 %collective-permute-start.24 = (bf16[128,2048]{1,0:T(8,128)(2,1)S(1)}, bf16[128,2048]{1,0:T(8,128)(2,1)S(1)}, u32[]{:S(2)}, u32[]{:S(2)}) collective-permute-start(bf16[128,2048]{1,0:T(8,128)(2,1)S(1)} %copy-done.39), channel_id=1, source_target_pairs={{0,2},{1,3},{2,4},{3,5},{4,6},{5,7},{6,0},{7,1},{8,10},{9,11},{10,... | collective-permute-start | bytes 1572872 | tf_op jit(solution)/shard_map/ppermute | solution.py:300
  115.9 15.9 %collective-permute-start.25 = (bf16[128,2048]{1,0:T(8,128)(2,1)S(1)}, bf16[128,2048]{1,0:T(8,128)(2,1)S(1)}, u32[]{:S(2)}, u32[]{:S(2)}) collective-permute-start(bf16[128,2048]{1,0:T(8,128)(2,1)S(1)} %copy-done.33), channel_id=1, source_target_pairs={{0,6},{1,7},{2,0},{3,1},{4,2},{5,3},{6,4},{7,5},{8,14},{9,15},{10,... | collective-permute-start | bytes 1572872 | tf_op jit(solution)/shard_map/ppermute | solution.py:300
  119.2 18.3 %collective-permute-start.22 = (bf16[64,2048]{1,0:T(8,128)(2,1)}, bf16[64,2048]{1,0:T(8,128)(2,1)S(1)}, u32[]{:S(2)}, u32[]{:S(2)}) collective-permute-start(bf16[64,2048]{1,0:T(8,128)(2,1)} %get-tuple-element.70), channel_id=1, source_target_pairs={{0,2},{1,3},{2,4},{3,5},{4,6},{5,7},{6,0},{7,1},{8,10},{9,11},{10,... | collective-permute-start | bytes 786440 | tf_op jit(solution)/shard_map/ppermute | solution.py:304
  119.2 19.0 %collective-permute-start.23 = (bf16[64,2048]{1,0:T(8,128)(2,1)}, bf16[64,2048]{1,0:T(8,128)(2,1)S(1)}, u32[]{:S(2)}, u32[]{:S(2)}) collective-permute-start(bf16[64,2048]{1,0:T(8,128)(2,1)} %get-tuple-element.67.refs_7_), channel_id=1, source_target_pairs={{0,6},{1,7},{2,0},{3,1},{4,2},{5,3},{6,4},{7,5},{8,14},{9,15},{10,... | collective-permute-start | bytes 786440 | tf_op jit(solution)/shard_map/ppermute | solution.py:304
  131.9 20.6 %collective-permute-start.31 = (bf16[128,1024]{1,0:T(8,128)(2,1)}, bf16[128,1024]{1,0:T(8,128)(2,1)S(1)}, u32[]{:S(2)}, u32[]{:S(2)}) collective-permute-start(bf16[128,1024]{1,0:T(8,128)(2,1)} %get-tuple-element.78), channel_id=1, source_target_pairs={{0,2},{1,3},{2,4},{3,5},{4,6},{5,7},{6,0},{7,1},{8,10},{9,11},{10,... | collective-permute-start | bytes 786440 | tf_op jit(solution)/shard_map/ppermute | solution.py:300
  131.9 23.9 %collective-permute-start.32 = (bf16[128,1024]{1,0:T(8,128)(2,1)}, bf16[128,1024]{1,0:T(8,128)(2,1)}, u32[]{:S(2)}, u32[]{:S(2)}) collective-permute-start(bf16[128,1024]{1,0:T(8,128)(2,1)} %get-tuple-element.73.refs_6_), channel_id=1, source_target_pairs={{0,6},{1,7},{2,0},{3,1},{4,2},{5,3},{6,4},{7,5},{8,14},{9,15},{10,... | collective-permute-start | bytes 786440 | tf_op jit(solution)/shard_map/ppermute | solution.py:300
  138.2 18.7 %collective-permute-start.29 = (bf16[64,2048]{1,0:T(8,128)(2,1)}, bf16[64,2048]{1,0:T(8,128)(2,1)}, u32[]{:S(2)}, u32[]{:S(2)}) collective-permute-start(bf16[64,2048]{1,0:T(8,128)(2,1)} %get-tuple-element.77), channel_id=1, source_target_pairs={{0,2},{1,3},{2,4},{3,5},{4,6},{5,7},{6,0},{7,1},{8,10},{9,11},{10,... | collective-permute-start | bytes 786440 | tf_op jit(solution)/shard_map/ppermute | solution.py:304
  138.9 18.0 %collective-permute-start.30 = (bf16[64,2048]{1,0:T(8,128)(2,1)}, bf16[64,2048]{1,0:T(8,128)(2,1)}, u32[]{:S(2)}, u32[]{:S(2)}) collective-permute-start(bf16[64,2048]{1,0:T(8,128)(2,1)} %get-tuple-element.74.refs_7_), channel_id=1, source_target_pairs={{0,6},{1,7},{2,0},{3,1},{4,2},{5,3},{6,4},{7,5},{8,14},{9,15},{10,... | collective-permute-start | bytes 786440 | tf_op jit(solution)/shard_map/ppermute | solution.py:304
  152.4 11.8 %collective-permute-start.27 = (bf16[128,1024]{1,0:T(8,128)(2,1)S(1)}, bf16[128,1024]{1,0:T(8,128)(2,1)S(1)}, u32[]{:S(2)}, u32[]{:S(2)}) collective-permute-start(bf16[128,1024]{1,0:T(8,128)(2,1)S(1)} %get-tuple-element.75), channel_id=1, source_target_pairs={{0,2},{1,3},{2,4},{3,5},{4,6},{5,7},{6,0},{7,1},{8,10},{9,11},{10,... | collective-permute-start | bytes 786440 | tf_op jit(solution)/shard_map/ppermute | solution.py:300
  152.5 11.7 %collective-permute-start.28 = (bf16[128,1024]{1,0:T(8,128)(2,1)S(1)}, bf16[128,1024]{1,0:T(8,128)(2,1)S(1)}, u32[]{:S(2)}, u32[]{:S(2)}) collective-permute-start(bf16[128,1024]{1,0:T(8,128)(2,1)S(1)} %get-tuple-element.76.refs_6_), channel_id=1, source_target_pairs={{0,6},{1,7},{2,0},{3,1},{4,2},{5,3},{6,4},{7,5},{8,14},{9,15},{10,... | collective-permute-start | bytes 786440 | tf_op jit(solution)/shard_map/ppermute | solution.py:300
  159.9 14.8 %collective-permute-start.38 = (bf16[64,4096]{1,0:T(8,128)(2,1)S(1)}, bf16[64,4096]{1,0:T(8,128)(2,1)S(1)}, u32[]{:S(2)}, u32[]{:S(2)}) collective-permute-start(bf16[64,4096]{1,0:T(8,128)(2,1)S(1)} %get-tuple-element.80.refs_6_), channel_id=1, source_target_pairs={{0,8},{1,9},{2,10},{3,11},{4,12},{5,13},{6,14},{7,15},{8,0},{9,1},... | collective-permute-start | bytes 1572872 | tf_op jit(solution)/shard_map/ppermute | solution.py:311
  161.0 6.2 %collective-permute-start.35 = (bf16[64,1024]{1,0:T(8,128)(2,1)S(1)}, bf16[64,1024]{1,0:T(8,128)(2,1)S(1)}, u32[]{:S(2)}, u32[]{:S(2)}) collective-permute-start(bf16[64,1024]{1,0:T(8,128)(2,1)S(1)} %get-tuple-element.83), channel_id=1, source_target_pairs={{0,2},{1,3},{2,4},{3,5},{4,6},{5,7},{6,0},{7,1},{8,10},{9,11},{10,... | collective-permute-start | bytes 393224 | tf_op jit(solution)/shard_map/ppermute | solution.py:304
  161.0 6.2 %collective-permute-start.36 = (bf16[64,1024]{1,0:T(8,128)(2,1)S(1)}, bf16[64,1024]{1,0:T(8,128)(2,1)S(1)}, u32[]{:S(2)}, u32[]{:S(2)}) collective-permute-start(bf16[64,1024]{1,0:T(8,128)(2,1)S(1)} %get-tuple-element.79.refs_8_), channel_id=1, source_target_pairs={{0,6},{1,7},{2,0},{3,1},{4,2},{5,3},{6,4},{7,5},{8,14},{9,15},{10,... | collective-permute-start | bytes 393224 | tf_op jit(solution)/shard_map/ppermute | solution.py:304
  168.4 9.0 %collective-permute-start.37 = (bf16[64,2048]{1,0:T(8,128)(2,1)S(1)}, bf16[64,2048]{1,0:T(8,128)(2,1)S(1)}, u32[]{:S(2)}, u32[]{:S(2)}) collective-permute-start(bf16[64,2048]{1,0:T(8,128)(2,1)S(1)} %get-tuple-element.85.refs_3_), channel_id=1, source_target_pairs={{0,8},{1,9},{2,10},{3,11},{4,12},{5,13},{6,14},{7,15},{8,0},{9,1},... | collective-permute-start | bytes 786440 | tf_op jit(solution)/shard_map/ppermute | solution.py:311
  169.5 8.8 %collective-permute-start.33 = (bf16[64,1024]{1,0:T(8,128)(2,1)S(1)}, bf16[64,1024]{1,0:T(8,128)(2,1)S(1)}, u32[]{:S(2)}, u32[]{:S(2)}) collective-permute-start(bf16[64,1024]{1,0:T(8,128)(2,1)S(1)} %get-tuple-element.81), channel_id=1, source_target_pairs={{0,2},{1,3},{2,4},{3,5},{4,6},{5,7},{6,0},{7,1},{8,10},{9,11},{10,... | collective-permute-start | bytes 393224 | tf_op jit(solution)/shard_map/ppermute | solution.py:304
  169.5 8.8 %collective-permute-start.34 = (bf16[64,1024]{1,0:T(8,128)(2,1)S(1)}, bf16[64,1024]{1,0:T(8,128)(2,1)S(1)}, u32[]{:S(2)}, u32[]{:S(2)}) collective-permute-start(bf16[64,1024]{1,0:T(8,128)(2,1)S(1)} %get-tuple-element.82.refs_8_), channel_id=1, source_target_pairs={{0,6},{1,7},{2,0},{3,1},{4,2},{5,3},{6,4},{7,5},{8,14},{9,15},{10,... | collective-permute-start | bytes 393224 | tf_op jit(solution)/shard_map/ppermute | solution.py:304
  179.6 6.5 %collective-permute-start.39 = (bf16[64,2048]{1,0:T(8,128)(2,1)S(1)}, bf16[64,2048]{1,0:T(8,128)(2,1)S(1)}, u32[]{:S(2)}, u32[]{:S(2)}) collective-permute-start(bf16[64,2048]{1,0:T(8,128)(2,1)S(1)} %get-tuple-element.88.refs_3_), channel_id=1, source_target_pairs={{0,8},{1,9},{2,10},{3,11},{4,12},{5,13},{6,14},{7,15},{8,0},{9,1},... | collective-permute-start | bytes 786440 | tf_op jit(solution)/shard_map/ppermute | solution.py:311
  (32 other events, 95.9 us)

commit v2 on v0

v2 whole, which is shorter than its diff:
```python
import jax
import jax.numpy as jnp
from jax import lax
from jax.experimental import pallas as pl
from jax.experimental.pallas import tpu as pltpu
from jax.sharding import PartitionSpec as P

F32, BF16 = jnp.float32, jnp.bfloat16
SLAB_DEV = 128
LONG = 100_000_000
HALF = 64
CHIP = 128
VMEM = 20 * 1024 * 1024

Y_UP = [(z * 4 + y, z * 4 + (y + 1) % 4) for z in range(2) for y in range(4)]
Y_DOWN = [(d, s) for s, d in Y_UP]
Y_FAR = [(z * 4 + y, z * 4 + (y + 2) % 4) for z in range(2) for y in range(4)]
Z_FAR = [(z * 4 + y, (1 - z) * 4 + y) for z in range(2) for y in range(4)]


def gc(z, x, c):
    return (z * 4 + x % 4) * 2 + c


EACH = [(z, x, c) for z in range(2) for x in range(4) for c in range(2)]
X_UP = [(gc(z, x, c), gc(z, x + 1, c)) for z, x, c in EACH]
X_DOWN = [(gc(z, x, c), gc(z, x - 1, c)) for z, x, c in EACH]
Z_NEAR = [(gc(z, x, c), gc(1 - z, x, c)) for z, x, c in EACH]
CORE = [(gc(z, x, c), gc(z, x, 1 - c)) for z, x, c in EACH]

UNITS = [256, 512, 256]
PLAN = [
    ("cut", 0),
    ("cut", 1),
    ("cut", 2),
    ("order", 0),
    ("product", (0, 0)),
    ("send", (0, 0), None),
    ("product", (0, 1)),
    ("send", (0, 1), (0, 0)),
    ("order", 1),
    ("product", (1, 1)),
    ("product", (2, 2)),
    ("send", (1, 1), (0, 1)),
    ("product", (1, 0)),
    ("sum", (0, 0)),
    ("send", (1, 0), (1, 1)),
    ("sum", (0, 1)),
    ("send", (2, 2), (1, 0)),
    ("sum", (1, 1)),
    ("sum", (1, 0)),
    ("send", None, (2, 2)),
    ("swap", (1, 1)),
    ("sum", (2, 2)),
    ("swap", (1, 0)),
]


def dot(s, a):
    return lax.dot_general(s, a, (((1,), (1,)), ((), ())), preferred_element_type=F32)


def cost(flops, nbytes):
    return pl.CostEstimate(flops=flops, bytes_accessed=nbytes, transcendentals=0)


def params():
    return pltpu.CompilerParams(vmem_limit_bytes=VMEM)


def run(kernel, grid, outs, ins, dep, nbytes=1000):
    shapes = [jax.ShapeDtypeStruct(shape, dtype) for (shape, dtype), _, _ in outs]
    spec = lambda block, where: pl.BlockSpec(block, where) if block else pl.BlockSpec(memory_space=where)
    out_specs = [spec(block, where) for _, block, where in outs]
    in_specs = [spec(block, where) for _, block, where in ins]
    arrays = [array for array, _, _ in ins]
    arrays += dep
    in_specs += [pl.BlockSpec(memory_space=pl.ANY)] * len(dep)

    def body(*refs):
        kernel(*refs[: len(ins)], *refs[len(arrays) :])

    return pl.pallas_call(
        body,
        grid=grid,
        out_shape=shapes,
        in_specs=in_specs,
        out_specs=out_specs,
        compiler_params=params(),
        cost_estimate=cost(1000, nbytes),
    )(*arrays)


def vmem(arrays):
    return [(array, None, pltpu.VMEM) for array in arrays]


def over(n, step, body):
    step = min(n, step)

    def one(i, carry):
        body(pl.multiple_of(i * step, step), step)
        return carry

    lax.fori_loop(0, n // step, one, 0)


def cut(a, place, start, n, tile, dep):
    k, half = a.shape[1], a.shape[0] // 2

    def kernel(at, a_ref, *refs):
        refs[-1][...] = a_ref[...]

    return pl.pallas_call(
        kernel,
        grid_spec=pltpu.PrefetchScalarGridSpec(
            num_scalar_prefetch=1,
            grid=(n // tile,),
            in_specs=[pl.BlockSpec((tile, k), lambda i, at: ((1 - at[1]) * (half // tile) + start // tile + i, 0))]
            + [pl.BlockSpec(memory_space=pl.ANY)] * len(dep),
            out_specs=pl.BlockSpec((tile, k), lambda i, at: (i, 0)),
        ),
        out_shape=jax.ShapeDtypeStruct((n, k), BF16),
        compiler_params=params(),
        cost_estimate=cost(1000, 1000),
    )(place, a, *dep)


def order(place, pieces, dep):
    k = pieces[0].shape[1]

    def kernel(at, *refs):
        for d in range(4):
            to = (d + at[0]) % 4
            refs[4][pl.ds(pl.multiple_of(to * CHIP, CHIP), CHIP), :] = refs[d][...]

    ins = [(place, None, pltpu.SMEM)] + vmem(pieces)
    return run(kernel, (), [(((4 * CHIP, k), BF16), None, pltpu.VMEM)], ins, dep)[0]


def product(slabs, a, other, place, start, tile, dep):
    n, k = other.shape
    half = a.shape[0] // 2
    halves = len(slabs) // 2
    rows = slabs[0].shape[0]

    def kernel(at, *refs):
        s, (a_ref, o_ref), outs = refs[: 2 * halves], refs[2 * halves : 2 * halves + 2], refs[-halves:]
        for kind in range(halves):
            if halves == 1:
                mine, theirs = s[0][...], s[1][...]
            else:
                first = at[2] == kind
                mine, theirs = jnp.where(first, s[0][...], s[2][...]), jnp.where(first, s[1][...], s[3][...])
            total = dot(mine, a_ref[...]) + dot(theirs, o_ref[...])
            outs[kind][...] = total.astype(outs[kind].dtype)

    block = pl.BlockSpec((rows, tile), lambda i, at: (0, i))
    return pl.pallas_call(
        kernel,
        grid_spec=pltpu.PrefetchScalarGridSpec(
            num_scalar_prefetch=1,
            grid=(n // tile,),
            in_specs=[pl.BlockSpec((rows, k), lambda i, at: (0, 0))] * (2 * halves)
            + [
                pl.BlockSpec((tile, k), lambda i, at: (at[1] * (half // tile) + start // tile + i, 0)),
                pl.BlockSpec((tile, k), lambda i, at: (i, 0)),
            ]
            + [pl.BlockSpec(memory_space=pl.ANY)] * len(dep),
            out_specs=[block] * halves,
        ),
        out_shape=[jax.ShapeDtypeStruct((rows, n), dtype) for dtype in (F32, BF16)[:halves]],
        compiler_params=params(),
        cost_estimate=cost(1000, LONG),
    )(place, *slabs, a, other, *dep)


def added(refs, block, columns):
    total = None
    for ref in refs:
        term = wide(ref[block * CHIP : (block + 1) * CHIP, columns])
        total = term if total is None else total + term
    return total


class Unit:
    def __init__(self, terms, n):
        self.terms, self.n, self.half = terms, n, n // 2


def send(first, second, dep):
    n_first = first.half if first else 0
    n_second = second.half // 2 if second else 0
    ins = first.terms if first else []
    ins2 = second.terms + [second.up1, second.down1] if second else []

    def kernel(*refs):
        terms, terms2 = refs[: len(ins)], refs[len(ins) : len(ins) + len(ins2) - 2]
        up, down = refs[-2:]

        def one(c, step):
            left, right = pl.ds(c, step), pl.ds(n_first + c, step)
            up[:CHIP, left] = added(terms, 2, left).astype(BF16)
            up[CHIP:, left] = added(terms, 1, right).astype(BF16)
            down[:CHIP, left] = added(terms, 2, right).astype(BF16)
            down[CHIP:, left] = added(terms, 3, left).astype(BF16)

        def two(c, step):
            up1, down1 = refs[len(ins) + len(ins2) - 2 : len(ins) + len(ins2)]
            to = pl.ds(n_first + c, step)
            for i in range(2):
                rows = slice(i * CHIP, (i + 1) * CHIP)
                here = pl.ds(i * n_second + c, step)
                there = pl.ds((i + 2) * n_second + c, step)
                up[rows, to] = (added(terms2, 1, here) + wide(up1[:CHIP, here])).astype(BF16)
                down[rows, to] = (added(terms2, 3, there) + wide(down1[:CHIP, here])).astype(BF16)

        if first:
            over(n_first, 128, one)
        if second:
            over(n_second, 128, two)

    shape = (2 * CHIP, n_first + n_second), BF16
    up, down = run(kernel, (), [(shape, None, pltpu.VMEM)] * 2, vmem(ins + ins2), dep, LONG)
    up, down, dep = lax.ppermute(up, "gc", X_UP), lax.ppermute(down, "gc", X_DOWN), [down]
    if first:
        first.up1, first.down1 = up, down
    if second:
        second.up2, second.down2, second.at = up, down, n_first
    return dep


def sum_over_x(unit, outs, extra, store, dep):
    n_terms, half, at = len(unit.terms), unit.half, unit.at

    def kernel(*refs):
        terms = refs[:n_terms]
        up1, down1, up2, down2 = refs[n_terms : n_terms + 4]
        rest = refs[n_terms + 4 :]

        def one(c, step):
            for i in range(2):
                low, rows = i * (half // 2), slice(i * CHIP, (i + 1) * CHIP)
                here, moved = pl.ds(low + c, step), pl.ds(at + c, step)
                left = added(terms, 0, here) + wide(up2[rows, moved]) + wide(down1[CHIP:, here])
                store(low + c, step, left, rest)
                right = added(terms, 0, pl.ds(half + low + c, step)) + wide(down2[rows, moved]) + wide(up1[CHIP:, here])
                store(half + low + c, step, right, rest)

        over(half // 2, 128, one)

    ins = vmem(unit.terms + [unit.up1, unit.down1, unit.up2, unit.down2]) + extra
    return run(kernel, (), outs, ins, dep, LONG)


def keep(unit, dep):
    def store(c, step, total, refs):
        refs[0][:, pl.ds(c, step)] = total

    return sum_over_x(unit, [(((CHIP, unit.n), F32), None, pltpu.VMEM)], [], store, dep)[0]


def split_over_z(unit, held, place, dep):
    def store(c, step, total, refs):
        h, at, stays, goes = refs
        to = pl.ds(c, step)
        yes = at[2] == 0
        stays[:, to] = jnp.where(yes, h[:, to], total)
        goes[:, to] = jnp.where(yes, total, h[:, to]).astype(BF16)

    shape = CHIP, unit.n
    outs = [((shape, F32), None, pltpu.VMEM), ((shape, BF16), None, pltpu.VMEM)]
    return sum_over_x(unit, outs, vmem([held]) + [(place, None, pltpu.SMEM)], store, dep)


def split_rows(place, at, total):
    first = place[1] == 0
    top, low = total[:HALF], total[HALF:]
    return jnp.where(first, top, low), jnp.where(first, low, top)


def swap(stays, came, place, dep):
    n = stays.shape[1]

    def kernel(s, c, at, mine, theirs):
        def one(c0, step):
            to = pl.ds(c0, step)
            mine[:, to], theirs[:, to] = split_rows(at, None, s[:, to] + wide(c[:, to]))

        over(n, 128, one)

    shape = (HALF, n), F32
    return run(kernel, (), [(shape, None, pltpu.VMEM)] * 2, vmem([stays, came]) + [(place, None, pltpu.SMEM)], dep)


def keep_rows(unit, place, dep):
    def store(c, step, total, refs):
        at, mine, theirs = refs
        mine[:, pl.ds(c, step)], theirs[:, pl.ds(c, step)] = split_rows(at, None, total)

    outs = [(((HALF, unit.n), F32), None, pltpu.VMEM)] * 2
    return sum_over_x(unit, outs, [(place, None, pltpu.SMEM)], store, dep)


def wide(v):
    return v.astype(F32)


def shards(a, scaling):
    n_half = a.shape[0] // 2
    gr, at = lax.axis_index("gr"), lax.axis_index("gc")
    core, x, z_lo = at % 2, (at // 2) % 4, at // 8
    y, z_hi = gr % 4, gr // 4
    place = jnp.stack([(y - x + 4) % 4, core, z_lo ^ z_hi]).astype(jnp.int32)
    tile = n_half // 4
    start = [0]
    for size in UNITS:
        start.append(start[-1] + size * n_half // 1024)

    mine = (a[:SLAB_DEV].astype(F32) * scaling[None, :]).astype(BF16)
    y_up = lax.ppermute(mine, "gr", Y_UP)
    y_down = lax.ppermute(mine, "gr", Y_DOWN)
    y_far = lax.ppermute(mine, "gr", Y_FAR)
    z_far = lax.ppermute(mine, "gr", Z_FAR)
    near = [mine, y_down, y_far, y_up]
    far = [z_far, lax.ppermute(z_far, "gr", Y_DOWN), lax.ppermute(y_far, "gr", Z_FAR), lax.ppermute(z_far, "gr", Y_UP)]

    a = pltpu.with_memory_space_constraint(a, pltpu.HBM)
    dep = [y_up]
    others, parts = {}, {}

    slabs, units, held, z_parts, done = {}, {}, {}, {}, {}
    for what, *names in PLAN:
        name = names[0]
        if what == "cut":
            part = cut(a, place, start[name], start[name + 1] - start[name], tile, dep)
            parts[name] = part
            dep = [part]
        elif what == "order":
            dep = dep + [z_far]
            own = order(place, far if name else near, dep)
            slabs[name] = [own, lax.ppermute(own, "gc", CORE)]
            if name == 0:
                for i in range(len(UNITS)):
                    start_after = (y_down, y_far, z_far) if i == 0 else (slabs[0][1], others[0])
                    part = lax.optimization_barrier((parts[i], *start_after))[0]
                    others[i] = lax.ppermute(part, "gc", CORE)
            dep = [own]
        elif what == "product":
            e, i = name
            if name == (0, 1):
                dep = dep + far
            operands = slabs[0] + slabs[1] if e == 2 else slabs[e]
            own, *sent = product(operands, a, others[i], place, start[i], tile, dep)
            units[name] = Unit([own] + [lax.ppermute(v, "gc", Z_NEAR) for v in sent], others[i].shape[0])
            dep = [own]
        elif what == "send":
            dep = send(*(units[name] if name else None for name in names), dep)
        elif what == "sum" and name[0] == 0:
            held[name[1]] = keep(units[name], dep)
            dep = [held[name[1]]]
        elif what == "sum" and name[0] == 1:
            stays, goes = split_over_z(units[name], held[name[1]], place, dep)
            z_parts[name[1]] = stays, lax.ppermute(goes, "gc", Z_NEAR)
            dep = [goes]
        else:
            if what == "swap":
                own, given = swap(*z_parts[name[1]], place, dep)
            else:
                own, given = keep_rows(units[name], place, dep)
            done[name[1]] = own, lax.ppermute(given, "gc", CORE)
            dep = [given]
    own, came = (jnp.concatenate([done[i][j] for i in range(len(UNITS))], axis=1) for j in range(2))
    first = core == 0
    return jnp.concatenate([jnp.where(first, own, came), jnp.where(first, came, own)], axis=1)


def solution(mesh):
    placed = (P("gr", "gc"), P("gc"))
    return jax.shard_map(shards, mesh=mesh, in_specs=placed, out_specs=P("gc", "gr"), check_vma=False)
```

time: 286 us -> 142 us (0.50)
  waiting for transfers between devices: 242 us -> 38.2 us
  Pallas kernels: 0 us -> 54.4 us
  starting transfers between devices: 0.04 us -> 42.1 us
  matrix products: 28.7 us -> 0 us
  between operations: 13.4 us -> 0.35 us
    reduce_scatter x1 -> x0, waiting for transfers between devices: 181 us -> none  [shards(): return lax.psum_scatter(partial_sums, 'gc', scatter_dimension=0, tiled=True)]
    all_gather x1 -> x0, waiting for transfers between devices: 60.7 us -> none  [shards(): lax.all_gather(scaled, 'gr', axis=0, tiled=True)]
    pallas_call x0 -> x23, Pallas kernels: none -> 54.4 us  [the longest x5 34.7 us: product(): pl.pallas_call(kernel, grid_spec=pltpu.PrefetchScalarGridSpec(num_scalar_...]
    ppermute x0 -> x30, starting transfers between devices: none -> 42.1 us  [the longest x6 17.2 us: send(): lax.ppermute(down, 'gc', X_DOWN)]
    ppermute x0 -> x30, waiting for transfers between devices: none -> 38.2 us  [the longest x6 22.5 us: send(): lax.ppermute(up, 'gc', X_UP)]
    dot_general x1 -> x0, matrix products: 28.7 us -> none  [shards(): lax.dot_general(lax.all_gather(scaled, 'gr', axis=0, tiled=True), a_matri...]
  transfers between devices with their start and end apart: 2 -> 30, of which waited for: 2 -> 11; matrix products, arithmetic and copies ran while one was open for 0% -> 0% of each run, Pallas kernels for 0% -> 38%
where the time goes in v2:
time: 142 us; the launch traced here: 140 us
  Pallas kernels  54.4 us (38%)
  starting transfers between devices  42.1 us (30%)
  waiting for transfers between devices  38.2 us (27%)
  other arithmetic  2.75 us (2%)
  local copies, waits for them, and re-layouts  2.38 us (2%)
    pallas_call x5, Pallas kernels, product(): pl.pallas_call(kernel, grid_spec=pltpu.PrefetchScalarGridSpec(num_scalar_...  34.7 us
    ppermute x6, waiting for transfers between devices, send(): lax.ppermute(up, 'gc', X_UP)  22.5 us
    ppermute x6, starting transfers between devices, send(): lax.ppermute(down, 'gc', X_DOWN)  17.2 us
    pallas_call x15, Pallas kernels, run(): pl.pallas_call(body, grid=grid, out_shape=shapes, in_specs=in_specs, out_...  11.9 us
    pallas_call x3, Pallas kernels, cut(): pl.pallas_call(kernel, grid_spec=pltpu.PrefetchScalarGridSpec(num_scalar_...  7.88 us
    ppermute x1, starting transfers between devices, shards(): lax.ppermute(y_far, 'gr', Z_FAR)  3.89 us
    ppermute x1, starting transfers between devices, shards(): z_far = lax.ppermute(mine, 'gr', Z_FAR)  3.88 us
    ppermute x6, starting transfers between devices, send(): lax.ppermute(up, 'gc', X_UP)  3.52 us
  transfers between devices with their start and end apart: 30, of which 11 were waited for; matrix products, arithmetic and copies ran while one was open for 0% of the time, Pallas kernels for 38%

profile of v2, /device:TPU:0, one launch (start us, length us, event | category | flops | bytes accessed | tf_op | source)
XLA Modules:
  0.0 140.3 jit_solution(14290820551844126418)
XLA Ops:
  0.0 1.0 multiply_convert_fusion.refs_1_
  1.0 1.7 %collective-permute-start.6 = (bf16[128,1152]{1,0:T(8,128)(2,1)S(1)}, bf16[128,1152]{1,0:T(8,128)(2,1)S(1)}, u32[]{:S(2)}, u32[]{:S(2)}) collective-permute-start(bf16[128,1152]{1,0:T(8,128)(2,1)S(1)} %multiply_convert_fusion.refs_1_), channel_id=1, source_target_pairs={{0,16},{16,32},{32,48},{48,0},{64,80},{80,96},{96,112},{112,64},{1... | collective-permute-start | bytes 884744 | tf_op jit(solution)/shard_map/ppermute | solution.py:321
  2.8 1.6 %collective-permute-start.5 = (bf16[128,1152]{1,0:T(8,128)(2,1)S(1)}, bf16[128,1152]{1,0:T(8,128)(2,1)S(1)}, u32[]{:S(2)}, u32[]{:S(2)}) collective-permute-start(bf16[128,1152]{1,0:T(8,128)(2,1)S(1)} %multiply_convert_fusion.refs_1_), channel_id=1, source_target_pairs={{16,0},{32,16},{48,32},{0,48},{80,64},{96,80},{112,96},{64,112},{1... | collective-permute-start | bytes 884744 | tf_op jit(solution)/shard_map/ppermute | solution.py:322
  4.3 2.1 %collective-permute-start.2 = (bf16[128,1152]{1,0:T(8,128)(2,1)S(1)}, bf16[128,1152]{1,0:T(8,128)(2,1)S(1)}, u32[]{:S(2)}, u32[]{:S(2)}) collective-permute-start(bf16[128,1152]{1,0:T(8,128)(2,1)S(1)} %multiply_convert_fusion.refs_1_), channel_id=1, source_target_pairs={{0,32},{16,48},{32,0},{48,16},{64,96},{80,112},{96,64},{112,80},{1... | collective-permute-start | bytes 884744 | tf_op jit(solution)/shard_map/ppermute | solution.py:323
  6.4 3.9 %collective-permute-start = (bf16[128,1152]{1,0:T(8,128)(2,1)S(1)}, bf16[128,1152]{1,0:T(8,128)(2,1)S(1)}, u32[]{:S(2)}, u32[]{:S(2)}) collective-permute-start(bf16[128,1152]{1,0:T(8,128)(2,1)S(1)} %multiply_convert_fusion.refs_1_), channel_id=1, source_target_pairs={{0,64},{16,80},{32,96},{48,112},{64,0},{80,16},{96,32},{112,48},{1... | collective-permute-start | bytes 884744 | tf_op jit(solution)/shard_map/ppermute | solution.py:324
  10.4 0.8 collective-permute-done.6.refs_0_.refs_4_
  11.2 2.4 %shard_map.28.refs_0_ = bf16[1024,1152]{1,0:T(8,128)(2,1)S(1)} custom-call(s32[3]{0:T(128)S(1)} %pad_add_fusion.at.refs_0_.refs_6_.refs_2_, bf16[8192,1152]{1,0:T(8,128)(2,1)} %refs_2_.7, bf16[128,1152]{1,0:T(8,128)(2,1)S(1)} %collective-permute-done.6.refs_0_.refs_4_), custom_call_target="tpu_custom_call" | custom-call | flops 1000 | bytes 1000 | tf_op jit(solution)/shard_map/pallas_call | solution.py:114
  13.6 3.3 %collective-permute-done.5.refs_2_ = bf16[128,1152]{1,0:T(8,128)(2,1)S(1)} collective-permute-done((bf16[128,1152]{1,0:T(8,128)(2,1)S(1)}, bf16[128,1152]{1,0:T(8,128)(2,1)S(1)}, u32[]{:S(2)}, u32[]{:S(2)}) %collective-permute-start.5) | collective-permute-done | bytes 294944 | tf_op jit(solution)/shard_map/ppermute | solution.py:322
  16.9 1.8 %collective-permute-done.2.refs_3_ = bf16[128,1152]{1,0:T(8,128)(2,1)S(1)} collective-permute-done((bf16[128,1152]{1,0:T(8,128)(2,1)S(1)}, bf16[128,1152]{1,0:T(8,128)(2,1)S(1)}, u32[]{:S(2)}, u32[]{:S(2)}) %collective-permute-start.2) | collective-permute-done | bytes 294944 | tf_op jit(solution)/shard_map/ppermute | solution.py:323
  18.7 3.1 %shard_map.29.refs_0_ = bf16[2048,1152]{1,0:T(8,128)(2,1)S(1)} custom-call(s32[3]{0:T(128)S(1)} %pad_add_fusion.at.refs_0_.refs_6_.refs_2_, bf16[8192,1152]{1,0:T(8,128)(2,1)} %refs_2_.7, bf16[1024,1152]{1,0:T(8,128)(2,1)S(1)} %shard_map.28.refs_0_), custom_call_target="tpu_custom_call" | custom-call | flops 1000 | bytes 1000 | tf_op jit(solution)/shard_map/pallas_call | solution.py:114
  21.8 2.4 %shard_map.30.refs_5_ = bf16[1024,1152]{1,0:T(8,128)(2,1)S(1)} custom-call(s32[3]{0:T(128)S(1)} %pad_add_fusion.at.refs_0_.refs_6_.refs_2_, bf16[8192,1152]{1,0:T(8,128)(2,1)} %refs_2_.7, bf16[2048,1152]{1,0:T(8,128)(2,1)S(1)} %shard_map.29.refs_0_), custom_call_target="tpu_custom_call" | custom-call | flops 1000 | bytes 1000 | tf_op jit(solution)/shard_map/pallas_call | solution.py:114
  24.2 0.6 shard_map.31.refs_0_.refs_4_
  25.5 2.5 %collective-permute-done.7.refs_1_ = bf16[512,1152]{1,0:T(8,128)(2,1)S(1)} collective-permute-done((bf16[512,1152]{1,0:T(8,128)(2,1)S(1)}, bf16[512,1152]{1,0:T(8,128)(2,1)S(1)}, u32[]{:S(2)}, u32[]{:S(2)}) %collective-permute-start.7) | collective-permute-done | bytes 1179680 | tf_op jit(solution)/shard_map/ppermute | solution.py:342
  28.4 3.9 %collective-permute-start.3 = (bf16[128,1152]{1,0:T(8,128)(2,1)S(1)}, bf16[128,1152]{1,0:T(8,128)(2,1)S(1)}, u32[]{:S(2)}, u32[]{:S(2)}) collective-permute-start(bf16[128,1152]{1,0:T(8,128)(2,1)S(1)} %collective-permute-done.2.refs_3_), channel_id=1, source_target_pairs={{0,64},{16,80},{32,96},{48,112},{64,0},{80,16},{96,32},{112,48},{1... | collective-permute-start | bytes 884744 | tf_op jit(solution)/shard_map/ppermute | solution.py:326
  32.3 1.1 collective-permute-start.4
  33.5 2.1 %collective-permute-start.1 = (bf16[128,1152]{1,0:T(8,128)(2,1)S(1)}, bf16[128,1152]{1,0:T(8,128)(2,1)S(1)}, u32[]{:S(2)}, u32[]{:S(2)}) collective-permute-start(bf16[128,1152]{1,0:T(8,128)(2,1)S(1)} %collective-permute-done.refs_6_.refs_5_.refs_1_), channel_id=1, source_target_pairs={{16,0},{32,16},{48,32},{0,48},{80,64},{96,80},{112,96},{64,112},{1... | collective-permute-start | bytes 884744 | tf_op jit(solution)/shard_map/ppermute | solution.py:326
  35.6 5.1 %shard_map.32.refs_0_.refs_1_ = f32[512,1024]{1,0:T(8,128)S(1)} custom-call(s32[3]{0:T(128)S(1)} %pad_add_fusion.at.refs_0_.refs_6_.refs_2_, bf16[512,1152]{1,0:T(8,128)(2,1)S(1)} %shard_map.31.refs_0_.refs_4_, bf16[512,1152]{1,0:T(8,128)(2,1)S(1)} %collective-permute-done.7.refs_1_, bf16[8192,1152]{1,0:T(8,128)(2,1)} %refs_2_.7, ...), custom_call_target="tpu_custom_call" | custom-call | flops 1000 | bytes 100000000 | tf_op jit(solution)/shard_map/pallas_call | solution.py:159
  40.9 1.6 %collective-permute-start.10 = (bf16[256,512]{1,0:T(8,128)(2,1)S(1)}, bf16[256,512]{1,0:T(8,128)(2,1)S(1)}, u32[]{:S(2)}, u32[]{:S(2)}) collective-permute-start(bf16[256,512]{1,0:T(8,128)(2,1)S(1)} %get-tuple-element.35), channel_id=1, source_target_pairs={{0,2},{1,3},{2,4},{3,5},{4,6},{5,7},{6,0},{7,1},{8,10},{9,11},{10,... | collective-permute-start | bytes 786440 | tf_op jit(solution)/shard_map/ppermute | solution.py:225
  42.5 2.8 %collective-permute-start.11 = (bf16[256,512]{1,0:T(8,128)(2,1)S(1)}, bf16[256,512]{1,0:T(8,128)(2,1)S(1)}, u32[]{:S(2)}, u32[]{:S(2)}) collective-permute-start(bf16[256,512]{1,0:T(8,128)(2,1)S(1)} %get-tuple-element.34.refs_4_), channel_id=1, source_target_pairs={{0,6},{1,7},{2,0},{3,1},{4,2},{5,3},{6,4},{7,5},{8,14},{9,15},{10,... | collective-permute-start | bytes 786440 | tf_op jit(solution)/shard_map/ppermute | solution.py:225
  45.3 8.3 %shard_map.34.refs_0_.refs_4_.refs_1_ = f32[512,2048]{1,0:T(8,128)S(1)} custom-call(s32[3]{0:T(128)S(1)} %pad_add_fusion.at.refs_0_.refs_6_.refs_2_, bf16[512,1152]{1,0:T(8,128)(2,1)S(1)} %shard_map.31.refs_0_.refs_4_, bf16[512,1152]{1,0:T(8,128)(2,1)S(1)} %collective-permute-done.7.refs_1_, bf16[8192,1152]{1,0:T(8,128)(2,1)} %refs_2_.7, ...), custom_call_target="tpu_custom_call" | custom-call | flops 1000 | bytes 100000000 | tf_op jit(solution)/shard_map/pallas_call | solution.py:159
  54.9 3.2 %collective-permute-start.14 = (bf16[256,1280]{1,0:T(8,128)(2,1)S(1)}, bf16[256,1280]{1,0:T(8,128)(2,1)S(1)}, u32[]{:S(2)}, u32[]{:S(2)}) collective-permute-start(bf16[256,1280]{1,0:T(8,128)(2,1)S(1)} %get-tuple-element.36.refs_5_), channel_id=1, source_target_pairs={{0,6},{1,7},{2,0},{3,1},{4,2},{5,3},{6,4},{7,5},{8,14},{9,15},{10,... | collective-permute-start | bytes 1966088 | tf_op jit(solution)/shard_map/ppermute | solution.py:225
  58.1 8.3 %shard_map.37.refs_6_.refs_0_.refs_1_ = f32[512,2048]{1,0:T(8,128)S(1)} custom-call(s32[3]{0:T(128)S(1)} %pad_add_fusion.at.refs_0_.refs_6_.refs_2_, bf16[512,1152]{1,0:T(8,128)(2,1)S(1)} %shard_map.36.refs_0_.refs_4_.refs_2_, bf16[512,1152]{1,0:T(8,128)(2,1)S(1)} %collective-permute-done.12.refs_1_.refs_3_, bf16[8192,1152]{1,0:T(8,128)(2,1)} %refs_2_.7, ...), custom_call_target="tpu_custom_call" | custom-call | flops 1000 | bytes 100000000 | tf_op jit(solution)/shard_map/pallas_call | solution.py:159
  66.5 7.8 %shard_map.38 = (f32[512,1024]{1,0:T(8,128)S(1)}, bf16[512,1024]{1,0:T(8,128)(2,1)S(1)}) custom-call(s32[3]{0:T(128)S(1)} %pad_add_fusion.at.refs_0_.refs_6_.refs_2_, bf16[512,1152]{1,0:T(8,128)(2,1)S(1)} %shard_map.31.refs_0_.refs_4_, bf16[512,1152]{1,0:T(8,128)(2,1)S(1)} %collective-permute-done.7.refs_1_, ...), custom_call_target="tpu_custom_call" | custom-call | flops 1000 | bytes 100000000 | tf_op jit(solution)/shard_map/pallas_call | solution.py:159
  74.9 3.2 %collective-permute-start.17 = (bf16[256,1536]{1,0:T(8,128)(2,1)S(1)}, bf16[256,1536]{1,0:T(8,128)(2,1)S(1)}, u32[]{:S(2)}, u32[]{:S(2)}) collective-permute-start(bf16[256,1536]{1,0:T(8,128)(2,1)S(1)} %get-tuple-element.40.refs_4_), channel_id=1, source_target_pairs={{0,6},{1,7},{2,0},{3,1},{4,2},{5,3},{6,4},{7,5},{8,14},{9,15},{10,... | collective-permute-start | bytes 2359304 | tf_op jit(solution)/shard_map/ppermute | solution.py:225
  78.1 1.0 collective-permute-start.20
  79.2 5.1 %shard_map.40.refs_5_.refs_0_.refs_2_ = f32[512,1024]{1,0:T(8,128)S(1)} custom-call(s32[3]{0:T(128)S(1)} %pad_add_fusion.at.refs_0_.refs_6_.refs_2_, bf16[512,1152]{1,0:T(8,128)(2,1)S(1)} %shard_map.36.refs_0_.refs_4_.refs_2_, bf16[512,1152]{1,0:T(8,128)(2,1)S(1)} %collective-permute-done.12.refs_1_.refs_3_, bf16[8192,1152]{1,0:T(8,128)(2,1)} %refs_2_.7, ...), custom_call_target="tpu_custom_call" | custom-call | flops 1000 | bytes 100000000 | tf_op jit(solution)/shard_map/pallas_call | solution.py:159
  84.5 11.0 %collective-permute-done.16.refs_2_.refs_3_.refs_1_ = bf16[256,1536]{1,0:T(8,128)(2,1)S(1)} collective-permute-done((bf16[256,1536]{1,0:T(8,128)(2,1)S(1)}, bf16[256,1536]{1,0:T(8,128)(2,1)S(1)}, u32[]{:S(2)}, u32[]{:S(2)}) %collective-permute-start.16) | collective-permute-done | bytes 786464 | tf_op jit(solution)/shard_map/ppermute | solution.py:225
  95.9 3.2 %collective-permute-start.19 = (bf16[256,1024]{1,0:T(8,128)(2,1)S(1)}, bf16[256,1024]{1,0:T(8,128)(2,1)S(1)}, u32[]{:S(2)}, u32[]{:S(2)}) collective-permute-start(bf16[256,1024]{1,0:T(8,128)(2,1)S(1)} %get-tuple-element.43.refs_5_), channel_id=1, source_target_pairs={{0,6},{1,7},{2,0},{3,1},{4,2},{5,3},{6,4},{7,5},{8,14},{9,15},{10,... | collective-permute-start | bytes 1572872 | tf_op jit(solution)/shard_map/ppermute | solution.py:225
  99.5 3.0 %collective-permute-done.20.refs_1_ = bf16[512,1024]{1,0:T(8,128)(2,1)S(1)} collective-permute-done((bf16[512,1024]{1,0:T(8,128)(2,1)S(1)}, bf16[512,1024]{1,0:T(8,128)(2,1)S(1)}, u32[]{:S(2)}, u32[]{:S(2)}) %collective-permute-start.20) | collective-permute-done | bytes 1048608 | tf_op jit(solution)/shard_map/ppermute | solution.py:355
  102.5 7.4 %collective-permute-done.18.refs_3_.refs_1_ = bf16[256,1024]{1,0:T(8,128)(2,1)S(1)} collective-permute-done((bf16[256,1024]{1,0:T(8,128)(2,1)S(1)}, bf16[256,1024]{1,0:T(8,128)(2,1)S(1)}, u32[]{:S(2)}, u32[]{:S(2)}) %collective-permute-start.18) | collective-permute-done | bytes 524320 | tf_op jit(solution)/shard_map/ppermute | solution.py:225
  110.4 0.9 collective-permute-start.21
  111.3 2.4 %collective-permute-start.22 = (bf16[256,768]{1,0:T(8,128)(2,1)S(1)}, bf16[256,768]{1,0:T(8,128)(2,1)S(1)}, u32[]{:S(2)}, u32[]{:S(2)}) collective-permute-start(bf16[256,768]{1,0:T(8,128)(2,1)S(1)} %get-tuple-element.46.refs_7_), channel_id=1, source_target_pairs={{0,6},{1,7},{2,0},{3,1},{4,2},{5,3},{6,4},{7,5},{8,14},{9,15},{10,... | collective-permute-start | bytes 1179656 | tf_op jit(solution)/shard_map/ppermute | solution.py:225
  113.7 2.0 %shard_map.45 = (f32[128,2048]{1,0:T(8,128)S(1)}, bf16[128,2048]{1,0:T(8,128)(2,1)}) custom-call(f32[512,2048]{1,0:T(8,128)S(1)} %shard_map.37.refs_6_.refs_0_.refs_1_, bf16[256,1536]{1,0:T(8,128)(2,1)S(1)} %collective-permute-done.16.refs_2_.refs_3_.refs_1_, bf16[256,1536]{1,0:T(8,128)(2,1)S(1)} %collective-permute-done.17.refs_3_.refs_4_.refs_2_, ...), custom_call_target="tpu_custom_call" | custom-call | flops 1000 | bytes 100000000 | tf_op jit(solution)/shard_map/pallas_call | solution.py:83
  115.7 1.0 collective-permute-start.26
  116.7 4.1 %collective-permute-done.21.refs_3_.refs_2_ = bf16[256,768]{1,0:T(8,128)(2,1)S(1)} collective-permute-done((bf16[256,768]{1,0:T(8,128)(2,1)S(1)}, bf16[256,768]{1,0:T(8,128)(2,1)S(1)}, u32[]{:S(2)}, u32[]{:S(2)}) %collective-permute-start.21) | collective-permute-done | bytes 393248 | tf_op jit(solution)/shard_map/ppermute | solution.py:225
  120.8 1.5 %shard_map.46 = (f32[128,1024]{1,0:T(8,128)S(1)}, bf16[128,1024]{1,0:T(8,128)(2,1)}) custom-call(f32[512,1024]{1,0:T(8,128)S(1)} %shard_map.40.refs_5_.refs_0_.refs_2_, bf16[256,1024]{1,0:T(8,128)(2,1)S(1)} %collective-permute-done.18.refs_3_.refs_1_, bf16[256,1024]{1,0:T(8,128)(2,1)S(1)} %collective-permute-done.19.refs_4_.refs_2_, ...), custom_call_target="tpu_custom_call" | custom-call | flops 1000 | bytes 100000000 | tf_op jit(solution)/shard_map/pallas_call | solution.py:83
  122.3 1.0 collective-permute-start.23
  123.4 0.9 shard_map.47
  124.2 0.9 collective-permute-start.24
  125.1 2.4 %collective-permute-start.25 = (bf16[256,256]{1,0:T(8,128)(2,1)}, bf16[256,256]{1,0:T(8,128)(2,1)}, u32[]{:S(2)}, u32[]{:S(2)}) collective-permute-start(bf16[256,256]{1,0:T(8,128)(2,1)} %get-tuple-element.51.refs_3_), channel_id=1, source_target_pairs={{0,6},{1,7},{2,0},{3,1},{4,2},{5,3},{6,4},{7,5},{8,14},{9,15},{10,... | collective-permute-start | bytes 393224 | tf_op jit(solution)/shard_map/ppermute | solution.py:225
  127.5 2.7 %collective-permute-done.26.refs_1_ = bf16[128,2048]{1,0:T(8,128)(2,1)} collective-permute-done((bf16[128,2048]{1,0:T(8,128)(2,1)}, bf16[128,2048]{1,0:T(8,128)(2,1)}, u32[]{:S(2)}, u32[]{:S(2)}) %collective-permute-start.26) | collective-permute-done | bytes 524320 | tf_op jit(solution)/shard_map/ppermute | solution.py:364
  130.2 1.2 copy-done.3
  131.4 1.5 %shard_map.48 = (f32[64,2048]{1,0:T(8,128)S(1)}, f32[64,2048]{1,0:T(8,128)S(1)}) custom-call(f32[128,2048]{1,0:T(8,128)S(1)} %copy-done.3, bf16[128,2048]{1,0:T(8,128)(2,1)} %collective-permute-done.26.refs_1_, s32[3]{0:T(128)S(1)} %pad_add_fusion.at.refs_0_.refs_6_.refs_2_, bf16[256,256]{1,0:T(8,128)(2,1)} %get-tuple-element.51.refs_3_), custom_call_target="tpu_custom_call" | custom-call | flops 1000 | bytes 1000 | tf_op jit(solution)/shard_map/pallas_call | solution.py:83
  133.0 1.0 copy-done.1
  134.0 1.2 shard_map.49
  135.8 1.1 shard_map.50
  137.1 1.4 %collective-permute-done.27 = f32[64,1024]{1,0:T(8,128)S(1)} collective-permute-done((f32[64,1024]{1,0:T(8,128)S(1)}, f32[64,1024]{1,0:T(8,128)S(1)}, u32[]{:S(2)}, u32[]{:S(2)}) %collective-permute-start.27) | collective-permute-done | bytes 262176 | tf_op jit(solution)/shard_map/ppermute | solution.py:371
  138.8 1.5 %pad_maximum_fusion = f32[64,8192]{1,0:T(8,128)} fusion(f32[64,4096]{1,0:T(8,128)S(1)} %get-tuple-element.60, f32[64,4096]{1,0:T(8,128)S(1)} %get-tuple-element.59), kind=kLoop, calls=%fused_computation | loop fusion | flops 524288 | bytes 4194304 | tf_op jit(solution)/shard_map/concatenate | solution.py:375
  (57 shorter events, 5.8 us)
Async XLA Ops:
  1.0 10.2 %collective-permute-start.6 = (bf16[128,1152]{1,0:T(8,128)(2,1)S(1)}, bf16[128,1152]{1,0:T(8,128)(2,1)S(1)}, u32[]{:S(2)}, u32[]{:S(2)}) collective-permute-start(bf16[128,1152]{1,0:T(8,128)(2,1)S(1)} %multiply_convert_fusion.refs_1_), channel_id=1, source_target_pairs={{0,16},{16,32},{32,48},{48,0},{64,80},{80,96},{96,112},{112,64},{1... | collective-permute-start | bytes 884744 | tf_op jit(solution)/shard_map/ppermute | solution.py:321
  2.8 14.1 %collective-permute-start.5 = (bf16[128,1152]{1,0:T(8,128)(2,1)S(1)}, bf16[128,1152]{1,0:T(8,128)(2,1)S(1)}, u32[]{:S(2)}, u32[]{:S(2)}) collective-permute-start(bf16[128,1152]{1,0:T(8,128)(2,1)S(1)} %multiply_convert_fusion.refs_1_), channel_id=1, source_target_pairs={{16,0},{32,16},{48,32},{0,48},{80,64},{96,80},{112,96},{64,112},{1... | collective-permute-start | bytes 884744 | tf_op jit(solution)/shard_map/ppermute | solution.py:322
  4.3 14.4 %collective-permute-start.2 = (bf16[128,1152]{1,0:T(8,128)(2,1)S(1)}, bf16[128,1152]{1,0:T(8,128)(2,1)S(1)}, u32[]{:S(2)}, u32[]{:S(2)}) collective-permute-start(bf16[128,1152]{1,0:T(8,128)(2,1)S(1)} %multiply_convert_fusion.refs_1_), channel_id=1, source_target_pairs={{0,32},{16,48},{32,0},{48,16},{64,96},{80,112},{96,64},{112,80},{1... | collective-permute-start | bytes 884744 | tf_op jit(solution)/shard_map/ppermute | solution.py:323
  6.4 12.3 %collective-permute-start = (bf16[128,1152]{1,0:T(8,128)(2,1)S(1)}, bf16[128,1152]{1,0:T(8,128)(2,1)S(1)}, u32[]{:S(2)}, u32[]{:S(2)}) collective-permute-start(bf16[128,1152]{1,0:T(8,128)(2,1)S(1)} %multiply_convert_fusion.refs_1_), channel_id=1, source_target_pairs={{0,64},{16,80},{32,96},{48,112},{64,0},{80,16},{96,32},{112,48},{1... | collective-permute-start | bytes 884744 | tf_op jit(solution)/shard_map/ppermute | solution.py:324
  18.7 9.2 %collective-permute-start.8 = (bf16[1024,1152]{1,0:T(8,128)(2,1)S(1)}, bf16[1024,1152]{1,0:T(8,128)(2,1)S(1)}, u32[]{:S(2)}, u32[]{:S(2)}) collective-permute-start(bf16[1024,1152]{1,0:T(8,128)(2,1)S(1)} %shard_map.28.refs_0_), channel_id=1, source_target_pairs={{0,1},{1,0},{2,3},{3,2},{4,5},{5,4},{6,7},{7,6},{8,9},{9,8},{10,11... | collective-permute-start | bytes 7077896 | tf_op jit(solution)/shard_map/ppermute | solution.py:347
  24.9 3.1 %collective-permute-start.7 = (bf16[512,1152]{1,0:T(8,128)(2,1)S(1)}, bf16[512,1152]{1,0:T(8,128)(2,1)S(1)}, u32[]{:S(2)}, u32[]{:S(2)}) collective-permute-start(bf16[512,1152]{1,0:T(8,128)(2,1)S(1)} %shard_map.31.refs_0_.refs_4_), channel_id=1, source_target_pairs={{0,1},{1,0},{2,3},{3,2},{4,5},{5,4},{6,7},{7,6},{8,9},{9,8},{10,11... | collective-permute-start | bytes 3538952 | tf_op jit(solution)/shard_map/ppermute | solution.py:342
  27.9 17.4 %collective-permute-start.9 = (bf16[2048,1152]{1,0:T(8,128)(2,1)S(1)}, bf16[2048,1152]{1,0:T(8,128)(2,1)S(1)}, u32[]{:S(2)}, u32[]{:S(2)}) collective-permute-start(bf16[2048,1152]{1,0:T(8,128)(2,1)S(1)} %shard_map.29.refs_0_), channel_id=1, source_target_pairs={{0,1},{1,0},{2,3},{3,2},{4,5},{5,4},{6,7},{7,6},{8,9},{9,8},{10,11... | collective-permute-start | bytes 14155784 | tf_op jit(solution)/shard_map/ppermute | solution.py:347
  28.3 38.2 %collective-permute-start.15 = (bf16[1024,1152]{1,0:T(8,128)(2,1)S(1)}, bf16[1024,1152]{1,0:T(8,128)(2,1)S(1)}, u32[]{:S(2)}, u32[]{:S(2)}) collective-permute-start(bf16[1024,1152]{1,0:T(8,128)(2,1)S(1)} %shard_map.30.refs_5_), channel_id=1, source_target_pairs={{0,1},{1,0},{2,3},{3,2},{4,5},{5,4},{6,7},{7,6},{8,9},{9,8},{10,11... | collective-permute-start | bytes 7077896 | tf_op jit(solution)/shard_map/ppermute | solution.py:347
  28.4 12.4 %collective-permute-start.3 = (bf16[128,1152]{1,0:T(8,128)(2,1)S(1)}, bf16[128,1152]{1,0:T(8,128)(2,1)S(1)}, u32[]{:S(2)}, u32[]{:S(2)}) collective-permute-start(bf16[128,1152]{1,0:T(8,128)(2,1)S(1)} %collective-permute-done.2.refs_3_), channel_id=1, source_target_pairs={{0,64},{16,80},{32,96},{48,112},{64,0},{80,16},{96,32},{112,48},{1... | collective-permute-start | bytes 884744 | tf_op jit(solution)/shard_map/ppermute | solution.py:326
  32.3 10.2 %collective-permute-start.4 = (bf16[128,1152]{1,0:T(8,128)(2,1)S(1)}, bf16[128,1152]{1,0:T(8,128)(2,1)S(1)}, u32[]{:S(2)}, u32[]{:S(2)}) collective-permute-start(bf16[128,1152]{1,0:T(8,128)(2,1)S(1)} %collective-permute-done.refs_6_.refs_5_.refs_1_), channel_id=1, source_target_pairs={{0,16},{16,32},{32,48},{48,0},{64,80},{80,96},{96,112},{112,64},{1... | collective-permute-start | bytes 884744 | tf_op jit(solution)/shard_map/ppermute | solution.py:326
  33.5 11.8 %collective-permute-start.1 = (bf16[128,1152]{1,0:T(8,128)(2,1)S(1)}, bf16[128,1152]{1,0:T(8,128)(2,1)S(1)}, u32[]{:S(2)}, u32[]{:S(2)}) collective-permute-start(bf16[128,1152]{1,0:T(8,128)(2,1)S(1)} %collective-permute-done.refs_6_.refs_5_.refs_1_), channel_id=1, source_target_pairs={{16,0},{32,16},{48,32},{0,48},{80,64},{96,80},{112,96},{64,112},{1... | collective-permute-start | bytes 884744 | tf_op jit(solution)/shard_map/ppermute | solution.py:326
  40.9 12.8 %collective-permute-start.10 = (bf16[256,512]{1,0:T(8,128)(2,1)S(1)}, bf16[256,512]{1,0:T(8,128)(2,1)S(1)}, u32[]{:S(2)}, u32[]{:S(2)}) collective-permute-start(bf16[256,512]{1,0:T(8,128)(2,1)S(1)} %get-tuple-element.35), channel_id=1, source_target_pairs={{0,2},{1,3},{2,4},{3,5},{4,6},{5,7},{6,0},{7,1},{8,10},{9,11},{10,... | collective-permute-start | bytes 786440 | tf_op jit(solution)/shard_map/ppermute | solution.py:225
  42.5 11.1 %collective-permute-start.11 = (bf16[256,512]{1,0:T(8,128)(2,1)S(1)}, bf16[256,512]{1,0:T(8,128)(2,1)S(1)}, u32[]{:S(2)}, u32[]{:S(2)}) collective-permute-start(bf16[256,512]{1,0:T(8,128)(2,1)S(1)} %get-tuple-element.34.refs_4_), channel_id=1, source_target_pairs={{0,6},{1,7},{2,0},{3,1},{4,2},{5,3},{6,4},{7,5},{8,14},{9,15},{10,... | collective-permute-start | bytes 786440 | tf_op jit(solution)/shard_map/ppermute | solution.py:225
  54.7 3.4 %collective-permute-start.12 = (bf16[512,1152]{1,0:T(8,128)(2,1)S(1)}, bf16[512,1152]{1,0:T(8,128)(2,1)S(1)}, u32[]{:S(2)}, u32[]{:S(2)}) collective-permute-start(bf16[512,1152]{1,0:T(8,128)(2,1)S(1)} %shard_map.36.refs_0_.refs_4_.refs_2_), channel_id=1, source_target_pairs={{0,1},{1,0},{2,3},{3,2},{4,5},{5,4},{6,7},{7,6},{8,9},{9,8},{10,11... | collective-permute-start | bytes 3538952 | tf_op jit(solution)/shard_map/ppermute | solution.py:342
  54.8 19.5 %collective-permute-start.13 = (bf16[256,1280]{1,0:T(8,128)(2,1)S(1)}, bf16[256,1280]{1,0:T(8,128)(2,1)S(1)}, u32[]{:S(2)}, u32[]{:S(2)}) collective-permute-start(bf16[256,1280]{1,0:T(8,128)(2,1)S(1)} %get-tuple-element.37), channel_id=1, source_target_pairs={{0,2},{1,3},{2,4},{3,5},{4,6},{5,7},{6,0},{7,1},{8,10},{9,11},{10,... | collective-permute-start | bytes 1966088 | tf_op jit(solution)/shard_map/ppermute | solution.py:225
  54.9 19.4 %collective-permute-start.14 = (bf16[256,1280]{1,0:T(8,128)(2,1)S(1)}, bf16[256,1280]{1,0:T(8,128)(2,1)S(1)}, u32[]{:S(2)}, u32[]{:S(2)}) collective-permute-start(bf16[256,1280]{1,0:T(8,128)(2,1)S(1)} %get-tuple-element.36.refs_5_), channel_id=1, source_target_pairs={{0,6},{1,7},{2,0},{3,1},{4,2},{5,3},{6,4},{7,5},{8,14},{9,15},{10,... | collective-permute-start | bytes 1966088 | tf_op jit(solution)/shard_map/ppermute | solution.py:225
  74.8 20.6 %collective-permute-start.16 = (bf16[256,1536]{1,0:T(8,128)(2,1)S(1)}, bf16[256,1536]{1,0:T(8,128)(2,1)S(1)}, u32[]{:S(2)}, u32[]{:S(2)}) collective-permute-start(bf16[256,1536]{1,0:T(8,128)(2,1)S(1)} %get-tuple-element.41), channel_id=1, source_target_pairs={{0,2},{1,3},{2,4},{3,5},{4,6},{5,7},{6,0},{7,1},{8,10},{9,11},{10,... | collective-permute-start | bytes 2359304 | tf_op jit(solution)/shard_map/ppermute | solution.py:225
  74.9 20.5 %collective-permute-start.17 = (bf16[256,1536]{1,0:T(8,128)(2,1)S(1)}, bf16[256,1536]{1,0:T(8,128)(2,1)S(1)}, u32[]{:S(2)}, u32[]{:S(2)}) collective-permute-start(bf16[256,1536]{1,0:T(8,128)(2,1)S(1)} %get-tuple-element.40.refs_4_), channel_id=1, source_target_pairs={{0,6},{1,7},{2,0},{3,1},{4,2},{5,3},{6,4},{7,5},{8,14},{9,15},{10,... | collective-permute-start | bytes 2359304 | tf_op jit(solution)/shard_map/ppermute | solution.py:225
  78.1 24.4 %collective-permute-start.20 = (bf16[512,1024]{1,0:T(8,128)(2,1)S(1)}, bf16[512,1024]{1,0:T(8,128)(2,1)S(1)}, u32[]{:S(2)}, u32[]{:S(2)}) collective-permute-start(bf16[512,1024]{1,0:T(8,128)(2,1)S(1)} %get-tuple-element.44), channel_id=1, source_target_pairs={{0,8},{1,9},{2,10},{3,11},{4,12},{5,13},{6,14},{7,15},{8,0},{9,1},... | collective-permute-start | bytes 3145736 | tf_op jit(solution)/shard_map/ppermute | solution.py:355
  95.8 14.1 %collective-permute-start.18 = (bf16[256,1024]{1,0:T(8,128)(2,1)S(1)}, bf16[256,1024]{1,0:T(8,128)(2,1)S(1)}, u32[]{:S(2)}, u32[]{:S(2)}) collective-permute-start(bf16[256,1024]{1,0:T(8,128)(2,1)S(1)} %get-tuple-element.42), channel_id=1, source_target_pairs={{0,2},{1,3},{2,4},{3,5},{4,6},{5,7},{6,0},{7,1},{8,10},{9,11},{10,... | collective-permute-start | bytes 1572872 | tf_op jit(solution)/shard_map/ppermute | solution.py:225
  95.9 14.0 %collective-permute-start.19 = (bf16[256,1024]{1,0:T(8,128)(2,1)S(1)}, bf16[256,1024]{1,0:T(8,128)(2,1)S(1)}, u32[]{:S(2)}, u32[]{:S(2)}) collective-permute-start(bf16[256,1024]{1,0:T(8,128)(2,1)S(1)} %get-tuple-element.43.refs_5_), channel_id=1, source_target_pairs={{0,6},{1,7},{2,0},{3,1},{4,2},{5,3},{6,4},{7,5},{8,14},{9,15},{10,... | collective-permute-start | bytes 1572872 | tf_op jit(solution)/shard_map/ppermute | solution.py:225
  110.4 10.4 %collective-permute-start.21 = (bf16[256,768]{1,0:T(8,128)(2,1)S(1)}, bf16[256,768]{1,0:T(8,128)(2,1)S(1)}, u32[]{:S(2)}, u32[]{:S(2)}) collective-permute-start(bf16[256,768]{1,0:T(8,128)(2,1)S(1)} %get-tuple-element.45), channel_id=1, source_target_pairs={{0,2},{1,3},{2,4},{3,5},{4,6},{5,7},{6,0},{7,1},{8,10},{9,11},{10,... | collective-permute-start | bytes 1179656 | tf_op jit(solution)/shard_map/ppermute | solution.py:225
  111.3 9.5 %collective-permute-start.22 = (bf16[256,768]{1,0:T(8,128)(2,1)S(1)}, bf16[256,768]{1,0:T(8,128)(2,1)S(1)}, u32[]{:S(2)}, u32[]{:S(2)}) collective-permute-start(bf16[256,768]{1,0:T(8,128)(2,1)S(1)} %get-tuple-element.46.refs_7_), channel_id=1, source_target_pairs={{0,6},{1,7},{2,0},{3,1},{4,2},{5,3},{6,4},{7,5},{8,14},{9,15},{10,... | collective-permute-start | bytes 1179656 | tf_op jit(solution)/shard_map/ppermute | solution.py:225
  115.7 6.6 %copy-start.2 = (f32[128,2048]{1,0:T(8,128)}, f32[128,2048]{1,0:T(8,128)S(1)}, u32[]{:S(2)}) copy-start(f32[128,2048]{1,0:T(8,128)S(1)} %get-tuple-element.52.refs_0_) | copy-start | bytes 3145732
  115.7 14.5 %collective-permute-start.26 = (bf16[128,2048]{1,0:T(8,128)(2,1)}, bf16[128,2048]{1,0:T(8,128)(2,1)}, u32[]{:S(2)}, u32[]{:S(2)}) collective-permute-start(bf16[128,2048]{1,0:T(8,128)(2,1)} %get-tuple-element.47.refs_7_), channel_id=1, source_target_pairs={{0,8},{1,9},{2,10},{3,11},{4,12},{5,13},{6,14},{7,15},{8,0},{9,1},... | collective-permute-start | bytes 1572872 | tf_op jit(solution)/shard_map/ppermute | solution.py:364
  120.8 2.6 %copy-start = (bf16[256,768]{1,0:T(8,128)(2,1)}, bf16[256,768]{1,0:T(8,128)(2,1)S(1)}, u32[]{:S(2)}) copy-start(bf16[256,768]{1,0:T(8,128)(2,1)S(1)} %collective-permute-done.22.refs_4_.refs_3_) | copy-start | bytes 1179652
  122.3 1.9 %copy-start.4 = (f32[128,1024]{1,0:T(8,128)}, f32[128,1024]{1,0:T(8,128)S(1)}, u32[]{:S(2)}) copy-start(f32[128,1024]{1,0:T(8,128)S(1)} %get-tuple-element.48.refs_0_) | copy-start | bytes 1572868
  122.3 13.4 %collective-permute-start.23 = (bf16[128,1024]{1,0:T(8,128)(2,1)}, bf16[128,1024]{1,0:T(8,128)(2,1)}, u32[]{:S(2)}, u32[]{:S(2)}) collective-permute-start(bf16[128,1024]{1,0:T(8,128)(2,1)} %get-tuple-element.49.refs_4_), channel_id=1, source_target_pairs={{0,8},{1,9},{2,10},{3,11},{4,12},{5,13},{6,14},{7,15},{8,0},{9,1},... | collective-permute-start | bytes 786440 | tf_op jit(solution)/shard_map/ppermute | solution.py:364
  124.2 8.7 %collective-permute-start.24 = (bf16[256,256]{1,0:T(8,128)(2,1)}, bf16[256,256]{1,0:T(8,128)(2,1)}, u32[]{:S(2)}, u32[]{:S(2)}) collective-permute-start(bf16[256,256]{1,0:T(8,128)(2,1)} %get-tuple-element.50), channel_id=1, source_target_pairs={{0,2},{1,3},{2,4},{3,5},{4,6},{5,7},{6,0},{7,1},{8,10},{9,11},{10,... | collective-permute-start | bytes 393224 | tf_op jit(solution)/shard_map/ppermute | solution.py:225
  125.1 7.9 %collective-permute-start.25 = (bf16[256,256]{1,0:T(8,128)(2,1)}, bf16[256,256]{1,0:T(8,128)(2,1)}, u32[]{:S(2)}, u32[]{:S(2)}) collective-permute-start(bf16[256,256]{1,0:T(8,128)(2,1)} %get-tuple-element.51.refs_3_), channel_id=1, source_target_pairs={{0,6},{1,7},{2,0},{3,1},{4,2},{5,3},{6,4},{7,5},{8,14},{9,15},{10,... | collective-permute-start | bytes 393224 | tf_op jit(solution)/shard_map/ppermute | solution.py:225
  130.2 1.2 copy-start.3
  131.4 4.3 %copy-start.5 = (f32[128,1024]{1,0:T(8,128)S(1)}, f32[128,1024]{1,0:T(8,128)}, u32[]{:S(2)}) copy-start(f32[128,1024]{1,0:T(8,128)} %copy-done.4) | copy-start | bytes 1572868
  132.9 5.6 %collective-permute-start.28 = (f32[64,2048]{1,0:T(8,128)S(1)}, f32[64,2048]{1,0:T(8,128)S(1)}, u32[]{:S(2)}, u32[]{:S(2)}) collective-permute-start(f32[64,2048]{1,0:T(8,128)S(1)} %get-tuple-element.53.refs_7_), channel_id=1, source_target_pairs={{0,1},{1,0},{2,3},{3,2},{4,5},{5,4},{6,7},{7,6},{8,9},{9,8},{10,11... | collective-permute-start | bytes 1572872 | tf_op jit(solution)/shard_map/ppermute | solution.py:371
  133.0 1.0 copy-start.1
  135.2 3.4 %collective-permute-start.29 = (f32[64,1024]{1,0:T(8,128)S(1)}, f32[64,1024]{1,0:T(8,128)S(1)}, u32[]{:S(2)}, u32[]{:S(2)}) collective-permute-start(f32[64,1024]{1,0:T(8,128)S(1)} %get-tuple-element.54.refs_3_), channel_id=1, source_target_pairs={{0,1},{1,0},{2,3},{3,2},{4,5},{5,4},{6,7},{7,6},{8,9},{9,8},{10,11... | collective-permute-start | bytes 786440 | tf_op jit(solution)/shard_map/ppermute | solution.py:371
  136.9 1.6 %collective-permute-start.27 = (f32[64,1024]{1,0:T(8,128)S(1)}, f32[64,1024]{1,0:T(8,128)S(1)}, u32[]{:S(2)}, u32[]{:S(2)}) collective-permute-start(f32[64,1024]{1,0:T(8,128)S(1)} %get-tuple-element.58), channel_id=1, source_target_pairs={{0,1},{1,0},{2,3},{3,2},{4,5},{5,4},{6,7},{7,6},{8,9},{9,8},{10,11... | collective-permute-start | bytes 786440 | tf_op jit(solution)/shard_map/ppermute | solution.py:371

commit v3 on v2

--- a/solution.py
+++ b/solution.py
@@ -40,14 +40,14 @@
     ("send", (0, 1), (0, 0)),
     ("order", 1),
     ("product", (1, 1)),
+    ("send", (1, 1), (0, 1)),
     ("product", (2, 2)),
-    ("send", (1, 1), (0, 1)),
     ("product", (1, 0)),
     ("sum", (0, 0)),
     ("send", (1, 0), (1, 1)),
     ("sum", (0, 1)),
+    ("sum", (1, 1)),
     ("send", (2, 2), (1, 0)),
-    ("sum", (1, 1)),
     ("sum", (1, 0)),
     ("send", None, (2, 2)),
     ("swap", (1, 1)),
@@ -340,21 +340,25 @@
             dep = dep + [z_far]
             own = order(place, far if name else near, dep)
             slabs[name] = [own, lax.ppermute(own, "gc", CORE)]
+            if name == 1:
+                part = lax.optimization_barrier((parts[2], slabs[1][1]))[0]
+                others[2] = lax.ppermute(part, "gc", CORE)
             if name == 0:
-                for i in range(len(UNITS)):
-                    start_after = (y_down, y_far, z_far) if i == 0 else (slabs[0][1], others[0])
+                for i in range(2):
+                    last = parts[len(UNITS) - 1]
+                    start_after = (y_down, y_far, z_far, last) if i == 0 else (slabs[0][1], others[i - 1])
                     part = lax.optimization_barrier((parts[i], *start_after))[0]
                     others[i] = lax.ppermute(part, "gc", CORE)
             dep = [own]
         elif what == "product":
             e, i = name
-            if name == (0, 1):
-                dep = dep + far
             operands = slabs[0] + slabs[1] if e == 2 else slabs[e]
             own, *sent = product(operands, a, others[i], place, start[i], tile, dep)
             units[name] = Unit([own] + [lax.ppermute(v, "gc", Z_NEAR) for v in sent], others[i].shape[0])
             dep = [own]
         elif what == "send":
+            if name == (0, 1):
+                dep = dep + far
             dep = send(*(units[name] if name else None for name in names), dep)
         elif what == "sum" and name[0] == 0:
             held[name[1]] = keep(units[name], dep)

time: 142 us -> 142 us (level)
  the two profiles are of different devices: /device:TPU:0 before, /device:TPU:23 now
where the time goes in v3:
time: 142 us
  Pallas kernels  54.4 us (38%)
  waiting for transfers between devices  44.6 us (31%)
  starting transfers between devices  36.7 us (26%)
  local copies, waits for them, and re-layouts  2.91 us (2%)
  other arithmetic  2.75 us (2%)
    pallas_call x5, Pallas kernels, product(): pl.pallas_call(kernel, grid_spec=pltpu.PrefetchScalarGridSpec(num_scalar_...  34.7 us
    ppermute x6, waiting for transfers between devices, send(): lax.ppermute(up, 'gc', X_UP)  23.5 us
    pallas_call x15, Pallas kernels, run(): pl.pallas_call(body, grid=grid, out_shape=shapes, in_specs=in_specs, out_...  11.9 us
    pallas_call x3, Pallas kernels, cut(): pl.pallas_call(kernel, grid_spec=pltpu.PrefetchScalarGridSpec(num_scalar_...  7.88 us
    ppermute x2, waiting for transfers between devices, shards(): slabs[name] = [own, lax.ppermute(own, 'gc', CORE)]  7.58 us
    ppermute x3, starting transfers between devices, shards(): done[name[1]] = (own, lax.ppermute(given, 'gc', CORE))  7.06 us
    ppermute x6, waiting for transfers between devices, send(): lax.ppermute(down, 'gc', X_DOWN)  6.88 us
    ppermute x6, starting transfers between devices, send(): lax.ppermute(down, 'gc', X_DOWN)  6.01 us
  transfers between devices with their start and end apart: 30, of which 13 were waited for; matrix products, arithmetic and copies ran while one was open for 0% of the time, Pallas kernels for 37%

profile of v3, /device:TPU:23, one launch (start us, length us, event | category | flops | bytes accessed | tf_op | source)
XLA Modules:
  0.0 141.7 jit_solution(12140400264664615270)
XLA Ops:
  0.0 1.0 multiply_convert_fusion.refs_1_
  1.0 1.1 collective-permute-start.6
  2.1 3.6 %collective-permute-start = (bf16[128,1152]{1,0:T(8,128)(2,1)S(1)}, bf16[128,1152]{1,0:T(8,128)(2,1)S(1)}, u32[]{:S(2)}, u32[]{:S(2)}) collective-permute-start(bf16[128,1152]{1,0:T(8,128)(2,1)S(1)} %multiply_convert_fusion.refs_1_), channel_id=1, source_target_pairs={{0,64},{16,80},{32,96},{48,112},{64,0},{80,16},{96,32},{112,48},{1... | collective-permute-start | bytes 884744 | tf_op jit(solution)/shard_map/ppermute | solution.py:324
  6.1 0.9 collective-permute-start.5
  7.1 1.9 %collective-permute-done.6.refs_0_.refs_4_ = bf16[128,1152]{1,0:T(8,128)(2,1)S(1)} collective-permute-done((bf16[128,1152]{1,0:T(8,128)(2,1)S(1)}, bf16[128,1152]{1,0:T(8,128)(2,1)S(1)}, u32[]{:S(2)}, u32[]{:S(2)}) %collective-permute-start.6) | collective-permute-done | bytes 294944 | tf_op jit(solution)/shard_map/ppermute | solution.py:321
  9.0 2.4 %shard_map.28.refs_0_ = bf16[1024,1152]{1,0:T(8,128)(2,1)S(1)} custom-call(s32[3]{0:T(128)S(1)} %pad_add_fusion.at.refs_0_.refs_6_.refs_2_, bf16[8192,1152]{1,0:T(8,128)(2,1)} %refs_2_.7, bf16[128,1152]{1,0:T(8,128)(2,1)S(1)} %collective-permute-done.6.refs_0_.refs_4_), custom_call_target="tpu_custom_call" | custom-call | flops 1000 | bytes 1000 | tf_op jit(solution)/shard_map/pallas_call | solution.py:114
  11.4 3.1 %shard_map.29.refs_0_ = bf16[2048,1152]{1,0:T(8,128)(2,1)S(1)} custom-call(s32[3]{0:T(128)S(1)} %pad_add_fusion.at.refs_0_.refs_6_.refs_2_, bf16[8192,1152]{1,0:T(8,128)(2,1)} %refs_2_.7, bf16[1024,1152]{1,0:T(8,128)(2,1)S(1)} %shard_map.28.refs_0_), custom_call_target="tpu_custom_call" | custom-call | flops 1000 | bytes 1000 | tf_op jit(solution)/shard_map/pallas_call | solution.py:114
  14.5 2.4 %shard_map.30.refs_5_ = bf16[1024,1152]{1,0:T(8,128)(2,1)S(1)} custom-call(s32[3]{0:T(128)S(1)} %pad_add_fusion.at.refs_0_.refs_6_.refs_2_, bf16[8192,1152]{1,0:T(8,128)(2,1)} %refs_2_.7, bf16[2048,1152]{1,0:T(8,128)(2,1)S(1)} %shard_map.29.refs_0_), custom_call_target="tpu_custom_call" | custom-call | flops 1000 | bytes 1000 | tf_op jit(solution)/shard_map/pallas_call | solution.py:114
  16.9 3.3 %collective-permute-done.5.refs_2_ = bf16[128,1152]{1,0:T(8,128)(2,1)S(1)} collective-permute-done((bf16[128,1152]{1,0:T(8,128)(2,1)S(1)}, bf16[128,1152]{1,0:T(8,128)(2,1)S(1)}, u32[]{:S(2)}, u32[]{:S(2)}) %collective-permute-start.5) | collective-permute-done | bytes 294944 | tf_op jit(solution)/shard_map/ppermute | solution.py:322
  20.2 4.7 %collective-permute-start.8 = (bf16[1024,1152]{1,0:T(8,128)(2,1)S(1)}, bf16[1024,1152]{1,0:T(8,128)(2,1)S(1)}, u32[]{:S(2)}, u32[]{:S(2)}) collective-permute-start(bf16[1024,1152]{1,0:T(8,128)(2,1)S(1)} %shard_map.28.refs_0_), channel_id=1, source_target_pairs={{0,1},{1,0},{2,3},{3,2},{4,5},{5,4},{6,7},{7,6},{8,9},{9,8},{10,11... | collective-permute-start | bytes 7077896 | tf_op jit(solution)/shard_map/ppermute | solution.py:351
  25.6 5.1 %collective-permute-done.7.refs_1_ = bf16[512,1152]{1,0:T(8,128)(2,1)S(1)} collective-permute-done((bf16[512,1152]{1,0:T(8,128)(2,1)S(1)}, bf16[512,1152]{1,0:T(8,128)(2,1)S(1)}, u32[]{:S(2)}, u32[]{:S(2)}) %collective-permute-start.7) | collective-permute-done | bytes 1179680 | tf_op jit(solution)/shard_map/ppermute | solution.py:342
  31.1 1.5 %collective-permute-start.4 = (bf16[128,1152]{1,0:T(8,128)(2,1)S(1)}, bf16[128,1152]{1,0:T(8,128)(2,1)S(1)}, u32[]{:S(2)}, u32[]{:S(2)}) collective-permute-start(bf16[128,1152]{1,0:T(8,128)(2,1)S(1)} %collective-permute-done.refs_6_.refs_5_.refs_1_), channel_id=1, source_target_pairs={{0,16},{16,32},{32,48},{48,0},{64,80},{80,96},{96,112},{112,64},{1... | collective-permute-start | bytes 884744 | tf_op jit(solution)/shard_map/ppermute | solution.py:326
  32.5 3.6 %collective-permute-start.3 = (bf16[128,1152]{1,0:T(8,128)(2,1)S(1)}, bf16[128,1152]{1,0:T(8,128)(2,1)S(1)}, u32[]{:S(2)}, u32[]{:S(2)}) collective-permute-start(bf16[128,1152]{1,0:T(8,128)(2,1)S(1)} %collective-permute-done.2.refs_3_), channel_id=1, source_target_pairs={{0,64},{16,80},{32,96},{48,112},{64,0},{80,16},{96,32},{112,48},{1... | collective-permute-start | bytes 884744 | tf_op jit(solution)/shard_map/ppermute | solution.py:326
  36.1 5.1 %shard_map.32.refs_0_.refs_1_ = f32[512,1024]{1,0:T(8,128)S(1)} custom-call(s32[3]{0:T(128)S(1)} %pad_add_fusion.at.refs_0_.refs_6_.refs_2_, bf16[512,1152]{1,0:T(8,128)(2,1)S(1)} %shard_map.31.refs_0_.refs_4_, bf16[512,1152]{1,0:T(8,128)(2,1)S(1)} %collective-permute-done.7.refs_1_, bf16[8192,1152]{1,0:T(8,128)(2,1)} %refs_2_.7, ...), custom_call_target="tpu_custom_call" | custom-call | flops 1000 | bytes 100000000 | tf_op jit(solution)/shard_map/pallas_call | solution.py:159
  41.7 1.3 collective-permute-start.11
  43.0 8.3 %shard_map.34.refs_0_.refs_4_.refs_1_ = f32[512,2048]{1,0:T(8,128)S(1)} custom-call(s32[3]{0:T(128)S(1)} %pad_add_fusion.at.refs_0_.refs_6_.refs_2_, bf16[512,1152]{1,0:T(8,128)(2,1)S(1)} %shard_map.31.refs_0_.refs_4_, bf16[512,1152]{1,0:T(8,128)(2,1)S(1)} %collective-permute-done.7.refs_1_, bf16[8192,1152]{1,0:T(8,128)(2,1)} %refs_2_.7, ...), custom_call_target="tpu_custom_call" | custom-call | flops 1000 | bytes 100000000 | tf_op jit(solution)/shard_map/pallas_call | solution.py:159
  52.4 1.6 %collective-permute-start.12 = (bf16[512,1152]{1,0:T(8,128)(2,1)S(1)}, bf16[512,1152]{1,0:T(8,128)(2,1)S(1)}, u32[]{:S(2)}, u32[]{:S(2)}) collective-permute-start(bf16[512,1152]{1,0:T(8,128)(2,1)S(1)} %shard_map.36.refs_0_.refs_4_.refs_2_), channel_id=1, source_target_pairs={{0,1},{1,0},{2,3},{3,2},{4,5},{5,4},{6,7},{7,6},{8,9},{9,8},{10,11... | collective-permute-start | bytes 3538952 | tf_op jit(solution)/shard_map/ppermute | solution.py:342
  54.0 2.5 %collective-permute-done.12.refs_1_.refs_3_ = bf16[512,1152]{1,0:T(8,128)(2,1)S(1)} collective-permute-done((bf16[512,1152]{1,0:T(8,128)(2,1)S(1)}, bf16[512,1152]{1,0:T(8,128)(2,1)S(1)}, u32[]{:S(2)}, u32[]{:S(2)}) %collective-permute-start.12) | collective-permute-done | bytes 1179680 | tf_op jit(solution)/shard_map/ppermute | solution.py:342
  56.9 1.4 collective-permute-start.14
  58.4 8.3 %shard_map.37.refs_0_.refs_4_.refs_1_ = f32[512,2048]{1,0:T(8,128)S(1)} custom-call(s32[3]{0:T(128)S(1)} %pad_add_fusion.at.refs_0_.refs_6_.refs_2_, bf16[512,1152]{1,0:T(8,128)(2,1)S(1)} %shard_map.36.refs_0_.refs_4_.refs_2_, bf16[512,1152]{1,0:T(8,128)(2,1)S(1)} %collective-permute-done.12.refs_1_.refs_3_, bf16[8192,1152]{1,0:T(8,128)(2,1)} %refs_2_.7, ...), custom_call_target="tpu_custom_call" | custom-call | flops 1000 | bytes 100000000 | tf_op jit(solution)/shard_map/pallas_call | solution.py:159
  66.7 6.4 %collective-permute-done.14.refs_2_.refs_3_.refs_1_ = bf16[256,1280]{1,0:T(8,128)(2,1)S(1)} collective-permute-done((bf16[256,1280]{1,0:T(8,128)(2,1)S(1)}, bf16[256,1280]{1,0:T(8,128)(2,1)S(1)}, u32[]{:S(2)}, u32[]{:S(2)}) %collective-permute-start.14) | collective-permute-done | bytes 655392 | tf_op jit(solution)/shard_map/ppermute | solution.py:225
  73.1 2.3 %collective-permute-done.15.refs_3_.refs_4_.refs_2_ = bf16[256,1280]{1,0:T(8,128)(2,1)S(1)} collective-permute-done((bf16[256,1280]{1,0:T(8,128)(2,1)S(1)}, bf16[256,1280]{1,0:T(8,128)(2,1)S(1)}, u32[]{:S(2)}, u32[]{:S(2)}) %collective-permute-start.15) | collective-permute-done | bytes 655392 | tf_op jit(solution)/shard_map/ppermute | solution.py:225
  76.4 1.1 collective-permute-start.17
  77.6 7.8 %shard_map.39 = (f32[512,1024]{1,0:T(8,128)S(1)}, bf16[512,1024]{1,0:T(8,128)(2,1)S(1)}) custom-call(s32[3]{0:T(128)S(1)} %pad_add_fusion.at.refs_0_.refs_6_.refs_2_, bf16[512,1152]{1,0:T(8,128)(2,1)S(1)} %shard_map.31.refs_0_.refs_4_, bf16[512,1152]{1,0:T(8,128)(2,1)S(1)} %collective-permute-done.7.refs_1_, ...), custom_call_target="tpu_custom_call" | custom-call | flops 1000 | bytes 100000000 | tf_op jit(solution)/shard_map/pallas_call | solution.py:159
  85.4 0.8 collective-permute-start.20
  86.2 5.1 %shard_map.40.refs_5_.refs_0_.refs_2_ = f32[512,1024]{1,0:T(8,128)S(1)} custom-call(s32[3]{0:T(128)S(1)} %pad_add_fusion.at.refs_0_.refs_6_.refs_2_, bf16[512,1152]{1,0:T(8,128)(2,1)S(1)} %shard_map.36.refs_0_.refs_4_.refs_2_, bf16[512,1152]{1,0:T(8,128)(2,1)S(1)} %collective-permute-done.12.refs_1_.refs_3_, bf16[8192,1152]{1,0:T(8,128)(2,1)} %refs_2_.7, ...), custom_call_target="tpu_custom_call" | custom-call | flops 1000 | bytes 100000000 | tf_op jit(solution)/shard_map/pallas_call | solution.py:159
  91.5 2.3 %collective-permute-done.16.refs_2_.refs_3_.refs_1_ = bf16[256,1536]{1,0:T(8,128)(2,1)S(1)} collective-permute-done((bf16[256,1536]{1,0:T(8,128)(2,1)S(1)}, bf16[256,1536]{1,0:T(8,128)(2,1)S(1)}, u32[]{:S(2)}, u32[]{:S(2)}) %collective-permute-start.16) | collective-permute-done | bytes 786464 | tf_op jit(solution)/shard_map/ppermute | solution.py:225
  93.9 1.6 %collective-permute-done.17.refs_3_.refs_4_.refs_2_ = bf16[256,1536]{1,0:T(8,128)(2,1)S(1)} collective-permute-done((bf16[256,1536]{1,0:T(8,128)(2,1)S(1)}, bf16[256,1536]{1,0:T(8,128)(2,1)S(1)}, u32[]{:S(2)}, u32[]{:S(2)}) %collective-permute-start.17) | collective-permute-done | bytes 786464 | tf_op jit(solution)/shard_map/ppermute | solution.py:225
  96.2 1.2 collective-permute-start.19
  97.7 9.4 %collective-permute-done.18.refs_3_.refs_1_ = bf16[256,1024]{1,0:T(8,128)(2,1)S(1)} collective-permute-done((bf16[256,1024]{1,0:T(8,128)(2,1)S(1)}, bf16[256,1024]{1,0:T(8,128)(2,1)S(1)}, u32[]{:S(2)}, u32[]{:S(2)}) %collective-permute-start.18) | collective-permute-done | bytes 524320 | tf_op jit(solution)/shard_map/ppermute | solution.py:225
  107.2 1.5 %collective-permute-done.19.refs_4_.refs_2_ = bf16[256,1024]{1,0:T(8,128)(2,1)S(1)} collective-permute-done((bf16[256,1024]{1,0:T(8,128)(2,1)S(1)}, bf16[256,1024]{1,0:T(8,128)(2,1)S(1)}, u32[]{:S(2)}, u32[]{:S(2)}) %collective-permute-start.19) | collective-permute-done | bytes 524320 | tf_op jit(solution)/shard_map/ppermute | solution.py:225
  108.7 2.0 %shard_map.44 = (f32[128,2048]{1,0:T(8,128)S(1)}, bf16[128,2048]{1,0:T(8,128)(2,1)}) custom-call(f32[512,2048]{1,0:T(8,128)S(1)} %shard_map.37.refs_0_.refs_4_.refs_1_, bf16[256,1536]{1,0:T(8,128)(2,1)S(1)} %collective-permute-done.16.refs_2_.refs_3_.refs_1_, bf16[256,1536]{1,0:T(8,128)(2,1)S(1)} %collective-permute-done.17.refs_3_.refs_4_.refs_2_, ...), custom_call_target="tpu_custom_call" | custom-call | flops 1000 | bytes 100000000 | tf_op jit(solution)/shard_map/pallas_call | solution.py:83
  111.9 1.2 collective-permute-start.22
  113.1 0.7 collective-permute-start.26
  113.9 5.3 %collective-permute-done.21.refs_3_.refs_2_ = bf16[256,768]{1,0:T(8,128)(2,1)S(1)} collective-permute-done((bf16[256,768]{1,0:T(8,128)(2,1)S(1)}, bf16[256,768]{1,0:T(8,128)(2,1)S(1)}, u32[]{:S(2)}, u32[]{:S(2)}) %collective-permute-start.21) | collective-permute-done | bytes 393248 | tf_op jit(solution)/shard_map/ppermute | solution.py:225
  119.2 1.5 %collective-permute-done.22.refs_4_.refs_3_ = bf16[256,768]{1,0:T(8,128)(2,1)S(1)} collective-permute-done((bf16[256,768]{1,0:T(8,128)(2,1)S(1)}, bf16[256,768]{1,0:T(8,128)(2,1)S(1)}, u32[]{:S(2)}, u32[]{:S(2)}) %collective-permute-start.22) | collective-permute-done | bytes 393248 | tf_op jit(solution)/shard_map/ppermute | solution.py:225
  120.7 1.5 %shard_map.46 = (f32[128,1024]{1,0:T(8,128)S(1)}, bf16[128,1024]{1,0:T(8,128)(2,1)}) custom-call(f32[512,1024]{1,0:T(8,128)S(1)} %shard_map.40.refs_5_.refs_0_.refs_2_, bf16[256,1024]{1,0:T(8,128)(2,1)S(1)} %collective-permute-done.18.refs_3_.refs_1_, bf16[256,1024]{1,0:T(8,128)(2,1)S(1)} %collective-permute-done.19.refs_4_.refs_2_, ...), custom_call_target="tpu_custom_call" | custom-call | flops 1000 | bytes 100000000 | tf_op jit(solution)/shard_map/pallas_call | solution.py:83
  123.0 0.9 shard_map.47
  124.1 1.2 collective-permute-start.25
  125.3 1.2 copy-done.3
  126.6 1.5 %shard_map.48 = (f32[64,2048]{1,0:T(8,128)S(1)}, f32[64,2048]{1,0:T(8,128)S(1)}) custom-call(f32[128,2048]{1,0:T(8,128)S(1)} %copy-done.3, bf16[128,2048]{1,0:T(8,128)(2,1)} %collective-permute-done.26.refs_1_, s32[3]{0:T(128)S(1)} %pad_add_fusion.at.refs_0_.refs_6_.refs_2_, bf16[256,256]{1,0:T(8,128)(2,1)} %get-tuple-element.51.refs_3_), custom_call_target="tpu_custom_call" | custom-call | flops 1000 | bytes 1000 | tf_op jit(solution)/shard_map/pallas_call | solution.py:83
  128.0 4.9 %collective-permute-start.28 = (f32[64,2048]{1,0:T(8,128)S(1)}, f32[64,2048]{1,0:T(8,128)S(1)}, u32[]{:S(2)}, u32[]{:S(2)}) collective-permute-start(f32[64,2048]{1,0:T(8,128)S(1)} %get-tuple-element.53.refs_7_), channel_id=1, source_target_pairs={{0,1},{1,0},{2,3},{3,2},{4,5},{5,4},{6,7},{7,6},{8,9},{9,8},{10,11... | collective-permute-start | bytes 1572872 | tf_op jit(solution)/shard_map/ppermute | solution.py:375
  132.9 1.0 copy-done.1
  133.9 1.2 shard_map.49
  135.1 2.0 %collective-permute-start.29 = (f32[64,1024]{1,0:T(8,128)S(1)}, f32[64,1024]{1,0:T(8,128)S(1)}, u32[]{:S(2)}, u32[]{:S(2)}) collective-permute-start(f32[64,1024]{1,0:T(8,128)S(1)} %get-tuple-element.54.refs_3_), channel_id=1, source_target_pairs={{0,1},{1,0},{2,3},{3,2},{4,5},{5,4},{6,7},{7,6},{8,9},{9,8},{10,11... | collective-permute-start | bytes 786440 | tf_op jit(solution)/shard_map/ppermute | solution.py:375
  137.2 1.1 shard_map.50
  138.5 1.4 collective-permute-done.27
  140.2 1.5 %pad_maximum_fusion = f32[64,8192]{1,0:T(8,128)} fusion(f32[64,4096]{1,0:T(8,128)S(1)} %get-tuple-element.60, f32[64,4096]{1,0:T(8,128)S(1)} %get-tuple-element.59), kind=kLoop, calls=%fused_computation | loop fusion | flops 524288 | bytes 4194304 | tf_op jit(solution)/shard_map/concatenate | solution.py:379
  (57 shorter events, 8.5 us)
Async XLA Ops:
  1.0 7.9 %collective-permute-start.6 = (bf16[128,1152]{1,0:T(8,128)(2,1)S(1)}, bf16[128,1152]{1,0:T(8,128)(2,1)S(1)}, u32[]{:S(2)}, u32[]{:S(2)}) collective-permute-start(bf16[128,1152]{1,0:T(8,128)(2,1)S(1)} %multiply_convert_fusion.refs_1_), channel_id=1, source_target_pairs={{0,16},{16,32},{32,48},{48,0},{64,80},{80,96},{96,112},{112,64},{1... | collective-permute-start | bytes 884744 | tf_op jit(solution)/shard_map/ppermute | solution.py:321
  2.1 14.8 %collective-permute-start = (bf16[128,1152]{1,0:T(8,128)(2,1)S(1)}, bf16[128,1152]{1,0:T(8,128)(2,1)S(1)}, u32[]{:S(2)}, u32[]{:S(2)}) collective-permute-start(bf16[128,1152]{1,0:T(8,128)(2,1)S(1)} %multiply_convert_fusion.refs_1_), channel_id=1, source_target_pairs={{0,64},{16,80},{32,96},{48,112},{64,0},{80,16},{96,32},{112,48},{1... | collective-permute-start | bytes 884744 | tf_op jit(solution)/shard_map/ppermute | solution.py:324
  5.7 11.2 %collective-permute-start.2 = (bf16[128,1152]{1,0:T(8,128)(2,1)S(1)}, bf16[128,1152]{1,0:T(8,128)(2,1)S(1)}, u32[]{:S(2)}, u32[]{:S(2)}) collective-permute-start(bf16[128,1152]{1,0:T(8,128)(2,1)S(1)} %multiply_convert_fusion.refs_1_), channel_id=1, source_target_pairs={{0,32},{16,48},{32,0},{48,16},{64,96},{80,112},{96,64},{112,80},{1... | collective-permute-start | bytes 884744 | tf_op jit(solution)/shard_map/ppermute | solution.py:323
  6.1 14.1 %collective-permute-start.5 = (bf16[128,1152]{1,0:T(8,128)(2,1)S(1)}, bf16[128,1152]{1,0:T(8,128)(2,1)S(1)}, u32[]{:S(2)}, u32[]{:S(2)}) collective-permute-start(bf16[128,1152]{1,0:T(8,128)(2,1)S(1)} %multiply_convert_fusion.refs_1_), channel_id=1, source_target_pairs={{16,0},{32,16},{48,32},{0,48},{80,64},{96,80},{112,96},{64,112},{1... | collective-permute-start | bytes 884744 | tf_op jit(solution)/shard_map/ppermute | solution.py:322
  20.2 10.5 %collective-permute-start.8 = (bf16[1024,1152]{1,0:T(8,128)(2,1)S(1)}, bf16[1024,1152]{1,0:T(8,128)(2,1)S(1)}, u32[]{:S(2)}, u32[]{:S(2)}) collective-permute-start(bf16[1024,1152]{1,0:T(8,128)(2,1)S(1)} %shard_map.28.refs_0_), channel_id=1, source_target_pairs={{0,1},{1,0},{2,3},{3,2},{4,5},{5,4},{6,7},{7,6},{8,9},{9,8},{10,11... | collective-permute-start | bytes 7077896 | tf_op jit(solution)/shard_map/ppermute | solution.py:351
  25.5 5.2 %collective-permute-start.7 = (bf16[512,1152]{1,0:T(8,128)(2,1)S(1)}, bf16[512,1152]{1,0:T(8,128)(2,1)S(1)}, u32[]{:S(2)}, u32[]{:S(2)}) collective-permute-start(bf16[512,1152]{1,0:T(8,128)(2,1)S(1)} %shard_map.31.refs_0_.refs_4_), channel_id=1, source_target_pairs={{0,1},{1,0},{2,3},{3,2},{4,5},{5,4},{6,7},{7,6},{8,9},{9,8},{10,11... | collective-permute-start | bytes 3538952 | tf_op jit(solution)/shard_map/ppermute | solution.py:342
  30.7 11.0 %collective-permute-start.9 = (bf16[2048,1152]{1,0:T(8,128)(2,1)S(1)}, bf16[2048,1152]{1,0:T(8,128)(2,1)S(1)}, u32[]{:S(2)}, u32[]{:S(2)}) collective-permute-start(bf16[2048,1152]{1,0:T(8,128)(2,1)S(1)} %shard_map.29.refs_0_), channel_id=1, source_target_pairs={{0,1},{1,0},{2,3},{3,2},{4,5},{5,4},{6,7},{7,6},{8,9},{9,8},{10,11... | collective-permute-start | bytes 14155784 | tf_op jit(solution)/shard_map/ppermute | solution.py:351
  31.1 20.2 %collective-permute-start.1 = (bf16[128,1152]{1,0:T(8,128)(2,1)S(1)}, bf16[128,1152]{1,0:T(8,128)(2,1)S(1)}, u32[]{:S(2)}, u32[]{:S(2)}) collective-permute-start(bf16[128,1152]{1,0:T(8,128)(2,1)S(1)} %collective-permute-done.refs_6_.refs_5_.refs_1_), channel_id=1, source_target_pairs={{16,0},{32,16},{48,32},{0,48},{80,64},{96,80},{112,96},{64,112},{1... | collective-permute-start | bytes 884744 | tf_op jit(solution)/shard_map/ppermute | solution.py:326
  31.1 20.2 %collective-permute-start.4 = (bf16[128,1152]{1,0:T(8,128)(2,1)S(1)}, bf16[128,1152]{1,0:T(8,128)(2,1)S(1)}, u32[]{:S(2)}, u32[]{:S(2)}) collective-permute-start(bf16[128,1152]{1,0:T(8,128)(2,1)S(1)} %collective-permute-done.refs_6_.refs_5_.refs_1_), channel_id=1, source_target_pairs={{0,16},{16,32},{32,48},{48,0},{64,80},{80,96},{96,112},{112,64},{1... | collective-permute-start | bytes 884744 | tf_op jit(solution)/shard_map/ppermute | solution.py:326
  32.5 18.8 %collective-permute-start.3 = (bf16[128,1152]{1,0:T(8,128)(2,1)S(1)}, bf16[128,1152]{1,0:T(8,128)(2,1)S(1)}, u32[]{:S(2)}, u32[]{:S(2)}) collective-permute-start(bf16[128,1152]{1,0:T(8,128)(2,1)S(1)} %collective-permute-done.2.refs_3_), channel_id=1, source_target_pairs={{0,64},{16,80},{32,96},{48,112},{64,0},{80,16},{96,32},{112,48},{1... | collective-permute-start | bytes 884744 | tf_op jit(solution)/shard_map/ppermute | solution.py:326
  41.4 9.9 %collective-permute-start.10 = (bf16[256,512]{1,0:T(8,128)(2,1)S(1)}, bf16[256,512]{1,0:T(8,128)(2,1)S(1)}, u32[]{:S(2)}, u32[]{:S(2)}) collective-permute-start(bf16[256,512]{1,0:T(8,128)(2,1)S(1)} %get-tuple-element.35), channel_id=1, source_target_pairs={{0,2},{1,3},{2,4},{3,5},{4,6},{5,7},{6,0},{7,1},{8,10},{9,11},{10,... | collective-permute-start | bytes 786440 | tf_op jit(solution)/shard_map/ppermute | solution.py:225
  41.7 9.6 %collective-permute-start.11 = (bf16[256,512]{1,0:T(8,128)(2,1)S(1)}, bf16[256,512]{1,0:T(8,128)(2,1)S(1)}, u32[]{:S(2)}, u32[]{:S(2)}) collective-permute-start(bf16[256,512]{1,0:T(8,128)(2,1)S(1)} %get-tuple-element.34.refs_4_), channel_id=1, source_target_pairs={{0,6},{1,7},{2,0},{3,1},{4,2},{5,3},{6,4},{7,5},{8,14},{9,15},{10,... | collective-permute-start | bytes 786440 | tf_op jit(solution)/shard_map/ppermute | solution.py:225
  52.4 4.1 %collective-permute-start.12 = (bf16[512,1152]{1,0:T(8,128)(2,1)S(1)}, bf16[512,1152]{1,0:T(8,128)(2,1)S(1)}, u32[]{:S(2)}, u32[]{:S(2)}) collective-permute-start(bf16[512,1152]{1,0:T(8,128)(2,1)S(1)} %shard_map.36.refs_0_.refs_4_.refs_2_), channel_id=1, source_target_pairs={{0,1},{1,0},{2,3},{3,2},{4,5},{5,4},{6,7},{7,6},{8,9},{9,8},{10,11... | collective-permute-start | bytes 3538952 | tf_op jit(solution)/shard_map/ppermute | solution.py:342
  56.5 21.1 %collective-permute-start.13 = (bf16[1024,1152]{1,0:T(8,128)(2,1)S(1)}, bf16[1024,1152]{1,0:T(8,128)(2,1)S(1)}, u32[]{:S(2)}, u32[]{:S(2)}) collective-permute-start(bf16[1024,1152]{1,0:T(8,128)(2,1)S(1)} %shard_map.30.refs_5_), channel_id=1, source_target_pairs={{0,1},{1,0},{2,3},{3,2},{4,5},{5,4},{6,7},{7,6},{8,9},{9,8},{10,11... | collective-permute-start | bytes 7077896 | tf_op jit(solution)/shard_map/ppermute | solution.py:345
  56.9 16.2 %collective-permute-start.14 = (bf16[256,1280]{1,0:T(8,128)(2,1)S(1)}, bf16[256,1280]{1,0:T(8,128)(2,1)S(1)}, u32[]{:S(2)}, u32[]{:S(2)}) collective-permute-start(bf16[256,1280]{1,0:T(8,128)(2,1)S(1)} %get-tuple-element.38), channel_id=1, source_target_pairs={{0,2},{1,3},{2,4},{3,5},{4,6},{5,7},{6,0},{7,1},{8,10},{9,11},{10,... | collective-permute-start | bytes 1966088 | tf_op jit(solution)/shard_map/ppermute | solution.py:225
  58.3 17.1 %collective-permute-start.15 = (bf16[256,1280]{1,0:T(8,128)(2,1)S(1)}, bf16[256,1280]{1,0:T(8,128)(2,1)S(1)}, u32[]{:S(2)}, u32[]{:S(2)}) collective-permute-start(bf16[256,1280]{1,0:T(8,128)(2,1)S(1)} %get-tuple-element.36.refs_5_), channel_id=1, source_target_pairs={{0,6},{1,7},{2,0},{3,1},{4,2},{5,3},{6,4},{7,5},{8,14},{9,15},{10,... | collective-permute-start | bytes 1966088 | tf_op jit(solution)/shard_map/ppermute | solution.py:225
  75.9 18.0 %collective-permute-start.16 = (bf16[256,1536]{1,0:T(8,128)(2,1)S(1)}, bf16[256,1536]{1,0:T(8,128)(2,1)S(1)}, u32[]{:S(2)}, u32[]{:S(2)}) collective-permute-start(bf16[256,1536]{1,0:T(8,128)(2,1)S(1)} %get-tuple-element.41), channel_id=1, source_target_pairs={{0,2},{1,3},{2,4},{3,5},{4,6},{5,7},{6,0},{7,1},{8,10},{9,11},{10,... | collective-permute-start | bytes 2359304 | tf_op jit(solution)/shard_map/ppermute | solution.py:225
  76.4 19.0 %collective-permute-start.17 = (bf16[256,1536]{1,0:T(8,128)(2,1)S(1)}, bf16[256,1536]{1,0:T(8,128)(2,1)S(1)}, u32[]{:S(2)}, u32[]{:S(2)}) collective-permute-start(bf16[256,1536]{1,0:T(8,128)(2,1)S(1)} %get-tuple-element.39.refs_6_), channel_id=1, source_target_pairs={{0,6},{1,7},{2,0},{3,1},{4,2},{5,3},{6,4},{7,5},{8,14},{9,15},{10,... | collective-permute-start | bytes 2359304 | tf_op jit(solution)/shard_map/ppermute | solution.py:225
  85.4 25.3 %collective-permute-start.20 = (bf16[512,1024]{1,0:T(8,128)(2,1)S(1)}, bf16[512,1024]{1,0:T(8,128)(2,1)S(1)}, u32[]{:S(2)}, u32[]{:S(2)}) collective-permute-start(bf16[512,1024]{1,0:T(8,128)(2,1)S(1)} %get-tuple-element.44), channel_id=1, source_target_pairs={{0,8},{1,9},{2,10},{3,11},{4,12},{5,13},{6,14},{7,15},{8,0},{9,1},... | collective-permute-start | bytes 3145736 | tf_op jit(solution)/shard_map/ppermute | solution.py:357
  95.8 11.3 %collective-permute-start.18 = (bf16[256,1024]{1,0:T(8,128)(2,1)S(1)}, bf16[256,1024]{1,0:T(8,128)(2,1)S(1)}, u32[]{:S(2)}, u32[]{:S(2)}) collective-permute-start(bf16[256,1024]{1,0:T(8,128)(2,1)S(1)} %get-tuple-element.42), channel_id=1, source_target_pairs={{0,2},{1,3},{2,4},{3,5},{4,6},{5,7},{6,0},{7,1},{8,10},{9,11},{10,... | collective-permute-start | bytes 1572872 | tf_op jit(solution)/shard_map/ppermute | solution.py:225
  96.2 12.5 %collective-permute-start.19 = (bf16[256,1024]{1,0:T(8,128)(2,1)S(1)}, bf16[256,1024]{1,0:T(8,128)(2,1)S(1)}, u32[]{:S(2)}, u32[]{:S(2)}) collective-permute-start(bf16[256,1024]{1,0:T(8,128)(2,1)S(1)} %get-tuple-element.43.refs_5_), channel_id=1, source_target_pairs={{0,6},{1,7},{2,0},{3,1},{4,2},{5,3},{6,4},{7,5},{8,14},{9,15},{10,... | collective-permute-start | bytes 1572872 | tf_op jit(solution)/shard_map/ppermute | solution.py:225
  110.7 1.0 copy-start.2
  111.7 7.5 %collective-permute-start.21 = (bf16[256,768]{1,0:T(8,128)(2,1)S(1)}, bf16[256,768]{1,0:T(8,128)(2,1)S(1)}, u32[]{:S(2)}, u32[]{:S(2)}) collective-permute-start(bf16[256,768]{1,0:T(8,128)(2,1)S(1)} %get-tuple-element.46), channel_id=1, source_target_pairs={{0,2},{1,3},{2,4},{3,5},{4,6},{5,7},{6,0},{7,1},{8,10},{9,11},{10,... | collective-permute-start | bytes 1179656 | tf_op jit(solution)/shard_map/ppermute | solution.py:225
  111.9 8.8 %collective-permute-start.22 = (bf16[256,768]{1,0:T(8,128)(2,1)S(1)}, bf16[256,768]{1,0:T(8,128)(2,1)S(1)}, u32[]{:S(2)}, u32[]{:S(2)}) collective-permute-start(bf16[256,768]{1,0:T(8,128)(2,1)S(1)} %get-tuple-element.47.refs_7_), channel_id=1, source_target_pairs={{0,6},{1,7},{2,0},{3,1},{4,2},{5,3},{6,4},{7,5},{8,14},{9,15},{10,... | collective-permute-start | bytes 1179656 | tf_op jit(solution)/shard_map/ppermute | solution.py:225
  113.1 12.2 %collective-permute-start.26 = (bf16[128,2048]{1,0:T(8,128)(2,1)}, bf16[128,2048]{1,0:T(8,128)(2,1)}, u32[]{:S(2)}, u32[]{:S(2)}) collective-permute-start(bf16[128,2048]{1,0:T(8,128)(2,1)} %get-tuple-element.45.refs_5_), channel_id=1, source_target_pairs={{0,8},{1,9},{2,10},{3,11},{4,12},{5,13},{6,14},{7,15},{8,0},{9,1},... | collective-permute-start | bytes 1572872 | tf_op jit(solution)/shard_map/ppermute | solution.py:368
  120.7 2.3 %copy-start = (bf16[256,768]{1,0:T(8,128)(2,1)}, bf16[256,768]{1,0:T(8,128)(2,1)S(1)}, u32[]{:S(2)}) copy-start(bf16[256,768]{1,0:T(8,128)(2,1)S(1)} %collective-permute-done.22.refs_4_.refs_3_) | copy-start | bytes 1179652
  122.2 1.6 %copy-start.4 = (f32[128,1024]{1,0:T(8,128)}, f32[128,1024]{1,0:T(8,128)S(1)}, u32[]{:S(2)}) copy-start(f32[128,1024]{1,0:T(8,128)S(1)} %get-tuple-element.48.refs_0_) | copy-start | bytes 1572868
  122.2 14.9 %collective-permute-start.23 = (bf16[128,1024]{1,0:T(8,128)(2,1)}, bf16[128,1024]{1,0:T(8,128)(2,1)}, u32[]{:S(2)}, u32[]{:S(2)}) collective-permute-start(bf16[128,1024]{1,0:T(8,128)(2,1)} %get-tuple-element.49.refs_4_), channel_id=1, source_target_pairs={{0,8},{1,9},{2,10},{3,11},{4,12},{5,13},{6,14},{7,15},{8,0},{9,1},... | collective-permute-start | bytes 786440 | tf_op jit(solution)/shard_map/ppermute | solution.py:368
  123.9 9.1 %collective-permute-start.24 = (bf16[256,256]{1,0:T(8,128)(2,1)}, bf16[256,256]{1,0:T(8,128)(2,1)}, u32[]{:S(2)}, u32[]{:S(2)}) collective-permute-start(bf16[256,256]{1,0:T(8,128)(2,1)} %get-tuple-element.50), channel_id=1, source_target_pairs={{0,2},{1,3},{2,4},{3,5},{4,6},{5,7},{6,0},{7,1},{8,10},{9,11},{10,... | collective-permute-start | bytes 393224 | tf_op jit(solution)/shard_map/ppermute | solution.py:225
  124.1 8.8 %collective-permute-start.25 = (bf16[256,256]{1,0:T(8,128)(2,1)}, bf16[256,256]{1,0:T(8,128)(2,1)}, u32[]{:S(2)}, u32[]{:S(2)}) collective-permute-start(bf16[256,256]{1,0:T(8,128)(2,1)} %get-tuple-element.51.refs_3_), channel_id=1, source_target_pairs={{0,6},{1,7},{2,0},{3,1},{4,2},{5,3},{6,4},{7,5},{8,14},{9,15},{10,... | collective-permute-start | bytes 393224 | tf_op jit(solution)/shard_map/ppermute | solution.py:225
  125.3 1.2 copy-start.3
  126.6 10.6 %copy-start.5 = (f32[128,1024]{1,0:T(8,128)S(1)}, f32[128,1024]{1,0:T(8,128)}, u32[]{:S(2)}) copy-start(f32[128,1024]{1,0:T(8,128)} %copy-done.4) | copy-start | bytes 1572868
  128.0 11.9 %collective-permute-start.28 = (f32[64,2048]{1,0:T(8,128)S(1)}, f32[64,2048]{1,0:T(8,128)S(1)}, u32[]{:S(2)}, u32[]{:S(2)}) collective-permute-start(f32[64,2048]{1,0:T(8,128)S(1)} %get-tuple-element.53.refs_7_), channel_id=1, source_target_pairs={{0,1},{1,0},{2,3},{3,2},{4,5},{5,4},{6,7},{7,6},{8,9},{9,8},{10,11... | collective-permute-start | bytes 1572872 | tf_op jit(solution)/shard_map/ppermute | solution.py:375
  132.9 1.0 copy-start.1
  135.1 4.9 %collective-permute-start.29 = (f32[64,1024]{1,0:T(8,128)S(1)}, f32[64,1024]{1,0:T(8,128)S(1)}, u32[]{:S(2)}, u32[]{:S(2)}) collective-permute-start(f32[64,1024]{1,0:T(8,128)S(1)} %get-tuple-element.54.refs_3_), channel_id=1, source_target_pairs={{0,1},{1,0},{2,3},{3,2},{4,5},{5,4},{6,7},{7,6},{8,9},{9,8},{10,11... | collective-permute-start | bytes 786440 | tf_op jit(solution)/shard_map/ppermute | solution.py:375
  138.3 1.6 %collective-permute-start.27 = (f32[64,1024]{1,0:T(8,128)S(1)}, f32[64,1024]{1,0:T(8,128)S(1)}, u32[]{:S(2)}, u32[]{:S(2)}) collective-permute-start(f32[64,1024]{1,0:T(8,128)S(1)} %get-tuple-element.58), channel_id=1, source_target_pairs={{0,1},{1,0},{2,3},{3,2},{4,5},{5,4},{6,7},{7,6},{8,9},{9,8},{10,11... | collective-permute-start | bytes 786440 | tf_op jit(solution)/shard_map/ppermute | solution.py:375

commit v4 on v2

--- a/solution.py
+++ b/solution.py
@@ -216,9 +216,9 @@
                 down[rows, to] = (added(terms2, 3, there) + wide(down1[:CHIP, here])).astype(BF16)
 
         if first:
-            over(n_first, 128, one)
+            over(n_first, 256, one)
         if second:
-            over(n_second, 128, two)
+            over(n_second, 256, two)
 
     shape = (2 * CHIP, n_first + n_second), BF16
     up, down = run(kernel, (), [(shape, None, pltpu.VMEM)] * 2, vmem(ins + ins2), dep, LONG)
@@ -247,7 +247,7 @@
                 right = added(terms, 0, pl.ds(half + low + c, step)) + wide(down2[rows, moved]) + wide(up1[CHIP:, here])
                 store(half + low + c, step, right, rest)
 
-        over(half // 2, 128, one)
+        over(half // 2, 256, one)
 
     ins = vmem(unit.terms + [unit.up1, unit.down1, unit.up2, unit.down2]) + extra
     return run(kernel, (), outs, ins, dep, LONG)
@@ -287,7 +287,7 @@
             to = pl.ds(c0, step)
             mine[:, to], theirs[:, to] = split_rows(at, None, s[:, to] + wide(c[:, to]))
 
-        over(n, 128, one)
+        over(n, 256, one)
 
     shape = (HALF, n), F32
     return run(kernel, (), [(shape, None, pltpu.VMEM)] * 2, vmem([stays, came]) + [(place, None, pltpu.SMEM)], dep)

time: 142 us -> 140 us (0.986)
  Pallas kernels: 54.4 us -> 52.5 us
    pallas_call x15, Pallas kernels: 11.9 us -> 9.97 us  [run(): pl.pallas_call(body, grid=grid, out_shape=shapes, in_specs=in_specs, out_...]
  transfers between devices with their start and end apart: 30 -> 30, of which waited for: 11 -> 11; matrix products, arithmetic and copies ran while one was open for 0% -> 0% of each run, Pallas kernels for 38% -> 37%
where the time goes in v4:
time: 140 us; the launch traced here: 139 us
  Pallas kernels  52.5 us (38%)
  starting transfers between devices  42.1 us (30%)
  waiting for transfers between devices  38.8 us (28%)
  other arithmetic  2.75 us (2%)
  local copies, waits for them, and re-layouts  2.38 us (2%)
    pallas_call x5, Pallas kernels, product(): pl.pallas_call(kernel, grid_spec=pltpu.PrefetchScalarGridSpec(num_scalar_...  34.7 us
    ppermute x6, waiting for transfers between devices, send(): lax.ppermute(up, 'gc', X_UP)  22.6 us
    ppermute x6, starting transfers between devices, send(): lax.ppermute(down, 'gc', X_DOWN)  17.2 us
    pallas_call x15, Pallas kernels, run(): pl.pallas_call(body, grid=grid, out_shape=shapes, in_specs=in_specs, out_...  9.97 us
    pallas_call x3, Pallas kernels, cut(): pl.pallas_call(kernel, grid_spec=pltpu.PrefetchScalarGridSpec(num_scalar_...  7.88 us
    ppermute x1, starting transfers between devices, shards(): lax.ppermute(y_far, 'gr', Z_FAR)  3.89 us
    ppermute x1, starting transfers between devices, shards(): z_far = lax.ppermute(mine, 'gr', Z_FAR)  3.88 us
    ppermute x6, starting transfers between devices, send(): lax.ppermute(up, 'gc', X_UP)  3.52 us
  transfers between devices with their start and end apart: 30, of which 11 were waited for; matrix products, arithmetic and copies ran while one was open for 0% of the time, Pallas kernels for 37%

profile of v4, /device:TPU:0, one launch (start us, length us, event | category | flops | bytes accessed | tf_op | source)
XLA Modules:
  0.0 138.9 jit_solution(6124834499063276401)
XLA Ops:
  0.0 1.0 multiply_convert_fusion.refs_1_
  1.0 1.7 %collective-permute-start.6 = (bf16[128,1152]{1,0:T(8,128)(2,1)S(1)}, bf16[128,1152]{1,0:T(8,128)(2,1)S(1)}, u32[]{:S(2)}, u32[]{:S(2)}) collective-permute-start(bf16[128,1152]{1,0:T(8,128)(2,1)S(1)} %multiply_convert_fusion.refs_1_), channel_id=1, source_target_pairs={{0,16},{16,32},{32,48},{48,0},{64,80},{80,96},{96,112},{112,64},{1... | collective-permute-start | bytes 884744 | tf_op jit(solution)/shard_map/ppermute | solution.py:321
  2.8 1.6 %collective-permute-start.5 = (bf16[128,1152]{1,0:T(8,128)(2,1)S(1)}, bf16[128,1152]{1,0:T(8,128)(2,1)S(1)}, u32[]{:S(2)}, u32[]{:S(2)}) collective-permute-start(bf16[128,1152]{1,0:T(8,128)(2,1)S(1)} %multiply_convert_fusion.refs_1_), channel_id=1, source_target_pairs={{16,0},{32,16},{48,32},{0,48},{80,64},{96,80},{112,96},{64,112},{1... | collective-permute-start | bytes 884744 | tf_op jit(solution)/shard_map/ppermute | solution.py:322
  4.3 2.1 %collective-permute-start.2 = (bf16[128,1152]{1,0:T(8,128)(2,1)S(1)}, bf16[128,1152]{1,0:T(8,128)(2,1)S(1)}, u32[]{:S(2)}, u32[]{:S(2)}) collective-permute-start(bf16[128,1152]{1,0:T(8,128)(2,1)S(1)} %multiply_convert_fusion.refs_1_), channel_id=1, source_target_pairs={{0,32},{16,48},{32,0},{48,16},{64,96},{80,112},{96,64},{112,80},{1... | collective-permute-start | bytes 884744 | tf_op jit(solution)/shard_map/ppermute | solution.py:323
  6.4 3.9 %collective-permute-start = (bf16[128,1152]{1,0:T(8,128)(2,1)S(1)}, bf16[128,1152]{1,0:T(8,128)(2,1)S(1)}, u32[]{:S(2)}, u32[]{:S(2)}) collective-permute-start(bf16[128,1152]{1,0:T(8,128)(2,1)S(1)} %multiply_convert_fusion.refs_1_), channel_id=1, source_target_pairs={{0,64},{16,80},{32,96},{48,112},{64,0},{80,16},{96,32},{112,48},{1... | collective-permute-start | bytes 884744 | tf_op jit(solution)/shard_map/ppermute | solution.py:324
  10.4 0.8 collective-permute-done.6.refs_0_.refs_4_
  11.2 2.4 %shard_map.28.refs_0_ = bf16[1024,1152]{1,0:T(8,128)(2,1)S(1)} custom-call(s32[3]{0:T(128)S(1)} %pad_add_fusion.at.refs_0_.refs_6_.refs_2_, bf16[8192,1152]{1,0:T(8,128)(2,1)} %refs_2_.7, bf16[128,1152]{1,0:T(8,128)(2,1)S(1)} %collective-permute-done.6.refs_0_.refs_4_), custom_call_target="tpu_custom_call" | custom-call | flops 1000 | bytes 1000 | tf_op jit(solution)/shard_map/pallas_call | solution.py:114
  13.6 3.3 %collective-permute-done.5.refs_2_ = bf16[128,1152]{1,0:T(8,128)(2,1)S(1)} collective-permute-done((bf16[128,1152]{1,0:T(8,128)(2,1)S(1)}, bf16[128,1152]{1,0:T(8,128)(2,1)S(1)}, u32[]{:S(2)}, u32[]{:S(2)}) %collective-permute-start.5) | collective-permute-done | bytes 294944 | tf_op jit(solution)/shard_map/ppermute | solution.py:322
  16.9 1.8 %collective-permute-done.2.refs_3_ = bf16[128,1152]{1,0:T(8,128)(2,1)S(1)} collective-permute-done((bf16[128,1152]{1,0:T(8,128)(2,1)S(1)}, bf16[128,1152]{1,0:T(8,128)(2,1)S(1)}, u32[]{:S(2)}, u32[]{:S(2)}) %collective-permute-start.2) | collective-permute-done | bytes 294944 | tf_op jit(solution)/shard_map/ppermute | solution.py:323
  18.7 3.1 %shard_map.29.refs_0_ = bf16[2048,1152]{1,0:T(8,128)(2,1)S(1)} custom-call(s32[3]{0:T(128)S(1)} %pad_add_fusion.at.refs_0_.refs_6_.refs_2_, bf16[8192,1152]{1,0:T(8,128)(2,1)} %refs_2_.7, bf16[1024,1152]{1,0:T(8,128)(2,1)S(1)} %shard_map.28.refs_0_), custom_call_target="tpu_custom_call" | custom-call | flops 1000 | bytes 1000 | tf_op jit(solution)/shard_map/pallas_call | solution.py:114
  21.8 2.4 %shard_map.30.refs_5_ = bf16[1024,1152]{1,0:T(8,128)(2,1)S(1)} custom-call(s32[3]{0:T(128)S(1)} %pad_add_fusion.at.refs_0_.refs_6_.refs_2_, bf16[8192,1152]{1,0:T(8,128)(2,1)} %refs_2_.7, bf16[2048,1152]{1,0:T(8,128)(2,1)S(1)} %shard_map.29.refs_0_), custom_call_target="tpu_custom_call" | custom-call | flops 1000 | bytes 1000 | tf_op jit(solution)/shard_map/pallas_call | solution.py:114
  24.2 0.6 shard_map.31.refs_0_.refs_4_
  25.5 2.5 %collective-permute-done.7.refs_1_ = bf16[512,1152]{1,0:T(8,128)(2,1)S(1)} collective-permute-done((bf16[512,1152]{1,0:T(8,128)(2,1)S(1)}, bf16[512,1152]{1,0:T(8,128)(2,1)S(1)}, u32[]{:S(2)}, u32[]{:S(2)}) %collective-permute-start.7) | collective-permute-done | bytes 1179680 | tf_op jit(solution)/shard_map/ppermute | solution.py:342
  28.4 3.9 %collective-permute-start.3 = (bf16[128,1152]{1,0:T(8,128)(2,1)S(1)}, bf16[128,1152]{1,0:T(8,128)(2,1)S(1)}, u32[]{:S(2)}, u32[]{:S(2)}) collective-permute-start(bf16[128,1152]{1,0:T(8,128)(2,1)S(1)} %collective-permute-done.2.refs_3_), channel_id=1, source_target_pairs={{0,64},{16,80},{32,96},{48,112},{64,0},{80,16},{96,32},{112,48},{1... | collective-permute-start | bytes 884744 | tf_op jit(solution)/shard_map/ppermute | solution.py:326
  32.3 1.1 collective-permute-start.4
  33.5 2.1 %collective-permute-start.1 = (bf16[128,1152]{1,0:T(8,128)(2,1)S(1)}, bf16[128,1152]{1,0:T(8,128)(2,1)S(1)}, u32[]{:S(2)}, u32[]{:S(2)}) collective-permute-start(bf16[128,1152]{1,0:T(8,128)(2,1)S(1)} %collective-permute-done.refs_6_.refs_5_.refs_1_), channel_id=1, source_target_pairs={{16,0},{32,16},{48,32},{0,48},{80,64},{96,80},{112,96},{64,112},{1... | collective-permute-start | bytes 884744 | tf_op jit(solution)/shard_map/ppermute | solution.py:326
  35.6 5.1 %shard_map.32.refs_0_.refs_1_ = f32[512,1024]{1,0:T(8,128)S(1)} custom-call(s32[3]{0:T(128)S(1)} %pad_add_fusion.at.refs_0_.refs_6_.refs_2_, bf16[512,1152]{1,0:T(8,128)(2,1)S(1)} %shard_map.31.refs_0_.refs_4_, bf16[512,1152]{1,0:T(8,128)(2,1)S(1)} %collective-permute-done.7.refs_1_, bf16[8192,1152]{1,0:T(8,128)(2,1)} %refs_2_.7, ...), custom_call_target="tpu_custom_call" | custom-call | flops 1000 | bytes 100000000 | tf_op jit(solution)/shard_map/pallas_call | solution.py:159
  40.8 1.6 %collective-permute-start.10 = (bf16[256,512]{1,0:T(8,128)(2,1)S(1)}, bf16[256,512]{1,0:T(8,128)(2,1)S(1)}, u32[]{:S(2)}, u32[]{:S(2)}) collective-permute-start(bf16[256,512]{1,0:T(8,128)(2,1)S(1)} %get-tuple-element.35), channel_id=1, source_target_pairs={{0,2},{1,3},{2,4},{3,5},{4,6},{5,7},{6,0},{7,1},{8,10},{9,11},{10,... | collective-permute-start | bytes 786440 | tf_op jit(solution)/shard_map/ppermute | solution.py:225
  42.5 2.8 %collective-permute-start.11 = (bf16[256,512]{1,0:T(8,128)(2,1)S(1)}, bf16[256,512]{1,0:T(8,128)(2,1)S(1)}, u32[]{:S(2)}, u32[]{:S(2)}) collective-permute-start(bf16[256,512]{1,0:T(8,128)(2,1)S(1)} %get-tuple-element.34.refs_4_), channel_id=1, source_target_pairs={{0,6},{1,7},{2,0},{3,1},{4,2},{5,3},{6,4},{7,5},{8,14},{9,15},{10,... | collective-permute-start | bytes 786440 | tf_op jit(solution)/shard_map/ppermute | solution.py:225
  45.3 8.3 %shard_map.34.refs_0_.refs_4_.refs_1_ = f32[512,2048]{1,0:T(8,128)S(1)} custom-call(s32[3]{0:T(128)S(1)} %pad_add_fusion.at.refs_0_.refs_6_.refs_2_, bf16[512,1152]{1,0:T(8,128)(2,1)S(1)} %shard_map.31.refs_0_.refs_4_, bf16[512,1152]{1,0:T(8,128)(2,1)S(1)} %collective-permute-done.7.refs_1_, bf16[8192,1152]{1,0:T(8,128)(2,1)} %refs_2_.7, ...), custom_call_target="tpu_custom_call" | custom-call | flops 1000 | bytes 100000000 | tf_op jit(solution)/shard_map/pallas_call | solution.py:159
  54.7 3.2 %collective-permute-start.14 = (bf16[256,1280]{1,0:T(8,128)(2,1)S(1)}, bf16[256,1280]{1,0:T(8,128)(2,1)S(1)}, u32[]{:S(2)}, u32[]{:S(2)}) collective-permute-start(bf16[256,1280]{1,0:T(8,128)(2,1)S(1)} %get-tuple-element.36.refs_5_), channel_id=1, source_target_pairs={{0,6},{1,7},{2,0},{3,1},{4,2},{5,3},{6,4},{7,5},{8,14},{9,15},{10,... | collective-permute-start | bytes 1966088 | tf_op jit(solution)/shard_map/ppermute | solution.py:225
  57.9 8.3 %shard_map.37.refs_6_.refs_0_.refs_1_ = f32[512,2048]{1,0:T(8,128)S(1)} custom-call(s32[3]{0:T(128)S(1)} %pad_add_fusion.at.refs_0_.refs_6_.refs_2_, bf16[512,1152]{1,0:T(8,128)(2,1)S(1)} %shard_map.36.refs_0_.refs_4_.refs_2_, bf16[512,1152]{1,0:T(8,128)(2,1)S(1)} %collective-permute-done.12.refs_1_.refs_3_, bf16[8192,1152]{1,0:T(8,128)(2,1)} %refs_2_.7, ...), custom_call_target="tpu_custom_call" | custom-call | flops 1000 | bytes 100000000 | tf_op jit(solution)/shard_map/pallas_call | solution.py:159
  66.3 7.8 %shard_map.38 = (f32[512,1024]{1,0:T(8,128)S(1)}, bf16[512,1024]{1,0:T(8,128)(2,1)S(1)}) custom-call(s32[3]{0:T(128)S(1)} %pad_add_fusion.at.refs_0_.refs_6_.refs_2_, bf16[512,1152]{1,0:T(8,128)(2,1)S(1)} %shard_map.31.refs_0_.refs_4_, bf16[512,1152]{1,0:T(8,128)(2,1)S(1)} %collective-permute-done.7.refs_1_, ...), custom_call_target="tpu_custom_call" | custom-call | flops 1000 | bytes 100000000 | tf_op jit(solution)/shard_map/pallas_call | solution.py:159
  74.5 3.2 %collective-permute-start.17 = (bf16[256,1536]{1,0:T(8,128)(2,1)S(1)}, bf16[256,1536]{1,0:T(8,128)(2,1)S(1)}, u32[]{:S(2)}, u32[]{:S(2)}) collective-permute-start(bf16[256,1536]{1,0:T(8,128)(2,1)S(1)} %get-tuple-element.40.refs_4_), channel_id=1, source_target_pairs={{0,6},{1,7},{2,0},{3,1},{4,2},{5,3},{6,4},{7,5},{8,14},{9,15},{10,... | collective-permute-start | bytes 2359304 | tf_op jit(solution)/shard_map/ppermute | solution.py:225
  77.7 1.0 collective-permute-start.20
  78.7 5.1 %shard_map.40.refs_5_.refs_0_.refs_2_ = f32[512,1024]{1,0:T(8,128)S(1)} custom-call(s32[3]{0:T(128)S(1)} %pad_add_fusion.at.refs_0_.refs_6_.refs_2_, bf16[512,1152]{1,0:T(8,128)(2,1)S(1)} %shard_map.36.refs_0_.refs_4_.refs_2_, bf16[512,1152]{1,0:T(8,128)(2,1)S(1)} %collective-permute-done.12.refs_1_.refs_3_, bf16[8192,1152]{1,0:T(8,128)(2,1)} %refs_2_.7, ...), custom_call_target="tpu_custom_call" | custom-call | flops 1000 | bytes 100000000 | tf_op jit(solution)/shard_map/pallas_call | solution.py:159
  83.9 11.1 %collective-permute-done.16.refs_2_.refs_3_.refs_1_ = bf16[256,1536]{1,0:T(8,128)(2,1)S(1)} collective-permute-done((bf16[256,1536]{1,0:T(8,128)(2,1)S(1)}, bf16[256,1536]{1,0:T(8,128)(2,1)S(1)}, u32[]{:S(2)}, u32[]{:S(2)}) %collective-permute-start.16) | collective-permute-done | bytes 786464 | tf_op jit(solution)/shard_map/ppermute | solution.py:225
  95.3 3.2 %collective-permute-start.19 = (bf16[256,1024]{1,0:T(8,128)(2,1)S(1)}, bf16[256,1024]{1,0:T(8,128)(2,1)S(1)}, u32[]{:S(2)}, u32[]{:S(2)}) collective-permute-start(bf16[256,1024]{1,0:T(8,128)(2,1)S(1)} %get-tuple-element.43.refs_5_), channel_id=1, source_target_pairs={{0,6},{1,7},{2,0},{3,1},{4,2},{5,3},{6,4},{7,5},{8,14},{9,15},{10,... | collective-permute-start | bytes 1572872 | tf_op jit(solution)/shard_map/ppermute | solution.py:225
  98.8 3.3 %collective-permute-done.20.refs_1_ = bf16[512,1024]{1,0:T(8,128)(2,1)S(1)} collective-permute-done((bf16[512,1024]{1,0:T(8,128)(2,1)S(1)}, bf16[512,1024]{1,0:T(8,128)(2,1)S(1)}, u32[]{:S(2)}, u32[]{:S(2)}) %collective-permute-start.20) | collective-permute-done | bytes 1048608 | tf_op jit(solution)/shard_map/ppermute | solution.py:355
  102.1 7.3 %collective-permute-done.18.refs_3_.refs_1_ = bf16[256,1024]{1,0:T(8,128)(2,1)S(1)} collective-permute-done((bf16[256,1024]{1,0:T(8,128)(2,1)S(1)}, bf16[256,1024]{1,0:T(8,128)(2,1)S(1)}, u32[]{:S(2)}, u32[]{:S(2)}) %collective-permute-start.18) | collective-permute-done | bytes 524320 | tf_op jit(solution)/shard_map/ppermute | solution.py:225
  109.5 0.9 collective-permute-start.21
  110.4 2.4 %collective-permute-start.22 = (bf16[256,768]{1,0:T(8,128)(2,1)S(1)}, bf16[256,768]{1,0:T(8,128)(2,1)S(1)}, u32[]{:S(2)}, u32[]{:S(2)}) collective-permute-start(bf16[256,768]{1,0:T(8,128)(2,1)S(1)} %get-tuple-element.46.refs_7_), channel_id=1, source_target_pairs={{0,6},{1,7},{2,0},{3,1},{4,2},{5,3},{6,4},{7,5},{8,14},{9,15},{10,... | collective-permute-start | bytes 1179656 | tf_op jit(solution)/shard_map/ppermute | solution.py:225
  112.8 1.8 %shard_map.45 = (f32[128,2048]{1,0:T(8,128)S(1)}, bf16[128,2048]{1,0:T(8,128)(2,1)}) custom-call(f32[512,2048]{1,0:T(8,128)S(1)} %shard_map.37.refs_6_.refs_0_.refs_1_, bf16[256,1536]{1,0:T(8,128)(2,1)S(1)} %collective-permute-done.16.refs_2_.refs_3_.refs_1_, bf16[256,1536]{1,0:T(8,128)(2,1)S(1)} %collective-permute-done.17.refs_3_.refs_4_.refs_2_, ...), custom_call_target="tpu_custom_call" | custom-call | flops 1000 | bytes 100000000 | tf_op jit(solution)/shard_map/pallas_call | solution.py:83
  114.7 1.0 collective-permute-start.26
  115.7 4.2 %collective-permute-done.21.refs_3_.refs_2_ = bf16[256,768]{1,0:T(8,128)(2,1)S(1)} collective-permute-done((bf16[256,768]{1,0:T(8,128)(2,1)S(1)}, bf16[256,768]{1,0:T(8,128)(2,1)S(1)}, u32[]{:S(2)}, u32[]{:S(2)}) %collective-permute-start.21) | collective-permute-done | bytes 393248 | tf_op jit(solution)/shard_map/ppermute | solution.py:225
  119.9 1.4 shard_map.46
  121.3 1.0 collective-permute-start.23
  122.3 0.8 shard_map.47
  123.1 0.9 collective-permute-start.24
  124.0 2.4 %collective-permute-start.25 = (bf16[256,256]{1,0:T(8,128)(2,1)}, bf16[256,256]{1,0:T(8,128)(2,1)}, u32[]{:S(2)}, u32[]{:S(2)}) collective-permute-start(bf16[256,256]{1,0:T(8,128)(2,1)} %get-tuple-element.51.refs_3_), channel_id=1, source_target_pairs={{0,6},{1,7},{2,0},{3,1},{4,2},{5,3},{6,4},{7,5},{8,14},{9,15},{10,... | collective-permute-start | bytes 393224 | tf_op jit(solution)/shard_map/ppermute | solution.py:225
  126.3 2.8 %collective-permute-done.26.refs_1_ = bf16[128,2048]{1,0:T(8,128)(2,1)} collective-permute-done((bf16[128,2048]{1,0:T(8,128)(2,1)}, bf16[128,2048]{1,0:T(8,128)(2,1)}, u32[]{:S(2)}, u32[]{:S(2)}) %collective-permute-start.26) | collective-permute-done | bytes 524320 | tf_op jit(solution)/shard_map/ppermute | solution.py:364
  129.2 1.2 copy-done.3
  130.4 1.3 shard_map.48
  131.8 1.0 copy-done.1
  132.8 1.1 shard_map.49
  134.5 1.0 shard_map.50
  135.7 1.4 %collective-permute-done.27 = f32[64,1024]{1,0:T(8,128)S(1)} collective-permute-done((f32[64,1024]{1,0:T(8,128)S(1)}, f32[64,1024]{1,0:T(8,128)S(1)}, u32[]{:S(2)}, u32[]{:S(2)}) %collective-permute-start.27) | collective-permute-done | bytes 262176 | tf_op jit(solution)/shard_map/ppermute | solution.py:371
  137.5 1.5 %pad_maximum_fusion = f32[64,8192]{1,0:T(8,128)} fusion(f32[64,4096]{1,0:T(8,128)S(1)} %get-tuple-element.60, f32[64,4096]{1,0:T(8,128)S(1)} %get-tuple-element.59), kind=kLoop, calls=%fused_computation | loop fusion | flops 524288 | bytes 4194304 | tf_op jit(solution)/shard_map/concatenate | solution.py:375
  (57 shorter events, 4.7 us)
Async XLA Ops:
  1.0 10.2 %collective-permute-start.6 = (bf16[128,1152]{1,0:T(8,128)(2,1)S(1)}, bf16[128,1152]{1,0:T(8,128)(2,1)S(1)}, u32[]{:S(2)}, u32[]{:S(2)}) collective-permute-start(bf16[128,1152]{1,0:T(8,128)(2,1)S(1)} %multiply_convert_fusion.refs_1_), channel_id=1, source_target_pairs={{0,16},{16,32},{32,48},{48,0},{64,80},{80,96},{96,112},{112,64},{1... | collective-permute-start | bytes 884744 | tf_op jit(solution)/shard_map/ppermute | solution.py:321
  2.8 14.1 %collective-permute-start.5 = (bf16[128,1152]{1,0:T(8,128)(2,1)S(1)}, bf16[128,1152]{1,0:T(8,128)(2,1)S(1)}, u32[]{:S(2)}, u32[]{:S(2)}) collective-permute-start(bf16[128,1152]{1,0:T(8,128)(2,1)S(1)} %multiply_convert_fusion.refs_1_), channel_id=1, source_target_pairs={{16,0},{32,16},{48,32},{0,48},{80,64},{96,80},{112,96},{64,112},{1... | collective-permute-start | bytes 884744 | tf_op jit(solution)/shard_map/ppermute | solution.py:322
  4.3 14.4 %collective-permute-start.2 = (bf16[128,1152]{1,0:T(8,128)(2,1)S(1)}, bf16[128,1152]{1,0:T(8,128)(2,1)S(1)}, u32[]{:S(2)}, u32[]{:S(2)}) collective-permute-start(bf16[128,1152]{1,0:T(8,128)(2,1)S(1)} %multiply_convert_fusion.refs_1_), channel_id=1, source_target_pairs={{0,32},{16,48},{32,0},{48,16},{64,96},{80,112},{96,64},{112,80},{1... | collective-permute-start | bytes 884744 | tf_op jit(solution)/shard_map/ppermute | solution.py:323
  6.4 12.3 %collective-permute-start = (bf16[128,1152]{1,0:T(8,128)(2,1)S(1)}, bf16[128,1152]{1,0:T(8,128)(2,1)S(1)}, u32[]{:S(2)}, u32[]{:S(2)}) collective-permute-start(bf16[128,1152]{1,0:T(8,128)(2,1)S(1)} %multiply_convert_fusion.refs_1_), channel_id=1, source_target_pairs={{0,64},{16,80},{32,96},{48,112},{64,0},{80,16},{96,32},{112,48},{1... | collective-permute-start | bytes 884744 | tf_op jit(solution)/shard_map/ppermute | solution.py:324
  18.7 9.2 %collective-permute-start.8 = (bf16[1024,1152]{1,0:T(8,128)(2,1)S(1)}, bf16[1024,1152]{1,0:T(8,128)(2,1)S(1)}, u32[]{:S(2)}, u32[]{:S(2)}) collective-permute-start(bf16[1024,1152]{1,0:T(8,128)(2,1)S(1)} %shard_map.28.refs_0_), channel_id=1, source_target_pairs={{0,1},{1,0},{2,3},{3,2},{4,5},{5,4},{6,7},{7,6},{8,9},{9,8},{10,11... | collective-permute-start | bytes 7077896 | tf_op jit(solution)/shard_map/ppermute | solution.py:347
  24.9 3.1 %collective-permute-start.7 = (bf16[512,1152]{1,0:T(8,128)(2,1)S(1)}, bf16[512,1152]{1,0:T(8,128)(2,1)S(1)}, u32[]{:S(2)}, u32[]{:S(2)}) collective-permute-start(bf16[512,1152]{1,0:T(8,128)(2,1)S(1)} %shard_map.31.refs_0_.refs_4_), channel_id=1, source_target_pairs={{0,1},{1,0},{2,3},{3,2},{4,5},{5,4},{6,7},{7,6},{8,9},{9,8},{10,11... | collective-permute-start | bytes 3538952 | tf_op jit(solution)/shard_map/ppermute | solution.py:342
  27.9 17.4 %collective-permute-start.9 = (bf16[2048,1152]{1,0:T(8,128)(2,1)S(1)}, bf16[2048,1152]{1,0:T(8,128)(2,1)S(1)}, u32[]{:S(2)}, u32[]{:S(2)}) collective-permute-start(bf16[2048,1152]{1,0:T(8,128)(2,1)S(1)} %shard_map.29.refs_0_), channel_id=1, source_target_pairs={{0,1},{1,0},{2,3},{3,2},{4,5},{5,4},{6,7},{7,6},{8,9},{9,8},{10,11... | collective-permute-start | bytes 14155784 | tf_op jit(solution)/shard_map/ppermute | solution.py:347
  28.3 37.9 %collective-permute-start.15 = (bf16[1024,1152]{1,0:T(8,128)(2,1)S(1)}, bf16[1024,1152]{1,0:T(8,128)(2,1)S(1)}, u32[]{:S(2)}, u32[]{:S(2)}) collective-permute-start(bf16[1024,1152]{1,0:T(8,128)(2,1)S(1)} %shard_map.30.refs_5_), channel_id=1, source_target_pairs={{0,1},{1,0},{2,3},{3,2},{4,5},{5,4},{6,7},{7,6},{8,9},{9,8},{10,11... | collective-permute-start | bytes 7077896 | tf_op jit(solution)/shard_map/ppermute | solution.py:347
  28.4 12.3 %collective-permute-start.3 = (bf16[128,1152]{1,0:T(8,128)(2,1)S(1)}, bf16[128,1152]{1,0:T(8,128)(2,1)S(1)}, u32[]{:S(2)}, u32[]{:S(2)}) collective-permute-start(bf16[128,1152]{1,0:T(8,128)(2,1)S(1)} %collective-permute-done.2.refs_3_), channel_id=1, source_target_pairs={{0,64},{16,80},{32,96},{48,112},{64,0},{80,16},{96,32},{112,48},{1... | collective-permute-start | bytes 884744 | tf_op jit(solution)/shard_map/ppermute | solution.py:326
  32.3 10.2 %collective-permute-start.4 = (bf16[128,1152]{1,0:T(8,128)(2,1)S(1)}, bf16[128,1152]{1,0:T(8,128)(2,1)S(1)}, u32[]{:S(2)}, u32[]{:S(2)}) collective-permute-start(bf16[128,1152]{1,0:T(8,128)(2,1)S(1)} %collective-permute-done.refs_6_.refs_5_.refs_1_), channel_id=1, source_target_pairs={{0,16},{16,32},{32,48},{48,0},{64,80},{80,96},{96,112},{112,64},{1... | collective-permute-start | bytes 884744 | tf_op jit(solution)/shard_map/ppermute | solution.py:326
  33.5 11.8 %collective-permute-start.1 = (bf16[128,1152]{1,0:T(8,128)(2,1)S(1)}, bf16[128,1152]{1,0:T(8,128)(2,1)S(1)}, u32[]{:S(2)}, u32[]{:S(2)}) collective-permute-start(bf16[128,1152]{1,0:T(8,128)(2,1)S(1)} %collective-permute-done.refs_6_.refs_5_.refs_1_), channel_id=1, source_target_pairs={{16,0},{32,16},{48,32},{0,48},{80,64},{96,80},{112,96},{64,112},{1... | collective-permute-start | bytes 884744 | tf_op jit(solution)/shard_map/ppermute | solution.py:326
  40.8 12.9 %collective-permute-start.10 = (bf16[256,512]{1,0:T(8,128)(2,1)S(1)}, bf16[256,512]{1,0:T(8,128)(2,1)S(1)}, u32[]{:S(2)}, u32[]{:S(2)}) collective-permute-start(bf16[256,512]{1,0:T(8,128)(2,1)S(1)} %get-tuple-element.35), channel_id=1, source_target_pairs={{0,2},{1,3},{2,4},{3,5},{4,6},{5,7},{6,0},{7,1},{8,10},{9,11},{10,... | collective-permute-start | bytes 786440 | tf_op jit(solution)/shard_map/ppermute | solution.py:225
  42.5 11.1 %collective-permute-start.11 = (bf16[256,512]{1,0:T(8,128)(2,1)S(1)}, bf16[256,512]{1,0:T(8,128)(2,1)S(1)}, u32[]{:S(2)}, u32[]{:S(2)}) collective-permute-start(bf16[256,512]{1,0:T(8,128)(2,1)S(1)} %get-tuple-element.34.refs_4_), channel_id=1, source_target_pairs={{0,6},{1,7},{2,0},{3,1},{4,2},{5,3},{6,4},{7,5},{8,14},{9,15},{10,... | collective-permute-start | bytes 786440 | tf_op jit(solution)/shard_map/ppermute | solution.py:225
  54.5 3.4 %collective-permute-start.12 = (bf16[512,1152]{1,0:T(8,128)(2,1)S(1)}, bf16[512,1152]{1,0:T(8,128)(2,1)S(1)}, u32[]{:S(2)}, u32[]{:S(2)}) collective-permute-start(bf16[512,1152]{1,0:T(8,128)(2,1)S(1)} %shard_map.36.refs_0_.refs_4_.refs_2_), channel_id=1, source_target_pairs={{0,1},{1,0},{2,3},{3,2},{4,5},{5,4},{6,7},{7,6},{8,9},{9,8},{10,11... | collective-permute-start | bytes 3538952 | tf_op jit(solution)/shard_map/ppermute | solution.py:342
  54.6 19.5 %collective-permute-start.13 = (bf16[256,1280]{1,0:T(8,128)(2,1)S(1)}, bf16[256,1280]{1,0:T(8,128)(2,1)S(1)}, u32[]{:S(2)}, u32[]{:S(2)}) collective-permute-start(bf16[256,1280]{1,0:T(8,128)(2,1)S(1)} %get-tuple-element.37), channel_id=1, source_target_pairs={{0,2},{1,3},{2,4},{3,5},{4,6},{5,7},{6,0},{7,1},{8,10},{9,11},{10,... | collective-permute-start | bytes 1966088 | tf_op jit(solution)/shard_map/ppermute | solution.py:225
  54.7 19.4 %collective-permute-start.14 = (bf16[256,1280]{1,0:T(8,128)(2,1)S(1)}, bf16[256,1280]{1,0:T(8,128)(2,1)S(1)}, u32[]{:S(2)}, u32[]{:S(2)}) collective-permute-start(bf16[256,1280]{1,0:T(8,128)(2,1)S(1)} %get-tuple-element.36.refs_5_), channel_id=1, source_target_pairs={{0,6},{1,7},{2,0},{3,1},{4,2},{5,3},{6,4},{7,5},{8,14},{9,15},{10,... | collective-permute-start | bytes 1966088 | tf_op jit(solution)/shard_map/ppermute | solution.py:225
  74.4 20.6 %collective-permute-start.16 = (bf16[256,1536]{1,0:T(8,128)(2,1)S(1)}, bf16[256,1536]{1,0:T(8,128)(2,1)S(1)}, u32[]{:S(2)}, u32[]{:S(2)}) collective-permute-start(bf16[256,1536]{1,0:T(8,128)(2,1)S(1)} %get-tuple-element.41), channel_id=1, source_target_pairs={{0,2},{1,3},{2,4},{3,5},{4,6},{5,7},{6,0},{7,1},{8,10},{9,11},{10,... | collective-permute-start | bytes 2359304 | tf_op jit(solution)/shard_map/ppermute | solution.py:225
  74.5 20.5 %collective-permute-start.17 = (bf16[256,1536]{1,0:T(8,128)(2,1)S(1)}, bf16[256,1536]{1,0:T(8,128)(2,1)S(1)}, u32[]{:S(2)}, u32[]{:S(2)}) collective-permute-start(bf16[256,1536]{1,0:T(8,128)(2,1)S(1)} %get-tuple-element.40.refs_4_), channel_id=1, source_target_pairs={{0,6},{1,7},{2,0},{3,1},{4,2},{5,3},{6,4},{7,5},{8,14},{9,15},{10,... | collective-permute-start | bytes 2359304 | tf_op jit(solution)/shard_map/ppermute | solution.py:225
  77.7 24.4 %collective-permute-start.20 = (bf16[512,1024]{1,0:T(8,128)(2,1)S(1)}, bf16[512,1024]{1,0:T(8,128)(2,1)S(1)}, u32[]{:S(2)}, u32[]{:S(2)}) collective-permute-start(bf16[512,1024]{1,0:T(8,128)(2,1)S(1)} %get-tuple-element.44), channel_id=1, source_target_pairs={{0,8},{1,9},{2,10},{3,11},{4,12},{5,13},{6,14},{7,15},{8,0},{9,1},... | collective-permute-start | bytes 3145736 | tf_op jit(solution)/shard_map/ppermute | solution.py:355
  95.2 14.1 %collective-permute-start.18 = (bf16[256,1024]{1,0:T(8,128)(2,1)S(1)}, bf16[256,1024]{1,0:T(8,128)(2,1)S(1)}, u32[]{:S(2)}, u32[]{:S(2)}) collective-permute-start(bf16[256,1024]{1,0:T(8,128)(2,1)S(1)} %get-tuple-element.42), channel_id=1, source_target_pairs={{0,2},{1,3},{2,4},{3,5},{4,6},{5,7},{6,0},{7,1},{8,10},{9,11},{10,... | collective-permute-start | bytes 1572872 | tf_op jit(solution)/shard_map/ppermute | solution.py:225
  95.3 14.0 %collective-permute-start.19 = (bf16[256,1024]{1,0:T(8,128)(2,1)S(1)}, bf16[256,1024]{1,0:T(8,128)(2,1)S(1)}, u32[]{:S(2)}, u32[]{:S(2)}) collective-permute-start(bf16[256,1024]{1,0:T(8,128)(2,1)S(1)} %get-tuple-element.43.refs_5_), channel_id=1, source_target_pairs={{0,6},{1,7},{2,0},{3,1},{4,2},{5,3},{6,4},{7,5},{8,14},{9,15},{10,... | collective-permute-start | bytes 1572872 | tf_op jit(solution)/shard_map/ppermute | solution.py:225
  109.5 10.4 %collective-permute-start.21 = (bf16[256,768]{1,0:T(8,128)(2,1)S(1)}, bf16[256,768]{1,0:T(8,128)(2,1)S(1)}, u32[]{:S(2)}, u32[]{:S(2)}) collective-permute-start(bf16[256,768]{1,0:T(8,128)(2,1)S(1)} %get-tuple-element.45), channel_id=1, source_target_pairs={{0,2},{1,3},{2,4},{3,5},{4,6},{5,7},{6,0},{7,1},{8,10},{9,11},{10,... | collective-permute-start | bytes 1179656 | tf_op jit(solution)/shard_map/ppermute | solution.py:225
  110.4 9.5 %collective-permute-start.22 = (bf16[256,768]{1,0:T(8,128)(2,1)S(1)}, bf16[256,768]{1,0:T(8,128)(2,1)S(1)}, u32[]{:S(2)}, u32[]{:S(2)}) collective-permute-start(bf16[256,768]{1,0:T(8,128)(2,1)S(1)} %get-tuple-element.46.refs_7_), channel_id=1, source_target_pairs={{0,6},{1,7},{2,0},{3,1},{4,2},{5,3},{6,4},{7,5},{8,14},{9,15},{10,... | collective-permute-start | bytes 1179656 | tf_op jit(solution)/shard_map/ppermute | solution.py:225
  114.7 6.6 %copy-start.2 = (f32[128,2048]{1,0:T(8,128)}, f32[128,2048]{1,0:T(8,128)S(1)}, u32[]{:S(2)}) copy-start(f32[128,2048]{1,0:T(8,128)S(1)} %get-tuple-element.52.refs_0_) | copy-start | bytes 3145732
  114.7 14.5 %collective-permute-start.26 = (bf16[128,2048]{1,0:T(8,128)(2,1)}, bf16[128,2048]{1,0:T(8,128)(2,1)}, u32[]{:S(2)}, u32[]{:S(2)}) collective-permute-start(bf16[128,2048]{1,0:T(8,128)(2,1)} %get-tuple-element.47.refs_7_), channel_id=1, source_target_pairs={{0,8},{1,9},{2,10},{3,11},{4,12},{5,13},{6,14},{7,15},{8,0},{9,1},... | collective-permute-start | bytes 1572872 | tf_op jit(solution)/shard_map/ppermute | solution.py:364
  119.9 2.4 %copy-start = (bf16[256,768]{1,0:T(8,128)(2,1)}, bf16[256,768]{1,0:T(8,128)(2,1)S(1)}, u32[]{:S(2)}) copy-start(bf16[256,768]{1,0:T(8,128)(2,1)S(1)} %collective-permute-done.22.refs_4_.refs_3_) | copy-start | bytes 1179652
  121.3 1.8 %copy-start.4 = (f32[128,1024]{1,0:T(8,128)}, f32[128,1024]{1,0:T(8,128)S(1)}, u32[]{:S(2)}) copy-start(f32[128,1024]{1,0:T(8,128)S(1)} %get-tuple-element.48.refs_0_) | copy-start | bytes 1572868
  121.3 13.2 %collective-permute-start.23 = (bf16[128,1024]{1,0:T(8,128)(2,1)}, bf16[128,1024]{1,0:T(8,128)(2,1)}, u32[]{:S(2)}, u32[]{:S(2)}) collective-permute-start(bf16[128,1024]{1,0:T(8,128)(2,1)} %get-tuple-element.49.refs_4_), channel_id=1, source_target_pairs={{0,8},{1,9},{2,10},{3,11},{4,12},{5,13},{6,14},{7,15},{8,0},{9,1},... | collective-permute-start | bytes 786440 | tf_op jit(solution)/shard_map/ppermute | solution.py:364
  123.1 8.7 %collective-permute-start.24 = (bf16[256,256]{1,0:T(8,128)(2,1)}, bf16[256,256]{1,0:T(8,128)(2,1)}, u32[]{:S(2)}, u32[]{:S(2)}) collective-permute-start(bf16[256,256]{1,0:T(8,128)(2,1)} %get-tuple-element.50), channel_id=1, source_target_pairs={{0,2},{1,3},{2,4},{3,5},{4,6},{5,7},{6,0},{7,1},{8,10},{9,11},{10,... | collective-permute-start | bytes 393224 | tf_op jit(solution)/shard_map/ppermute | solution.py:225
  124.0 7.8 %collective-permute-start.25 = (bf16[256,256]{1,0:T(8,128)(2,1)}, bf16[256,256]{1,0:T(8,128)(2,1)}, u32[]{:S(2)}, u32[]{:S(2)}) collective-permute-start(bf16[256,256]{1,0:T(8,128)(2,1)} %get-tuple-element.51.refs_3_), channel_id=1, source_target_pairs={{0,6},{1,7},{2,0},{3,1},{4,2},{5,3},{6,4},{7,5},{8,14},{9,15},{10,... | collective-permute-start | bytes 393224 | tf_op jit(solution)/shard_map/ppermute | solution.py:225
  129.2 1.2 copy-start.3
  130.4 4.1 %copy-start.5 = (f32[128,1024]{1,0:T(8,128)S(1)}, f32[128,1024]{1,0:T(8,128)}, u32[]{:S(2)}) copy-start(f32[128,1024]{1,0:T(8,128)} %copy-done.4) | copy-start | bytes 1572868
  131.7 5.5 %collective-permute-start.28 = (f32[64,2048]{1,0:T(8,128)S(1)}, f32[64,2048]{1,0:T(8,128)S(1)}, u32[]{:S(2)}, u32[]{:S(2)}) collective-permute-start(f32[64,2048]{1,0:T(8,128)S(1)} %get-tuple-element.53.refs_7_), channel_id=1, source_target_pairs={{0,1},{1,0},{2,3},{3,2},{4,5},{5,4},{6,7},{7,6},{8,9},{9,8},{10,11... | collective-permute-start | bytes 1572872 | tf_op jit(solution)/shard_map/ppermute | solution.py:371
  131.8 1.0 copy-start.1
  133.9 3.3 %collective-permute-start.29 = (f32[64,1024]{1,0:T(8,128)S(1)}, f32[64,1024]{1,0:T(8,128)S(1)}, u32[]{:S(2)}, u32[]{:S(2)}) collective-permute-start(f32[64,1024]{1,0:T(8,128)S(1)} %get-tuple-element.54.refs_3_), channel_id=1, source_target_pairs={{0,1},{1,0},{2,3},{3,2},{4,5},{5,4},{6,7},{7,6},{8,9},{9,8},{10,11... | collective-permute-start | bytes 786440 | tf_op jit(solution)/shard_map/ppermute | solution.py:371
  135.5 1.6 %collective-permute-start.27 = (f32[64,1024]{1,0:T(8,128)S(1)}, f32[64,1024]{1,0:T(8,128)S(1)}, u32[]{:S(2)}, u32[]{:S(2)}) collective-permute-start(f32[64,1024]{1,0:T(8,128)S(1)} %get-tuple-element.58), channel_id=1, source_target_pairs={{0,1},{1,0},{2,3},{3,2},{4,5},{5,4},{6,7},{7,6},{8,9},{9,8},{10,11... | collective-permute-start | bytes 786440 | tf_op jit(solution)/shard_map/ppermute | solution.py:371
